TPU v7x, 32 devices: a whole 2x2x4 slice. The times are simulated.
32 devices in a mesh: ctx: 8 (over z, core), head: 4 (over y, x).
Axes of the slice: x: 2, y: 2, z: 4, core: 2. Of those that a mesh axis runs over, the one named last changes fastest.
Arguments:
- q_nope: bfloat16 [1024, 8192], P('ctx', 'head'), may hold values from -6 to 6
- q_rope: bfloat16 [1024, 4096], P('ctx', 'head'), may hold values from -80 to 80
- kv_cache: bfloat16 [1024, 576], P('ctx'), may hold values from -180 to 180
- kv_gain: bfloat16 [512], replicated, may hold values from 0.099609375 to 1.8984375
- w_uk: bfloat16 [64, 128, 512], P('head'), may hold values from -0.5 to 0.5
- w_uv: bfloat16 [64, 512, 128], P('head'), may hold values from -0.25 to 0.25
- attn_out: bfloat16 [1024, 8192], P('ctx', 'head'), may hold values from -6 to 6
- d_out: bfloat16 [1024, 8192], P('ctx', 'head'), may hold values from -6 to 6
- span_table: int32 [8, 2], replicated, may hold values from 0 to 15, as said below
Outputs:
- d_q_nope: bfloat16 [1024, 8192], P('ctx', 'head')
- d_q_rope: bfloat16 [1024, 4096], P('ctx', 'head')
- d_cache: float32 [1024, 576], P('ctx')
Inputs may be any that keep to these rules, and one draw needn't show every extreme that they name: `span_table`: row d lists the two blocks of 64 positions held by the rows of ctx index d, in this order: a block c below 8, then its mirror 16 - 1 - c. The first column is a permutation.
All inputs are finite; a program needn't handle non-finite values.
Results may differ from a plain program's by a relative error of at most 0.02.
Values may be sent and summed in bfloat16 or wider, within the bound.
No kernel may reach another device: no remote copies, remote signals or barrier semaphores. Data moves between devices by JAX's collectives and lax.ppermute only.
A program may use at most 64 MiB of HBM per device.

v0:
```python
import jax
import jax.numpy as jnp
from jax import lax
from jax.sharding import PartitionSpec as P

neg_big = -1e30
eps_norm = 1e-06


def latent_rows(raw_rows, gain_rows):
    values = raw_rows.astype(jnp.float32)
    inverse = lax.rsqrt(jnp.mean(values * values, axis=-1, keepdims=True) + eps_norm)
    return (
        values,
        inverse,
        (values * inverse * gain_rows.astype(jnp.float32)).astype(jnp.bfloat16),
    )


def norm_backward(grad_rows, raw_rows, gain_rows, lat_width):
    values, inverse, unused_rows = latent_rows(raw_rows[:, :lat_width], gain_rows)
    scaled = grad_rows[:, :lat_width] * gain_rows.astype(jnp.float32)
    inner_mean = jnp.mean(values * scaled, axis=-1, keepdims=True)
    d_raw = inverse * scaled - values * inverse * inverse * inverse * inner_mean
    return jnp.concatenate([d_raw, grad_rows[:, lat_width:]], axis=1)


def add_latent(full_terms, latent_terms):
    width = latent_terms.shape[-1]
    return jnp.concatenate(
        [full_terms[..., :width] + latent_terms, full_terms[..., width:]], axis=-1
    )


def local(q_nope, q_rope, kv_cache, kv_gain, w_uk, w_uv, attn_out, d_out, span_table):
    tok_rows = q_nope.shape[0]
    span_len = tok_rows // 2
    head_count = w_uk.shape[0]
    nope_width = w_uk.shape[1]
    lat_width = w_uk.shape[2]
    value_width = w_uv.shape[2]
    rope_width = q_rope.shape[1] // head_count
    row_count = span_len * head_count
    cat_width = lat_width + rope_width
    score_scale = float(nope_width + rope_width) ** (-0.5)
    ctx_count = lax.axis_size("ctx")
    my_index = lax.axis_index("ctx")
    my_spans = lax.dynamic_index_in_dim(span_table, my_index, 0, keepdims=False)
    nope_view = q_nope.reshape(2, span_len, head_count, nope_width)
    q_latent = jnp.einsum(
        "schn,hnl->schl", nope_view, w_uk, preferred_element_type=jnp.float32
    ).astype(jnp.bfloat16)
    rope_view = q_rope.reshape(2, span_len, head_count, rope_width)
    query_cat = jnp.concatenate([q_latent, rope_view], axis=3).reshape(2, row_count, cat_width)
    grad_view = d_out.reshape(2, span_len, head_count, value_width)
    d_latent = jnp.einsum("schv,hlv->schl", grad_view, w_uv, preferred_element_type=jnp.float32)
    d_latent = d_latent.astype(jnp.bfloat16).reshape(2, row_count, lat_width)
    out_view = attn_out.reshape(2, span_len, head_count, value_width)
    row_delta = jnp.sum(
        grad_view.astype(jnp.float32) * out_view.astype(jnp.float32), axis=3
    ).reshape(2, row_count)
    offsets = jnp.arange(span_len, dtype=jnp.int32)
    row_offsets = jnp.arange(row_count, dtype=jnp.int32) // head_count
    query_pos = my_spans[:, None] * span_len + row_offsets[None, :]
    gathered = lax.all_gather(kv_cache, "ctx", axis=0, tiled=True)
    latent_all = latent_rows(gathered[:, :lat_width], kv_gain)[2]
    key_cat = jnp.concatenate([latent_all, gathered[:, lat_width:]], axis=1).reshape(
        ctx_count, 2, span_len, cat_width
    )
    upper_all = span_table[:, 0] > my_spans[0]

    def pair_scores(key_rows, key_table):
        upper_half = key_table[:, 0] > my_spans[0]
        first_keys = key_rows[:, 0]
        other_keys = jnp.where(upper_half[:, None, None], key_rows[:, 1], key_rows[:, 0])
        first_pos = key_table[:, 0][:, None] * span_len + offsets[None, :]
        other_pos = (
            jnp.where(upper_half, key_table[:, 1], key_table[:, 0])[:, None] * span_len
            + offsets[None, :]
        )
        picked_query = jnp.where(upper_half[:, None, None], query_cat[1][None], query_cat[0][None])
        picked_pos = jnp.where(upper_half[:, None], query_pos[1][None], query_pos[0][None])
        first_scores = (
            jnp.einsum("gkd,rd->gkr", first_keys, query_cat[1], preferred_element_type=jnp.float32)
            * score_scale
        )
        other_scores = (
            jnp.einsum("gkd,grd->gkr", other_keys, picked_query, preferred_element_type=jnp.float32)
            * score_scale
        )
        first_scores = jnp.where(
            first_pos[:, :, None] <= query_pos[1][None, None, :], first_scores, neg_big
        )
        other_scores = jnp.where(
            other_pos[:, :, None] <= picked_pos[:, None, :], other_scores, neg_big
        )
        return (first_scores, other_scores)

    group_size = min(8, ctx_count)
    group_count = ctx_count // group_size
    key_groups = key_cat.reshape(group_count, group_size, 2, span_len, cat_width)
    table_groups = span_table.reshape(group_count, group_size, 2)
    first_all, other_all = lax.map(
        lambda group_item: pair_scores(group_item[0], group_item[1]), (key_groups, table_groups)
    )
    first_all = first_all.reshape(ctx_count, span_len, row_count)
    other_all = other_all.reshape(ctx_count, span_len, row_count)
    own_keys = lax.dynamic_index_in_dim(key_cat, my_index, 0, keepdims=False)[1]
    own_pos = my_spans[1] * span_len + offsets
    own_scores = (
        jnp.einsum("kd,rd->kr", own_keys, query_cat[1], preferred_element_type=jnp.float32)
        * score_scale
    )
    own_scores = jnp.where(own_pos[:, None] <= query_pos[1][None, :], own_scores, neg_big)
    other_max = jnp.max(other_all, axis=1)
    top_upper = jnp.maximum(jnp.max(first_all, axis=(0, 1)), jnp.max(own_scores, axis=0))
    top_upper = jnp.maximum(
        top_upper, jnp.max(jnp.where(upper_all[:, None], other_max, neg_big), axis=0)
    )
    top_lower = jnp.max(jnp.where(upper_all[:, None], neg_big, other_max), axis=0)
    row_top = jnp.where(upper_all[:, None], top_upper[None, :], top_lower[None, :])
    other_sum = jnp.sum(jnp.exp(other_all - row_top[:, None, :]), axis=1)
    upper_sum = jnp.sum(jnp.exp(first_all - top_upper[None, None, :]), axis=(0, 1))
    upper_sum = upper_sum + jnp.sum(jnp.exp(own_scores - top_upper[None, :]), axis=0)
    upper_sum = upper_sum + jnp.sum(jnp.where(upper_all[:, None], other_sum, 0.0), axis=0)
    lower_sum = jnp.sum(jnp.where(upper_all[:, None], 0.0, other_sum), axis=0)
    log_total = jnp.stack([top_lower + jnp.log(lower_sum), top_upper + jnp.log(upper_sum)])
    own_prob = jnp.exp(own_scores - log_total[1][None, :])
    own_dp = jnp.einsum(
        "kl,rl->kr", own_keys[:, :lat_width], d_latent[1], preferred_element_type=jnp.float32
    )
    own_ds = (own_prob * (own_dp - row_delta[1][None, :]) * score_scale).astype(jnp.bfloat16)
    own_dq = jnp.einsum("kr,kd->rd", own_ds, own_keys, preferred_element_type=jnp.float32)
    own_dk = add_latent(
        jnp.einsum("kr,rd->kd", own_ds, query_cat[1], preferred_element_type=jnp.float32),
        jnp.einsum(
            "kr,rl->kl",
            own_prob.astype(jnp.bfloat16),
            d_latent[1],
            preferred_element_type=jnp.float32,
        ),
    )

    def pair_grads(key_rows, key_table, first_scores, other_scores, owner_ids):
        upper_half = key_table[:, 0] > my_spans[0]
        first_keys = key_rows[:, 0]
        other_keys = jnp.where(upper_half[:, None, None], key_rows[:, 1], key_rows[:, 0])
        picked_query = jnp.where(upper_half[:, None, None], query_cat[1][None], query_cat[0][None])
        picked_grad = jnp.where(upper_half[:, None, None], d_latent[1][None], d_latent[0][None])
        picked_delta = jnp.where(upper_half[:, None], row_delta[1][None], row_delta[0][None])
        picked_log = jnp.where(upper_half[:, None], log_total[1][None], log_total[0][None])
        first_prob = jnp.exp(first_scores - log_total[1][None, None, :])
        other_prob = jnp.exp(other_scores - picked_log[:, None, :])
        first_dp = jnp.einsum(
            "gkl,rl->gkr",
            first_keys[..., :lat_width],
            d_latent[1],
            preferred_element_type=jnp.float32,
        )
        other_dp = jnp.einsum(
            "gkl,grl->gkr",
            other_keys[..., :lat_width],
            picked_grad,
            preferred_element_type=jnp.float32,
        )
        first_ds = (first_prob * (first_dp - row_delta[1][None, None, :]) * score_scale).astype(
            jnp.bfloat16
        )
        other_ds = (other_prob * (other_dp - picked_delta[:, None, :]) * score_scale).astype(
            jnp.bfloat16
        )
        first_dq = jnp.einsum(
            "gkr,gkd->rd", first_ds, first_keys, preferred_element_type=jnp.float32
        )
        other_dq = jnp.einsum(
            "gkr,gkd->grd", other_ds, other_keys, preferred_element_type=jnp.float32
        )
        lower_dq = jnp.sum(jnp.where(upper_half[:, None, None], 0.0, other_dq), axis=0)
        upper_dq = jnp.sum(jnp.where(upper_half[:, None, None], other_dq, 0.0), axis=0) + first_dq
        first_dk = add_latent(
            jnp.einsum("gkr,rd->gkd", first_ds, query_cat[1], preferred_element_type=jnp.float32),
            jnp.einsum(
                "gkr,rl->gkl",
                first_prob.astype(jnp.bfloat16),
                d_latent[1],
                preferred_element_type=jnp.float32,
            ),
        )
        other_dk = add_latent(
            jnp.einsum("gkr,grd->gkd", other_ds, picked_query, preferred_element_type=jnp.float32),
            jnp.einsum(
                "gkr,grl->gkl",
                other_prob.astype(jnp.bfloat16),
                picked_grad,
                preferred_element_type=jnp.float32,
            ),
        )
        lower_rows = first_dk + jnp.where(upper_half[:, None, None], 0.0, other_dk)
        upper_rows = jnp.where(upper_half[:, None, None], other_dk, 0.0)
        upper_rows = upper_rows + jnp.where(
            (owner_ids == my_index)[:, None, None], own_dk[None], 0.0
        )
        owner_terms = jnp.concatenate([lower_rows, upper_rows], axis=1).astype(jnp.bfloat16)
        return (jnp.stack([lower_dq, upper_dq]), owner_terms)

    zero_dq = jnp.zeros((2, row_count, cat_width), jnp.float32)
    first_groups = first_all.reshape(group_count, group_size, span_len, row_count)
    other_groups = other_all.reshape(group_count, group_size, span_len, row_count)
    owner_groups = jnp.arange(ctx_count, dtype=jnp.int32).reshape(group_count, group_size)

    def group_step(dq_carry, group_item):
        dq_part, owner_terms = pair_grads(*group_item)
        return (dq_carry + dq_part, owner_terms)

    dq_sum, owner_terms = lax.scan(
        group_step, zero_dq, (key_groups, table_groups, first_groups, other_groups, owner_groups)
    )
    dq_total, owner_terms = (dq_sum, owner_terms.reshape(ctx_count, tok_rows, cat_width))
    received = lax.all_to_all(owner_terms, "ctx", split_axis=0, concat_axis=0, tiled=True)
    key_grads = jnp.sum(received.astype(jnp.float32), axis=0)
    summed = lax.psum(key_grads.astype(jnp.bfloat16), "head").astype(jnp.float32)
    d_cache = norm_backward(summed, kv_cache, kv_gain, lat_width)
    dq_total = dq_total + jnp.stack([jnp.zeros_like(own_dq), own_dq])
    dq_latent = (
        dq_total[..., :lat_width].astype(jnp.bfloat16).reshape(2, span_len, head_count, lat_width)
    )
    d_q_nope = jnp.einsum("schl,hnl->schn", dq_latent, w_uk, preferred_element_type=jnp.float32)
    d_q_nope = d_q_nope.astype(jnp.bfloat16).reshape(tok_rows, head_count * nope_width)
    d_q_rope = (
        dq_total[..., lat_width:].astype(jnp.bfloat16).reshape(tok_rows, head_count * rope_width)
    )
    return (d_q_nope, d_q_rope, d_cache)


def solution(mesh):
    in_specs = (
        P("ctx", "head"),
        P("ctx", "head"),
        P("ctx", None),
        P(),
        P("head", None, None),
        P("head", None, None),
        P("ctx", "head"),
        P("ctx", "head"),
        P(),
    )
    out_specs = (P("ctx", "head"), P("ctx", "head"), P("ctx", None))
    return jax.shard_map(local, mesh=mesh, in_specs=in_specs, out_specs=out_specs, check_vma=False)
```

profile of v0, /device:TPU:0, one launch (start us, length us, event | category | flops | bytes accessed | tf_op | source)
XLA Modules:
  0.0 149.5 jit_solution(683326452720872834)
XLA Ops:
  7.2 1.9 %copy.33 = bf16[128,576]{1,0:T(8,128)(2,1)} copy(bf16[128,576]{0,1:T(8,128)(2,1)} %param.11) | data formatting | bytes 294912 | tf_op args[2]
  11.8 1.7 %convert_bitcast_fusion.1 = bf16[2,64,16,512]{3,1,0,2:T(8,128)(2,1)} fusion(f32[16,512,2,64]{1,3,2,0:T(8,128)S(1)} %bitcast.119), kind=kLoop, calls=%fused_computation.45 | loop fusion | flops 1048576 | bytes 6291456 | tf_op jit(solution)/shard_map/convert_element_type | solution.py:52
  14.0 2.9 %fusion.37 = (bf16[1,64,16,576]{3,1,0,2:T(8,128)(2,1)S(1)}, bf16[1,64,16,576]{3,1,0,2:T(8,128)(2,1)}) fusion(bf16[2,64,16,512]{3,1,0,2:T(8,128)(2,1)} %convert_bitcast_fusion.1, bf16[2,64,16,64]{3,1,0,2:T(8,128)(2,1)S(1)} %copy.37), kind=kLoop, calls=%fused_computation.51 | loop fusion | flops 4718592 | bytes 4718592 | tf_op jit(solution)/shard_map/concatenate | solution.py:54
  17.6 1.5 copy.39
  19.1 3.2 %copy.40 = bf16[1,64,16,576]{3,2,1,0:T(8,128)(2,1)} copy(bf16[1,64,16,576]{3,1,0,2:T(8,128)(2,1)} %get-tuple-element.78) | data formatting | bytes 2359296 | tf_op jit(solution)/shard_map/while/body/eval_jaxpr/slice | solution.py:81
  22.2 2.4 %copy.41 = bf16[1024,576]{0,1:T(8,128)(2,1)} copy(bf16[1024,576]{1,0:T(8,128)(2,1)} %bitcast.134) | data formatting | bytes 2359296 | tf_op jit(solution)/shard_map/while/body/eval_jaxpr/jit(_where)/broadcast_in_dim | solution.py:81
  28.6 1.6 %copy.44 = bf16[1,64,16,512]{3,2,1,0:T(8,128)(2,1)} copy(bf16[1,64,16,512]{3,1,0,2:T(8,128)(2,1)S(1)} %get-tuple-element.79) | data formatting | bytes 2097152 | tf_op jit(solution)/shard_map/while/body/eval_jaxpr/slice | solution.py:149
  31.0 2.8 %copy.45 = bf16[1,64,16,512]{3,2,1,0:T(8,128)(2,1)} copy(bf16[1,64,16,512]{3,1,0,2:T(8,128)(2,1)} %get-tuple-element.80) | data formatting | bytes 2097152 | tf_op jit(solution)/shard_map/while/body/eval_jaxpr/slice | solution.py:149
  36.8 1.6 %fusion.22 = f32[1024]{0:T(1024)S(1)} fusion(bf16[1024,576]{1,0:T(8,128)(2,1)} %all-gather.2.cloned.1.call-done), kind=kLoop, calls=%fused_computation.30 | loop fusion | flops 1571840 | bytes 1052672 | tf_op jit(solution)/shard_map/reduce_sum | solution.py:12
  39.0 1.5 copy-done.14
  41.1 2.1 %fusion.80 = (f32[8,1024]{1,0:T(8,128)S(1)}, f32[8,64,1024]{2,1,0:T(8,128)S(1)}) fusion(bf16[8,64,576]{2,1,0:T(8,128)(2,1)S(1)} %fusion.58, pred[8]{0:T(512)(128)(4,1)S(1)} %compare_bitcast_fusion, bf16[1024,576]{0,1:T(8,128)(2,1)S(1)} %copy-done.15, bf16[1024,576]{0,1:T(8,128)(2,1)S(1)} %copy-done.14, s32[8,1024]{1,0:T(8,128)S(1)} %broadcast_select_fusion.3, ...), kind=kOutput, calls=%fused_computation.135 | convolution fusion | flops 610787328 | bytes 5113864 | tf_op jit(solution)/shard_map/while/body/eval_jaxpr/gkd,grd->gkr/dot_general | solution.py:88
  47.4 2.8 %multiply_convert_fusion.1 = bf16[8,64,1024]{2,1,0:T(8,128)(2,1)S(1)} fusion(f32[8,64,1024]{2,1,0:T(8,128)S(1)} %get-tuple-element.111, pred[8]{0:T(512)(128)(4,1)S(1)} %compare_bitcast_fusion, bf16[1024,512]{1,0:T(8,128)(2,1)S(1)} %bitcast.143, bf16[1024,512]{1,0:T(8,128)(2,1)S(1)} %bitcast.123, f32[8,1024]{1,0:T(8,128)S(1)} %get-tuple-element.109, ...), kind=kOutput, calls=%fused_computation.38 | convolution fusion | flops 543686656 | bytes 5833216 | tf_op jit(solution)/shard_map/while/body/eval_jaxpr/gkl,grl->gkr/dot_general | solution.py:160
  50.2 3.3 %fusion = f32[8,64,576]{2,1,0:T(8,128)S(1)} fusion(bf16[8,64,1024]{2,1,0:T(8,128)(2,1)S(1)} %multiply_convert_fusion.1, pred[8]{0:T(512)(128)(4,1)S(1)} %compare_bitcast_fusion, bf16[1024,576]{0,1:T(8,128)(2,1)S(1)} %copy-done.15, bf16[1024,576]{0,1:T(8,128)(2,1)S(1)} %copy-done.14), kind=kOutput, calls=%fused_computation.2 | convolution fusion | flops 608698368 | bytes 4587528 | tf_op jit(solution)/shard_map/while/body/eval_jaxpr/gkr,grd->gkd/dot_general | solution.py:190
  53.5 1.7 %fusion.34 = f32[8,64,512]{2,1,0:T(8,128)S(1)} fusion(pred[8]{0:T(512)(128)(4,1)S(1)} %compare_bitcast_fusion, bf16[1024,512]{1,0:T(8,128)(2,1)S(1)} %bitcast.144, bf16[1024,512]{1,0:T(8,128)(2,1)S(1)} %bitcast.124, f32[8,64,1024]{2,1,0:T(8,128)S(1)} %get-tuple-element.111, f32[8,64,576]{2,1,0:T(8,128)S(1)} %fusion, f32[8,1024]{1,0:T(8,128)S(1)} %get-tuple-element.108), kind=kOutput, calls=%fused_computation.50 | convolution fusion | flops 542375936 | bytes 6324232 | tf_op jit(solution)/shard_map/while/body/eval_jaxpr/gkr,grl->gkl/dot_general | solution.py:191
  58.6 1.5 %copy.52 = bf16[8,128,576]{1,2,0:T(8,128)(2,1)} copy(bf16[8,128,576]{2,1,0:T(8,128)(2,1)S(1)} %pad_maximum_fusion.3) | data formatting | bytes 2359296 | tf_op jit(solution)/shard_map/while/body/eval_jaxpr/concatenate | solution.py:203
  60.1 6.5 %all-to-all-start = ((bf16[8,128,576]{1,2,0:T(8,128)(2,1)}), bf16[8,128,576]{1,2,0:T(8,128)(2,1)}, u32[]{:S(2)}, u32[]{:S(2)}) async-start(bf16[8,128,576]{1,2,0:T(8,128)(2,1)} %copy.52), calls=%async_computation | async-start | bytes 2359296 | tf_op jit(solution)/shard_map/all_to_all | solution.py:219
  68.1 5.5 %select_reduce_fusion.1 = (f32[1024,576]{0,1:T(8,128)S(1)}, f32[1024,576]{0,1:T(8,128)S(1)}) fusion(pred[8]{0:T(512)(128)(4,1)S(1)} %compare_bitcast_fusion, bf16[8,64,1024]{2,1,0:T(8,128)(2,1)S(1)} %copy-done.27, bf16[8,64,576]{2,1,0:T(8,128)(2,1)S(1)} %copy-done.22), kind=kOutput, calls=%fused_computation.1 | convolution fusion | flops 621674496 | bytes 6357000 | tf_op jit(solution)/shard_map/while/body/eval_jaxpr/gkr,gkd->grd/dot_general | solution.py:175
  75.9 1.5 slice.199
  77.4 4.0 %copy.46 = bf16[2,1024,512]{2,1,0:T(8,128)(2,1)} copy(bf16[2,1024,512]{1,2,0:T(8,128)(2,1)} %slice.199) | data formatting | bytes 4194304 | tf_op jit(solution)/shard_map/slice | solution.py:225
  81.4 14.7 %all-to-all-done = bf16[8,128,576]{1,2,0:T(8,128)(2,1)} async-done(((bf16[8,128,576]{1,2,0:T(8,128)(2,1)}), bf16[8,128,576]{1,2,0:T(8,128)(2,1)}, u32[]{:S(2)}, u32[]{:S(2)}) %all-to-all-start) | async-done | bytes 1179680 | tf_op jit(solution)/shard_map/all_to_all | solution.py:219
  96.1 1.4 reduce_sum.123
  98.4 3.9 %fusion.44 = bf16[2,64,16,128]{3,1,0,2:T(8,128)(2,1)} fusion(bf16[16,128,512]{2,1,0:T(8,128)(2,1)S(1)} %copy-done, bf16[2,64,16,512]{3,2,1,0:T(8,128)(2,1)} %bitcast.138), kind=kOutput, calls=%fused_computation.60 | convolution fusion | flops 268697600 | bytes 4718592 | tf_op jit(solution)/shard_map/schl,hnl->schn/dot_general | solution.py:227
  104.7 1.4 copy.48
  107.0 32.7 %all-reduce.3.cloned.1.call-done = bf16[128,576]{1,0:T(8,128)(2,1)} async-done(((bf16[128,576]{1,0:T(8,128)(2,1)}), bf16[128,576]{1,0:T(8,128)(2,1)}) %all-reduce.3.cloned.1.call-update) | async-done | bytes 147472 | tf_op jit(solution)/shard_map/psum | solution.py:221
  (139 shorter events, 30.3 us)
Async XLA Ops:
  7.2 3.9 %copy-start = (bf16[16,128,512]{2,1,0:T(8,128)(2,1)S(1)}, bf16[16,128,512]{2,1,0:T(8,128)(2,1)}, u32[]{:S(2)}) copy-start(bf16[16,128,512]{2,1,0:T(8,128)(2,1)} %param.13) | copy-start | bytes 6291460
  7.2 29.6 %all-gather.2.cloned.1.call-start = ((), (), s32[]{:S(2)}) async-start(), calls=%async_computation.1 | async-start | bytes 1474560 | tf_op jit(solution)/shard_map/all_gather | solution.py:65
  11.8 1.7 %copy-start.24 = (bf16[128,1024]{1,0:T(8,128)(2,1)S(1)}, bf16[128,1024]{1,0:T(8,128)(2,1)}, u32[]{:S(2)}) copy-start(bf16[128,1024]{1,0:T(8,128)(2,1)} %param.10) | copy-start | bytes 786436
  24.6 1.8 %copy-start.11 = (bf16[16,512,128]{2,1,0:T(8,128)(2,1)S(1)}, bf16[16,512,128]{2,1,0:T(8,128)(2,1)}, u32[]{:S(2)}) copy-start(bf16[16,512,128]{2,1,0:T(8,128)(2,1)} %param.14) | copy-start | bytes 6291460
  28.6 1.6 %copy-start.23 = (bf16[128,2048]{1,0:T(8,128)(2,1)S(1)}, bf16[128,2048]{1,0:T(8,128)(2,1)}, u32[]{:S(2)}) copy-start(bf16[128,2048]{1,0:T(8,128)(2,1)} %param.15) | copy-start | bytes 1572868
  30.5 3.3 %copy-start.25 = (s32[8,2]{0,1:T(2,128)S(1)}, s32[8,2]{0,1:T(2,128)}, u32[]{:S(2)}) copy-start(s32[8,2]{0,1:T(2,128)} %param.17) | copy-start | bytes 196
  36.8 1.6 %copy-start.9 = (bf16[1024,576]{1,0:T(8,128)(2,1)S(1)}, bf16[1024,576]{1,0:T(8,128)(2,1)}, u32[]{:S(2)}) copy-start(bf16[1024,576]{1,0:T(8,128)(2,1)} %all-gather.2.cloned.1.call-done) | copy-start | bytes 3538948
  36.8 2.0 %slice-start = ((bf16[1024,576]{1,0:T(8,128)(2,1)}), bf16[1024,64]{1,0:T(8,128)(2,1)S(1)}, s32[]{:S(2)}) async-start(bf16[1024,576]{1,0:T(8,128)(2,1)} %all-gather.2.cloned.1.call-done), calls=%async_computation.3 | async-start | bytes 524288 | tf_op jit(solution)/shard_map/slice | solution.py:67
  38.7 1.8 %copy-start.14 = (bf16[1024,576]{0,1:T(8,128)(2,1)S(1)}, bf16[1024,576]{0,1:T(8,128)(2,1)}, u32[]{:S(2)}) copy-start(bf16[1024,576]{0,1:T(8,128)(2,1)} %copy.39) | copy-start | bytes 3538948
  38.7 2.3 %copy-start.15 = (bf16[1024,576]{0,1:T(8,128)(2,1)S(1)}, bf16[1024,576]{0,1:T(8,128)(2,1)}, u32[]{:S(2)}) copy-start(bf16[1024,576]{0,1:T(8,128)(2,1)} %copy.41) | copy-start | bytes 3538948
  38.9 16.3 %copy-start.6 = (bf16[1024,576]{1,0:T(8,128)(2,1)}, bf16[1024,576]{1,0:T(8,128)(2,1)S(1)}, u32[]{:S(2)}) copy-start(bf16[1024,576]{1,0:T(8,128)(2,1)S(1)} %pad_maximum_fusion.1) | copy-start | bytes 3538948
  39.0 8.3 %copy-start.21 = (bf16[8,64,576]{2,1,0:T(8,128)(2,1)}, bf16[8,64,576]{2,1,0:T(8,128)(2,1)S(1)}, u32[]{:S(2)}) copy-start(bf16[8,64,576]{2,1,0:T(8,128)(2,1)S(1)} %fusion.58) | copy-start | bytes 1769476
  47.0 3.2 %copy-start.20 = (f32[64,576]{1,0:T(8,128)}, f32[64,576]{1,0:T(8,128)S(1)}, u32[]{:S(2)}) copy-start(f32[64,576]{1,0:T(8,128)S(1)} %fusion.85) | copy-start | bytes 442372
  50.2 3.3 %copy-start.26 = (bf16[8,64,1024]{2,1,0:T(8,128)(2,1)}, bf16[8,64,1024]{2,1,0:T(8,128)(2,1)S(1)}, u32[]{:S(2)}) copy-start(bf16[8,64,1024]{2,1,0:T(8,128)(2,1)S(1)} %multiply_convert_fusion.1) | copy-start | bytes 3145732
  53.5 1.7 %copy-start.18 = (f32[8,64,576]{2,1,0:T(8,128)}, f32[8,64,576]{2,1,0:T(8,128)S(1)}, u32[]{:S(2)}) copy-start(f32[8,64,576]{2,1,0:T(8,128)S(1)} %fusion) | copy-start | bytes 3538948
  60.1 6.5 %copy-start.13 = (bf16[64,1024]{1,0:T(8,128)(2,1)S(1)}, bf16[64,1024]{1,0:T(8,128)(2,1)}, u32[]{:S(2)}) copy-start(bf16[64,1024]{1,0:T(8,128)(2,1)} %copy-done.12) | copy-start | bytes 393220
  60.1 36.0 %all-to-all-start = ((bf16[8,128,576]{1,2,0:T(8,128)(2,1)}), bf16[8,128,576]{1,2,0:T(8,128)(2,1)}, u32[]{:S(2)}, u32[]{:S(2)}) async-start(bf16[8,128,576]{1,2,0:T(8,128)(2,1)} %copy.52), calls=%async_computation | async-start | bytes 2359296 | tf_op jit(solution)/shard_map/all_to_all | solution.py:219
  66.6 73.2 %all-reduce.3.cloned.1.call-start = ((), (), s32[]{:S(2)}) async-start(), calls=%async_computation.2 | async-start | bytes 327680 | tf_op jit(solution)/shard_map/psum | solution.py:221
  68.1 6.4 %copy-start.3 = (f32[1,1024,576]{1,2,0:T(8,128)}, f32[1,1024,576]{1,2,0:T(8,128)S(1)}, u32[]{:S(2)}) copy-start(f32[1,1024,576]{1,2,0:T(8,128)S(1)} %convolution_bitcast_fusion) | copy-start | bytes 7077892
  68.1 5.5 %copy-start.7 = (bf16[1024,576]{1,0:T(8,128)(2,1)S(1)}, bf16[1024,576]{1,0:T(8,128)(2,1)}, u32[]{:S(2)}) copy-start(bf16[1024,576]{1,0:T(8,128)(2,1)} %copy-done.6) | copy-start | bytes 3538948
  68.1 5.5 %copy-start.17 = (bf16[8,64,1024]{2,1,0:T(8,128)(2,1)S(1)}, bf16[8,64,1024]{2,1,0:T(8,128)(2,1)}, u32[]{:S(2)}) copy-start(bf16[8,64,1024]{2,1,0:T(8,128)(2,1)} %copy-done.16) | copy-start | bytes 3145732
  98.4 4.0 %copy-start.2 = (f32[1,1024,576]{1,2,0:T(8,128)S(1)}, f32[1,1024,576]{1,2,0:T(8,128)}, u32[]{:S(2)}) copy-start(f32[1,1024,576]{1,2,0:T(8,128)} %copy-done.1) | copy-start | bytes 7077892
  98.4 3.9 %copy-start.4 = (f32[1,1024,576]{1,2,0:T(8,128)S(1)}, f32[1,1024,576]{1,2,0:T(8,128)}, u32[]{:S(2)}) copy-start(f32[1,1024,576]{1,2,0:T(8,128)} %copy-done.3) | copy-start | bytes 7077892
  103.4 37.3 %copy-start.10 = (bf16[128,576]{1,0:T(8,128)(2,1)S(1)}, bf16[128,576]{1,0:T(8,128)(2,1)}, u32[]{:S(2)}) copy-start(bf16[128,576]{1,0:T(8,128)(2,1)} %copy.33) | copy-start | bytes 442372
  (10 other events, 11.2 us)
Sparse Core Ops, SparseCore 0:
  10.2 26.1 all-gather.1
  98.5 41.1 all-reduce.2
where the time goes:
time: 150 us; the launch traced here: 149 us
  waiting for transfers between devices  47.5 us (32%)
  local copies, waits for them, and re-layouts  36.9 us (25%)
  matrix products  27.1 us (18%)
  other arithmetic  16.1 us (11%)
  between operations  15.4 us (10%)
  starting transfers between devices  6.53 us (4%)
    psum x1, waiting for transfers between devices, local(): lax.psum(key_grads.astype(jnp.bfloat16), 'head').astype(jnp.float32)  32.7 us
    all_to_all x1, waiting for transfers between devices, local(): lax.all_to_all(owner_terms, 'ctx', split_axis=0, concat_axis=0, tiled=True)  14.7 us
    unnamed x63, local copies, waits for them, and re-layouts  11.4 us
    all_to_all x1, starting transfers between devices, local(): lax.all_to_all(owner_terms, 'ctx', split_axis=0, concat_axis=0, tiled=True)  6.45 us
    dot_general x1, matrix products, pair_grads(): jnp.einsum('gkr,gkd->grd', other_ds, other_keys, preferred_element_type=j...  5.48 us
    slice x2, local copies, waits for them, and re-layouts, local(): dq_total[..., :lat_width].astype(jnp.bfloat16)  5.45 us
    dot_general x1, matrix products, local(): jnp.einsum('schl,hnl->schn', dq_latent, w_uk, preferred_element_type=jnp....  3.93 us
    broadcast_in_dim x2, local copies, waits for them, and re-layouts, pair_scores(): jnp.where(upper_half[:, None, None], query_cat[1][None], query_cat[0][None])  3.85 us
  transfers between devices with their start and end apart: 3, of which 2 were waited for; matrix products, arithmetic and copies ran while one was open for 32% of the time, Pallas kernels for 0%

commit v1 on v0

v1 whole, which is shorter than its diff:
```python
import functools

import jax
import jax.numpy as jnp
from jax import lax
from jax.experimental import pallas as pl
from jax.experimental.pallas import tpu as pltpu
from jax.sharding import PartitionSpec as P

neg_big = -1e30
eps_norm = 1e-06
log2_e = 1.4426950408889634
key_tile = 256
mib = 1024 * 1024
wide_mib = 53
fetch_mib = 54
query_mib = 51
delta_rows = 16
fetch_ahead = 3
row_chunk = 256
f32 = jnp.float32
bf16 = jnp.bfloat16
in_vmem = pl.BlockSpec(memory_space=pltpu.VMEM)
in_hbm = pl.BlockSpec(memory_space=pltpu.HBM)
in_any = pl.BlockSpec(memory_space=pl.ANY)
in_smem = pl.BlockSpec(memory_space=pltpu.SMEM)


def dot_nn(left, right):
    return lax.dot_general(left, right, (((1,), (0,)), ((), ())), preferred_element_type=f32)


def dot_nt(left, right):
    return lax.dot_general(left, right, (((1,), (1,)), ((), ())), preferred_element_type=f32)


def dot_tn(left, right):
    return lax.dot_general(left, right, (((0,), (0,)), ((), ())), preferred_element_type=f32)


def folds(rows):
    return rows % 32 == 0


def fold(block):
    rows, width = block.shape
    if not folds(rows):
        return block
    whole = width // 128
    half = rows // 2
    last = jnp.concatenate([block[:half, whole * 128 :], block[half:, whole * 128 :]], axis=1)
    return jnp.concatenate([block[:, j * 128 : (j + 1) * 128] for j in range(whole)] + [last], axis=0)


def unfold(block, rows, width):
    if not folds(rows):
        return block
    whole = width // 128
    last = block[whole * rows :]
    edge = jnp.concatenate([last[:, : width - whole * 128], last[:, width - whole * 128 :]], axis=0)
    return jnp.concatenate([block[j * rows : (j + 1) * rows] for j in range(whole)] + [edge], axis=1)


def folded(rows, width):
    return (rows * width // 128, 128) if folds(rows) else (rows, width)


def params(size):
    return pltpu.CompilerParams(vmem_limit_bytes=size * mib)


def keys_kernel(piece_rows, cache_t_ref, gain_ref, keys_ref, sib_ref, piece_ref, cache_scr, gain_scr, rows_scr, sems):
    lat_width = gain_ref.shape[0]
    copies = [
        pltpu.make_async_copy(cache_t_ref, cache_scr, sems.at[0]),
        pltpu.make_async_copy(gain_ref, gain_scr, sems.at[1]),
    ]
    for copy in copies:
        copy.start()
    for copy in copies:
        copy.wait()
    raw = jnp.transpose(cache_scr[...].astype(f32))
    latent = raw[:, :lat_width]
    inverse = lax.rsqrt(jnp.mean(latent * latent, axis=1, keepdims=True) + eps_norm)
    rows_scr[:, :lat_width] = latent * inverse * gain_scr[...].astype(f32)[None, :]
    rows_scr[:, lat_width:] = raw[:, lat_width:]
    keys_ref[...] = rows_scr[...].astype(bf16)
    sib_ref[...] = fold(rows_scr[...]).astype(bf16)
    start = pl.multiple_of(lax.axis_index("head") * piece_rows, piece_rows)
    piece_ref[...] = fold(rows_scr[pl.ds(start, piece_rows), :]).astype(bf16)


def columns(ref, i, parts):
    if len(ref.shape) == 3:
        size = ref.shape[0] // parts
        return ref.at[pl.ds(i * size, size)]
    size = ref.shape[1] // parts
    return ref.at[:, pl.ds(i * size, size)]


def fetches(sources, buffers, sems, parts):
    copies = [
        [
            pltpu.make_async_copy(columns(source, i, parts), columns(buffer, i, parts), sems.at[i, a])
            for a, (source, buffer) in enumerate(zip(sources, buffers))
        ]
        for i in range(parts)
    ]
    for part in copies[:fetch_ahead]:
        for copy in part:
            copy.start()
    return copies


def arrive(copies, i):
    for copy in copies[i]:
        copy.wait()
    if i + fetch_ahead < len(copies):
        for copy in copies[i + fetch_ahead]:
            copy.start()


def query_rows_kernel(*refs):
    sources, (unused_ref, q_hbm), buffers = refs[:3], refs[3:5], refs[5:8]
    q_ref, in_sems, out_sems = refs[8:]
    nope_ref, rope_ref, w_uk_ref = buffers
    heads, nope_width, lat_width = w_uk_ref.shape
    span = nope_ref.shape[0] // 2
    rope_width = rope_ref.shape[1] // heads
    pairs = heads // 2
    copies = fetches(sources, buffers, in_sems, pairs)
    outs = []
    for i in range(pairs):
        arrive(copies, i)
        for head in (2 * i, 2 * i + 1):
            rows = slice(head * span, (head + 1) * span)
            q_lat = dot_nn(nope_ref[:, head * nope_width : (head + 1) * nope_width], w_uk_ref[head]).astype(bf16)
            for s in range(2):
                tokens = slice(s * span, (s + 1) * span)
                q_ref[s, rows, :lat_width] = q_lat[tokens]
                q_ref[s, rows, lat_width:] = rope_ref[tokens, head * rope_width : (head + 1) * rope_width]
        rows = pl.ds(2 * i * span, 2 * span)
        outs.append(pltpu.make_async_copy(q_ref.at[:, rows], q_hbm.at[:, rows], out_sems.at[i]))
        outs[i].start()
    for copy in outs:
        copy.wait()


def grad_rows_kernel(*refs):
    sources, (unused_ref, dl_hbm), buffers = refs[:3], refs[3:5], refs[5:8]
    dl_ref, delta_scr, in_sems, out_sems = refs[8:]
    grad_ref, out_ref, w_uv_ref = buffers
    heads, lat_width, value_width = w_uv_ref.shape
    span = grad_ref.shape[0] // 2
    row_count = heads * span
    pairs = heads // 2
    copies = fetches(sources, buffers, in_sems, pairs)
    outs = []
    ones = jnp.ones((8, value_width), bf16)
    delta_scr[...] = jnp.zeros(delta_scr.shape, f32)
    for i in range(pairs):
        arrive(copies, i)
        wide = slice(2 * i * value_width, 2 * (i + 1) * value_width)
        products = grad_ref[:, wide].astype(f32) * out_ref[:, wide].astype(f32)
        for p in range(2):
            head = 2 * i + p
            rows = slice(head * span, (head + 1) * span)
            d_lat = dot_nt(grad_ref[:, head * value_width : (head + 1) * value_width], w_uv_ref[head]).astype(bf16)
            for s in range(2):
                dl_ref[s, rows, :] = d_lat[s * span : (s + 1) * span]
        for s in range(2):
            tokens = slice(s * span, (s + 1) * span)
            product = jnp.concatenate([products[tokens, :value_width], products[tokens, value_width:]], axis=0)
            high = product.astype(bf16)
            low = (product - high.astype(f32)).astype(bf16)
            delta = (dot_nt(ones, high) + dot_nt(ones, low))[:1]
            row, lane = divmod(2 * i * span, lat_width)
            delta_high = delta.astype(bf16).astype(f32)
            delta_scr[s, row : row + 1, lane : lane + 2 * span] = delta_high
            delta_scr[s, 8 + row : 9 + row, lane : lane + 2 * span] = delta - delta_high
        rows = pl.ds(2 * i * span, 2 * span)
        outs.append(pltpu.make_async_copy(dl_ref.at[:, rows], dl_hbm.at[:, rows], out_sems.at[i]))
        outs[i].start()
    dl_ref[:, row_count:, :] = delta_scr[...].astype(bf16)
    rows = pl.ds(row_count, delta_rows)
    outs.append(pltpu.make_async_copy(dl_ref.at[:, rows], dl_hbm.at[:, rows], out_sems.at[pairs]))
    outs[pairs].start()
    for copy in outs:
        copy.wait()


def join_kernel(*refs):
    refs[-2][...] = jnp.concatenate([ref[...].astype(f32) for ref in refs[:-3]], axis=0).astype(bf16)


def tile_place(u, tile_count, span, lower_block):
    per_tile = key_tile // span
    upper_count = (tile_count * per_tile - 1 - lower_block) // per_tile + 1
    if u <= tile_count // 2:
        return True, u
    if u == tile_count:
        return False, 0
    is_upper = u < upper_count
    return is_upper, jnp.where(is_upper, u, tile_count - u)


def pick(is_upper, upper, lower):
    if isinstance(is_upper, bool):
        return upper if is_upper else lower
    return jnp.where(is_upper, upper, lower)


def half_of(is_upper):
    return int(is_upper) if isinstance(is_upper, bool) else is_upper.astype(jnp.int32)


def tile_rows(kt):
    if isinstance(kt, int):
        return slice(kt * key_tile, (kt + 1) * key_tile)
    return pl.ds(pl.multiple_of(kt * key_tile, key_tile), key_tile)


def attend_kernel(scale, head_count, *refs):
    span_ref, own_ref, sib_ref, own_pieces, sib_pieces, q_hbm, dl_hbm, keys_ref, ds_hbm, keep_ref, send_ref = refs[:-9]
    e_scr, dk_scr, stage, q_ref, dl_ref, ds_ref, prob_scr, sems, ds_sems = refs[-9:]
    copies = [
        pltpu.make_async_copy(hbm.at[s], ref.at[s], sems.at[i, s])
        for i, (hbm, ref) in enumerate(((q_hbm, q_ref), (dl_hbm, dl_ref)))
        for s in (1, 0)
    ]
    copies[0].start()
    half_count, row_count, cat_width = q_ref.shape
    lat_width = dl_ref.shape[2]
    tok_rows = own_ref.shape[0]
    span = tok_rows // 2
    total = keys_ref.shape[0]
    tile_count = total // key_tile
    z_count = total // tok_rows // 2
    piece_rows = tok_rows // head_count
    per_span = span // piece_rows
    me, head = lax.axis_index("ctx"), lax.axis_index("head")
    z, core = me // 2, lax.rem(me, 2)

    def place(owner, quarter):
        block = span_ref[quarter // per_span, owner]
        start = block * span + lax.rem(quarter, per_span) * piece_rows
        return pl.ds(pl.multiple_of(start, piece_rows), piece_rows)

    sib_rows = unfold(sib_ref[...], tok_rows, cat_width)
    for owner, rows in ((me, own_ref[...]), (2 * z + 1 - core, sib_rows)):
        for s in range(2):
            start = pl.multiple_of(span_ref[s, owner] * span, span)
            stage[pl.ds(start, span), :] = rows[s * span : (s + 1) * span, :].astype(stage.dtype)
    for side, ref in enumerate((own_pieces, sib_pieces)):
        rows = ref[...].astype(stage.dtype)
        size = rows.shape[0] // (z_count - 1) // head_count
        for m in range(head_count):
            for k in range(1, z_count):
                owner = 2 * (z ^ k) + lax.rem(core + side, 2)
                start = (m * (z_count - 1) + k - 1) * size
                stage[place(owner, head ^ m), :] = unfold(rows[start : start + size], piece_rows, cat_width)
    keys_ref[...] = stage[...].astype(bf16)

    my_lower, my_upper = span_ref[0, me], span_ref[1, me]
    step_shape = (key_tile, min(row_chunk, row_count))
    key_step = lax.broadcasted_iota(jnp.int32, step_shape, 0)
    row_step = lax.rem(lax.broadcasted_iota(jnp.int32, step_shape, 1), span)
    step = row_step - key_step
    places = [tile_place(u, tile_count, span, my_lower) for u in range(tile_count + 1)]
    chunks = [slice(n, n + min(row_chunk, row_count)) for n in range(0, row_count, row_chunk)]
    tops, sums = [], []
    copies[0].wait()
    for copy in copies[1:]:
        copy.start()
    for u, (is_upper, kt) in enumerate(places):
        if u == tile_count // 2 + 1:
            copies[1].wait()
        top_parts, sum_parts = [], []
        for chunk in chunks:
            scores = dot_nt(keys_ref[tile_rows(kt), :], q_ref[half_of(is_upper), chunk]) * (scale * log2_e)
            if u >= tile_count // 2:
                base = kt * key_tile - pick(is_upper, my_upper, my_lower) * span
                scores = jnp.where(step >= base, scores, neg_big)
            top = jnp.max(scores, axis=0, keepdims=True)
            weights = jnp.exp2(scores - top)
            e_scr[u, :, chunk] = weights
            top_parts.append(top)
            sum_parts.append(jnp.sum(weights, axis=0, keepdims=True))
        tops.append(jnp.concatenate(top_parts, axis=1))
        sums.append(jnp.concatenate(sum_parts, axis=1))
    row_top, row_sum = [], []
    for s in range(2):
        kept = [jnp.where(half_of(is_upper) == s, top, neg_big) for (is_upper, kt), top in zip(places, tops)]
        best = functools.reduce(jnp.maximum, kept)
        row_top.append(best)
        row_sum.append(functools.reduce(jnp.add, [jnp.exp2(top - best) * add for top, add in zip(kept, sums)]))
    factors = []
    for (is_upper, kt), top in zip(places, tops):
        best = pick(is_upper, row_top[1], row_top[0])
        factors.append(jnp.exp2(top - best) / pick(is_upper, row_sum[1], row_sum[0]))
    dk_scr[(tile_count // 2 + 1) * key_tile :, :] = jnp.zeros(
        (total - (tile_count // 2 + 1) * key_tile, cat_width), f32
    )
    copies[2].wait()
    copies[3].wait()
    deltas = []
    for s in range(2):
        parts = dl_ref[s, row_count:, :].astype(f32)
        width = min(lat_width, row_count)
        rows = [parts[j : j + 1, :width] + parts[8 + j : 9 + j, :width] for j in range(row_count // width)]
        deltas.append(jnp.concatenate(rows, axis=1))
    ds_copies = []

    def score_grads(u):
        is_upper, kt = places[u]
        half = half_of(is_upper)
        delta = pick(is_upper, deltas[1], deltas[0])
        for chunk in chunks:
            d_prob = dot_nt(keys_ref[tile_rows(kt), :lat_width], dl_ref[half, chunk])
            prob = e_scr[u, :, chunk] * factors[u][:, chunk]
            ds_ref[u, :, chunk] = (prob * scale * (d_prob - delta[:, chunk])).astype(bf16)
            prob_scr[u % 2, :, chunk] = prob.astype(bf16)
        ds_copies.append(pltpu.make_async_copy(ds_ref.at[u], ds_hbm.at[u], ds_sems.at[u]))
        ds_copies[u].start()

    def key_grads(u):
        is_upper, kt = places[u]
        half = half_of(is_upper)
        key_part = dot_nn(ds_ref[u], q_ref[half])
        latent_part = key_part[:, :lat_width] + dot_nn(prob_scr[u % 2], dl_ref[half, :row_count])
        if u <= tile_count // 2:
            dk_scr[tile_rows(kt), :lat_width] = latent_part
            dk_scr[tile_rows(kt), lat_width:] = key_part[:, lat_width:]
        else:
            dk_scr[tile_rows(kt), :lat_width] += latent_part
            dk_scr[tile_rows(kt), lat_width:] += key_part[:, lat_width:]

    score_grads(0)
    for u in range(tile_count + 1):
        if u < tile_count:
            score_grads(u + 1)
        key_grads(u)
    for side, ref in ((0, keep_ref), (1, send_ref)):
        for quarter in range(head_count):
            rows = [
                fold(dk_scr[place(2 * other + lax.rem(core + side, 2), jnp.int32(quarter)), :])
                for other in range(z_count)
            ]
            share = ref.shape[0] // head_count
            ref[quarter * share : (quarter + 1) * share, :] = jnp.concatenate(rows, axis=0).astype(bf16)
    for copy in ds_copies:
        copy.wait()


def query_kernel(
    span_ref, keys_ref, ds_hbm, w_uk_hbm, unused_ref, nope_ref, rope_ref, token_ref, dq_scr, ds_ref, w_uk_ref, sems
):
    tile_total, unused_rows, row_count = ds_ref.shape
    copies = [pltpu.make_async_copy(ds_hbm.at[u], ds_ref.at[u], sems.at[u]) for u in range(tile_total)]
    copies.append(pltpu.make_async_copy(w_uk_hbm, w_uk_ref, sems.at[tile_total]))
    for copy in copies[:tile_total]:
        copy.start()
    token_ref[...] = jnp.zeros(token_ref.shape, f32)
    tile_count = tile_total - 1
    heads, nope_width, lat_width = w_uk_ref.shape
    span = row_count // heads
    cat_width = keys_ref.shape[1]
    my_lower = span_ref[0, lax.axis_index("ctx")]
    places = [tile_place(u, tile_count, span, my_lower) for u in range(tile_total)]
    sure = tile_count // 2 + 1
    for copy in copies[:sure]:
        copy.wait()
    copies[tile_total].start()
    dq_scr[1] = dot_tn(keys_ref[: sure * key_tile, :], ds_ref[:sure].reshape(sure * key_tile, row_count))
    for copy in copies[sure:tile_total]:
        copy.wait()
    dq_scr[0] = dot_tn(keys_ref[:key_tile, :], ds_ref[tile_count])
    for u, (is_upper, kt) in enumerate(places):
        if not isinstance(is_upper, bool):
            dq_scr[half_of(is_upper)] += dot_tn(keys_ref[tile_rows(kt), :], ds_ref[u])
    copies[tile_total].wait()
    for pair in range(heads // 2):
        wide = slice(pair * 2 * span, (pair + 1) * 2 * span)
        turned = [jnp.transpose(dq_scr[s, :, wide]) for s in range(2)]
        for p in range(2):
            head = 2 * pair + p
            rows = jnp.concatenate([t[p * span : (p + 1) * span, :lat_width] for t in turned], axis=0)
            nope_ref[:, head * nope_width : (head + 1) * nope_width] = dot_nt(
                rows.astype(bf16), w_uk_ref[head]
            ).astype(bf16)
        rope = [
            jnp.concatenate([t[p * span : (p + 1) * span, lat_width:] for t in turned], axis=0) for p in range(2)
        ]
        width = 2 * (cat_width - lat_width)
        rope_ref[:, pair * width : (pair + 1) * width] = jnp.concatenate(rope, axis=1).astype(bf16)


def pair_sum_kernel(keep_ref, recv_ref, own_ref, *send_refs):
    head = lax.axis_index("head")
    share = own_ref.shape[0]

    def both(target):
        rows = pl.ds(pl.multiple_of(target * share, share), share)
        return keep_ref[rows, :].astype(f32) + recv_ref[rows, :].astype(f32)

    own_ref[...] = both(head)
    for m, ref in enumerate(send_refs, 1):
        ref[...] = both(head ^ m).astype(bf16)


def head_sum_kernel(*refs):
    z_count = refs[0].shape[0] // refs[-2].shape[0]
    head_count = len(refs) - 2 - z_count
    terms, own_ref, send_refs, total = refs[:head_count], refs[head_count + 1], refs[head_count + 2 : -1], refs[-1]
    total[...] = functools.reduce(jnp.add, [ref[...].astype(f32) for ref in terms])
    rows = own_ref.shape[0]
    z = lax.axis_index("ctx") // 2

    def share(k):
        return total[pl.ds(pl.multiple_of((z ^ k) * rows, rows), rows), :]

    own_ref[...] = share(0)
    for k, ref in enumerate(send_refs, 1):
        ref[...] = share(k).astype(bf16)


def chip_sum_kernel(*refs):
    refs[-1][...] = functools.reduce(jnp.add, [ref[...].astype(f32) for ref in refs[:-1]]).astype(bf16)


def norm_back_kernel(cache_t_ref, gain_ref, *refs):
    shares, out_ref, total = refs[:-2], refs[-2], refs[-1]
    head = lax.axis_index("head")
    rows = total.shape[0] // len(shares)
    lat_width = gain_ref.shape[0]
    for m, ref in enumerate(shares):
        total[pl.ds(pl.multiple_of((head ^ m) * rows, rows), rows), :] = unfold(
            ref[...].astype(f32), rows, total.shape[1]
        )
    values = cache_t_ref[:lat_width, :].astype(f32)
    inverse = lax.rsqrt(jnp.mean(values * values, axis=0, keepdims=True) + eps_norm)
    scaled = jnp.transpose(total[:, :lat_width] * gain_ref[...].astype(f32)[None, :])
    inner = jnp.mean(values * scaled, axis=0, keepdims=True)
    out_ref[:lat_width, :] = inverse * scaled - values * (inverse * inverse * inverse * inner)
    out_ref[lat_width:, :] = jnp.transpose(total[:, lat_width:])


def local(q_nope, q_rope, kv_cache, kv_gain, w_uk, w_uv, attn_out, d_out, span_table):
    shape = jax.ShapeDtypeStruct
    tok_rows, cat_width = kv_cache.shape
    heads, nope_width, lat_width = w_uk.shape
    value_width = w_uv.shape[2]
    rope_width = q_rope.shape[1] // heads
    span = tok_rows // 2
    row_count = span * heads
    scale = float(nope_width + rope_width) ** (-0.5)
    ctx_count, head_count = lax.axis_size("ctx"), lax.axis_size("head")
    z_count = ctx_count // 2
    total = ctx_count * tok_rows
    tile_total = total // key_tile + 1
    piece_rows = tok_rows // head_count
    cache_t = kv_cache.T
    spans = span_table.T

    def to_core(rows):
        return lax.ppermute(rows, "ctx", [(i, i ^ 1) for i in range(ctx_count)])

    def to_chip(rows, k):
        return lax.ppermute(rows, "ctx", [(i, i ^ (2 * k)) for i in range(ctx_count)])

    def to_head(rows, m):
        return lax.ppermute(rows, "head", [(j, j ^ m) for j in range(head_count)])

    keys_own, keys_out, piece = pl.pallas_call(
        functools.partial(keys_kernel, piece_rows),
        out_shape=(
            shape((tok_rows, cat_width), bf16),
            shape(folded(tok_rows, cat_width), bf16),
            shape(folded(piece_rows, cat_width), bf16),
        ),
        in_specs=[in_hbm] * 2,
        out_specs=(in_vmem,) * 3,
        scratch_shapes=[
            pltpu.VMEM((cat_width, tok_rows), bf16),
            pltpu.VMEM((lat_width,), bf16),
            pltpu.VMEM((tok_rows, cat_width), f32),
            pltpu.SemaphoreType.DMA((2,)),
        ],
        compiler_params=params(fetch_mib),
        name="keys",
    )(cache_t, kv_gain)
    keys_sib = to_core(keys_out)
    pieces = [to_chip(piece, k) for k in range(1, z_count)]
    pairs = heads // 2
    projection = pl.CostEstimate(
        flops=4 * row_count * nope_width * lat_width, bytes_accessed=6 * mib, transcendentals=0
    )

    def project(kernel, inputs, order, out_shape, scratch, name):
        return pl.pallas_call(
            kernel,
            out_shape=shape(out_shape, bf16),
            in_specs=[in_any] * 4,
            out_specs=in_any,
            scratch_shapes=[pltpu.VMEM(a.shape, bf16) for a in inputs]
            + [pltpu.VMEM(out_shape, bf16)]
            + scratch
            + [pltpu.SemaphoreType.DMA((pairs, 3)), pltpu.SemaphoreType.DMA((pairs + 1,))],
            compiler_params=params(fetch_mib),
            cost_estimate=projection,
            name=name,
        )(*inputs, order)

    def join(rows, order, name):
        return pl.pallas_call(
            join_kernel,
            out_shape=(shape((sum(r.shape[0] for r in rows), rows[0].shape[1]), bf16), shape((4096, 256), f32)),
            in_specs=[in_vmem] * len(rows) + [in_any],
            out_specs=(in_vmem, in_any),
            compiler_params=params(wide_mib),
            name=name,
        )(*rows, order)

    queries = project(
        query_rows_kernel, (q_nope, q_rope, w_uk), piece, (2, row_count, cat_width), [], "query_rows"
    )
    pieces, token = join(pieces, queries, "join_chips")
    d_latent = project(
        grad_rows_kernel,
        (d_out, attn_out, w_uv),
        token,
        (2, row_count + delta_rows, lat_width),
        [pltpu.VMEM((2, delta_rows, lat_width), f32)],
        "grad_rows",
    )
    pieces, token = join([pieces] + [to_head(pieces, m) for m in range(1, head_count)], d_latent, "join_heads")
    sib_pieces = to_core(pieces)

    piece_shape = piece.shape
    share_shape = (z_count * piece_shape[0], piece_shape[1])
    all_shape = (head_count * share_shape[0], piece_shape[1])
    keys, d_score, keep, send = pl.pallas_call(
        functools.partial(attend_kernel, scale, head_count),
        out_shape=(
            shape((total, cat_width), bf16),
            shape((tile_total, key_tile, row_count), bf16),
            shape(all_shape, bf16),
            shape(all_shape, bf16),
        ),
        in_specs=[in_smem] + [in_vmem] * 4 + [in_any] * 2,
        out_specs=(in_vmem, in_any, in_vmem, in_vmem),
        scratch_shapes=[
            pltpu.VMEM((tile_total, key_tile, row_count), f32),
            pltpu.VMEM((total, cat_width), f32),
            pltpu.VMEM((total, cat_width), bf16 if piece_rows % 16 == 0 else f32),
            pltpu.VMEM(queries.shape, bf16),
            pltpu.VMEM(d_latent.shape, bf16),
            pltpu.VMEM((tile_total, key_tile, row_count), bf16),
            pltpu.VMEM((2, key_tile, row_count), bf16),
            pltpu.SemaphoreType.DMA((2, 2)),
            pltpu.SemaphoreType.DMA((tile_total,)),
        ],
        compiler_params=params(50),
        cost_estimate=pl.CostEstimate(
            flops=2 * tile_total * key_tile * row_count * (2 * cat_width + 2 * lat_width),
            bytes_accessed=12 * mib,
            transcendentals=tile_total * key_tile * row_count,
        ),
        name="attend",
    )(spans, keys_own, keys_sib, pieces, sib_pieces, queries, d_latent)

    recv = to_core(send)
    sums = pl.pallas_call(
        pair_sum_kernel,
        out_shape=(shape(share_shape, f32),) + (shape(share_shape, bf16),) * (head_count - 1),
        in_specs=[in_vmem] * 2,
        out_specs=(in_vmem,) * head_count,
        compiler_params=params(4),
        name="pair_sum",
    )(keep, recv)
    d_q_nope, d_q_rope, token = pl.pallas_call(
        query_kernel,
        out_shape=(shape(q_nope.shape, bf16), shape(q_rope.shape, bf16), shape((8, 128), f32)),
        in_specs=[in_smem, in_vmem] + [in_any] * 3,
        out_specs=(in_vmem,) * 3,
        scratch_shapes=[
            pltpu.VMEM((2, cat_width, row_count), f32),
            pltpu.VMEM(d_score.shape, bf16),
            pltpu.VMEM(w_uk.shape, bf16),
            pltpu.SemaphoreType.DMA((tile_total + 1,)),
        ],
        compiler_params=params(query_mib),
        cost_estimate=pl.CostEstimate(
            flops=2 * tile_total * key_tile * row_count * cat_width,
            bytes_accessed=8 * mib,
            transcendentals=0,
        ),
        name="query_grads",
    )(spans, keys, d_score, w_uk, sums[0])
    terms = [sums[0]] + [to_head(rows, m) for m, rows in enumerate(sums[1:], 1)]
    sums = pl.pallas_call(
        head_sum_kernel,
        out_shape=(shape(piece_shape, f32),) + (shape(piece_shape, bf16),) * (z_count - 1),
        in_specs=[in_vmem] * head_count + [in_any],
        out_specs=(in_vmem,) * z_count,
        scratch_shapes=[pltpu.VMEM(share_shape, f32)],
        compiler_params=params(4),
        name="head_sum",
    )(*terms, token)
    terms = [sums[0]] + [to_chip(rows, k) for k, rows in enumerate(sums[1:], 1)]
    share = pl.pallas_call(
        chip_sum_kernel,
        out_shape=shape(piece_shape, bf16),
        in_specs=[in_vmem] * z_count,
        out_specs=in_vmem,
        compiler_params=params(4),
        name="chip_sum",
    )(*terms)
    shares = [share] + [to_head(share, m) for m in range(1, head_count)]
    d_cache_t = pl.pallas_call(
        norm_back_kernel,
        out_shape=shape((cat_width, tok_rows), f32),
        in_specs=[in_vmem] * (2 + head_count),
        out_specs=in_vmem,
        scratch_shapes=[pltpu.VMEM((tok_rows, cat_width), f32)],
        compiler_params=params(8),
        name="norm_back",
    )(cache_t, kv_gain, *shares)
    return (d_q_nope, d_q_rope, d_cache_t.T)


def solution(mesh):
    in_specs = (
        P("ctx", "head"),
        P("ctx", "head"),
        P("ctx", None),
        P(),
        P("head", None, None),
        P("head", None, None),
        P("ctx", "head"),
        P("ctx", "head"),
        P(),
    )
    out_specs = (P("ctx", "head"), P("ctx", "head"), P("ctx", None))
    return jax.shard_map(local, mesh=mesh, in_specs=in_specs, out_specs=out_specs, check_vma=False)
```

time: 150 us -> 65.9 us (0.44)
  local copies, waits for them, and re-layouts: 36.9 us -> 0.02 us
  waiting for transfers between devices: 47.5 us -> 13.1 us
  Pallas kernels: 0 us -> 30 us
  matrix products: 27.1 us -> 0 us
  other arithmetic: 16.1 us -> 0 us
  starting transfers between devices: 6.53 us -> 21.6 us
  between operations: 15.4 us -> 0.79 us
    psum x1 -> x0, waiting for transfers between devices: 32.7 us -> none  [local(): lax.psum(key_grads.astype(jnp.bfloat16), 'head').astype(jnp.float32)]
    pallas_call x0 -> x11, Pallas kernels: none -> 30 us  [the longest x1 11.3 us: local(): pl.pallas_call(functools.partial(attend_kernel, scale, head_count), out_s...]
    dot_general x16 -> x0, matrix products: 25.7 us -> none  [the longest x1 5.48 us: pair_grads(): jnp.einsum('gkr,gkd->grd', other_ds, other_keys, preferred_element_type=j...]
    ppermute x0 -> x18, starting transfers between devices: none -> 21.6 us  [the longest x9 10.7 us: to_head(): return lax.ppermute(rows, 'head', [(j, j ^ m) for j in range(head_count)])]
    slice x19 -> x0, local copies, waits for them, and re-layouts: 16.7 us -> none  [the longest x2 5.45 us: local(): dq_total[..., :lat_width].astype(jnp.bfloat16)]
    all_to_all x1 -> x0, waiting for transfers between devices: 14.7 us -> none  [local(): lax.all_to_all(owner_terms, 'ctx', split_axis=0, concat_axis=0, tiled=True)]
    ppermute x0 -> x18, waiting for transfers between devices: none -> 13.1 us  [the longest x6 5.57 us: to_chip(): return lax.ppermute(rows, 'ctx', [(i, i ^ 2 * k) for i in range(ctx_count)])]
    unnamed x63 -> x10, local copies, waits for them, and re-layouts: 11.4 us -> 0.02 us
  transfers between devices with their start and end apart: 3 -> 18, of which waited for: 2 -> 8; matrix products, arithmetic and copies ran while one was open for 32% -> 0% of each run, Pallas kernels for 0% -> 23%
where the time goes in v1:
time: 65.9 us; the launch traced here: 65.5 us
  Pallas kernels  30 us (46%)
  starting transfers between devices  21.6 us (33%)
  waiting for transfers between devices  13.1 us (20%)
  between operations  0.79 us (1%)
    pallas_call x1, Pallas kernels, local(): pl.pallas_call(functools.partial(attend_kernel, scale, head_count), out_s...  11.3 us
    ppermute x9, starting transfers between devices, to_head(): return lax.ppermute(rows, 'head', [(j, j ^ m) for j in range(head_count)])  10.7 us
    ppermute x6, starting transfers between devices, to_chip(): return lax.ppermute(rows, 'ctx', [(i, i ^ 2 * k) for i in range(ctx_count)])  10.2 us
    pallas_call x2, Pallas kernels, project(): pl.pallas_call(kernel, out_shape=shape(out_shape, bf16), in_specs=[in_any...  9.47 us
    pallas_call x1, Pallas kernels, local(): pl.pallas_call(query_kernel, out_shape=(shape(q_nope.shape, bf16), shape(...  5.91 us
    ppermute x6, waiting for transfers between devices, to_chip(): return lax.ppermute(rows, 'ctx', [(i, i ^ 2 * k) for i in range(ctx_count)])  5.57 us
    ppermute x9, waiting for transfers between devices, to_head(): return lax.ppermute(rows, 'head', [(j, j ^ m) for j in range(head_count)])  4.12 us
    ppermute x3, waiting for transfers between devices, to_core(): return lax.ppermute(rows, 'ctx', [(i, i ^ 1) for i in range(ctx_count)])  3.39 us
  transfers between devices with their start and end apart: 18, of which 8 were waited for; matrix products, arithmetic and copies ran while one was open for 0% of the time, Pallas kernels for 23%

profile of v1, /device:TPU:0, one launch (start us, length us, event | category | flops | bytes accessed | tf_op | source)
XLA Modules:
  0.0 65.5 jit_solution(7596085809371270709)
XLA Ops:
  0.6 2.0 %keys.1 = (bf16[128,576]{1,0:T(8,128)(2,1)}, bf16[576,128]{1,0:T(8,128)(2,1)}, bf16[144,128]{1,0:T(8,128)(2,1)}) custom-call(bf16[576,128]{1,0:T(8,128)(2,1)} %bitcast.3, bf16[512]{0:T(512)(128)(2,1)} %gain_ref.3), custom_call_target="tpu_custom_call" | custom-call | tf_op jit(solution)/shard_map/keys/pallas_call | solution.py:474
  2.6 5.1 %collective-permute-start.3 = (bf16[144,128]{1,0:T(8,128)(2,1)}, bf16[144,128]{1,0:T(8,128)(2,1)S(1)}, u32[]{:S(2)}, u32[]{:S(2)}) collective-permute-start(bf16[144,128]{1,0:T(8,128)(2,1)} %get-tuple-element.26.refs_3_), channel_id=1, source_target_pairs={{0,24},{4,28},{8,16},{12,20},{16,8},{20,12},{24,0},{28,4},{1,25},{... | collective-permute-start | bytes 110600 | tf_op jit(solution)/shard_map/ppermute | solution.py:469
  7.7 0.6 collective-permute-start.1
  8.4 4.7 %query_rows.1.refs_3_.refs_5_ = bf16[2,1024,576]{2,1,0:T(8,128)(2,1)} custom-call(bf16[128,2048]{1,0:T(8,128)(2,1)} %refs_0_.2, bf16[128,1024]{1,0:T(8,128)(2,1)} %refs_1_.2, bf16[16,128,512]{2,1,0:T(8,128)(2,1)} %w_uk_hbm.1, bf16[144,128]{1,0:T(8,128)(2,1)} %get-tuple-element.26.refs_3_), custom_call_target="tpu_custom_call" | custom-call | flops 268435456 | bytes 6291456 | tf_op jit(solution)/shard_map/query_rows/pallas_call | solution.py:500
  13.1 2.7 %collective-permute-start.6 = (bf16[432,128]{1,0:T(8,128)(2,1)S(1)}, bf16[432,128]{1,0:T(8,128)(2,1)S(1)}, u32[]{:S(2)}, u32[]{:S(2)}) collective-permute-start(bf16[432,128]{1,0:T(8,128)(2,1)S(1)} %get-tuple-element.27.refs_0_), channel_id=1, source_target_pairs={{0,3},{1,2},{2,1},{3,0},{4,7},{5,6},{6,5},{7,4},{8,11},{9,10},{10,... | collective-permute-start | bytes 331784 | tf_op jit(solution)/shard_map/ppermute | solution.py:472
  16.7 4.8 %grad_rows.1.refs_4_.refs_6_ = bf16[2,1040,512]{2,1,0:T(8,128)(2,1)} custom-call(bf16[128,2048]{1,0:T(8,128)(2,1)} %refs_0_.3, bf16[128,2048]{1,0:T(8,128)(2,1)} %refs_1_.3, bf16[16,512,128]{2,1,0:T(8,128)(2,1)} %refs_2_.3, f32[4096,256]{1,0:T(8,128)} %get-tuple-element.28.refs_3_), custom_call_target="tpu_custom_call" | custom-call | flops 268435456 | bytes 6291456 | tf_op jit(solution)/shard_map/grad_rows/pallas_call | solution.py:500
  22.2 1.5 %collective-permute-done.refs_2_ = bf16[576,128]{1,0:T(8,128)(2,1)S(1)} collective-permute-done((bf16[576,128]{1,0:T(8,128)(2,1)S(1)}, bf16[576,128]{1,0:T(8,128)(2,1)S(1)}, u32[]{:S(2)}, u32[]{:S(2)}) %collective-permute-start) | collective-permute-done | bytes 147488 | tf_op jit(solution)/shard_map/ppermute | solution.py:466
  23.7 11.3 %attend.1 = (bf16[1024,576]{1,0:T(8,128)(2,1)S(1)}, bf16[5,256,1024]{2,1,0:T(8,128)(2,1)}, bf16[2304,128]{1,0:T(8,128)(2,1)S(1)}, bf16[2304,128]{1,0:T(8,128)(2,1)S(1)}) custom-call(s32[2,8]{1,0:T(2,128)S(1)} %bitcast.5, bf16[128,576]{1,0:T(8,128)(2,1)S(1)} %copy-done.3, bf16[576,128]{1,0:T(8,128)(2,1)S(1)} %collective-permute-done.refs_2_, ...), custom_call_target="tpu_custom_call" | custom-call | flops 5704253440 | bytes 12582912 | tf_op jit(solution)/shard_map/attend/pallas_call | solution.py:542
  35.1 1.9 %collective-permute-done.8.recv_ref = bf16[2304,128]{1,0:T(8,128)(2,1)S(1)} collective-permute-done((bf16[2304,128]{1,0:T(8,128)(2,1)S(1)}, bf16[2304,128]{1,0:T(8,128)(2,1)S(1)}, u32[]{:S(2)}, u32[]{:S(2)}) %collective-permute-start.8) | collective-permute-done | bytes 589856 | tf_op jit(solution)/shard_map/ppermute | solution.py:466
  37.2 1.7 %collective-permute-start.9 = (bf16[576,128]{1,0:T(8,128)(2,1)S(1)}, bf16[576,128]{1,0:T(8,128)(2,1)S(1)}, u32[]{:S(2)}, u32[]{:S(2)}) collective-permute-start(bf16[576,128]{1,0:T(8,128)(2,1)S(1)} %get-tuple-element.37), channel_id=1, source_target_pairs={{0,1},{1,0},{2,3},{3,2},{4,5},{5,4},{6,7},{7,6},{8,9},{9,8},{10,11... | collective-permute-start | bytes 442376 | tf_op jit(solution)/shard_map/ppermute | solution.py:472
  38.8 1.6 %collective-permute-start.10 = (bf16[576,128]{1,0:T(8,128)(2,1)S(1)}, bf16[576,128]{1,0:T(8,128)(2,1)S(1)}, u32[]{:S(2)}, u32[]{:S(2)}) collective-permute-start(bf16[576,128]{1,0:T(8,128)(2,1)S(1)} %get-tuple-element.38), channel_id=1, source_target_pairs={{0,2},{1,3},{2,0},{3,1},{4,6},{5,7},{6,4},{7,5},{8,10},{9,11},{10,... | collective-permute-start | bytes 442376 | tf_op jit(solution)/shard_map/ppermute | solution.py:472
  40.7 5.9 %query_grads.1 = (bf16[128,2048]{1,0:T(8,128)(2,1)}, bf16[128,1024]{1,0:T(8,128)(2,1)}, f32[8,128]{1,0:T(8,128)S(1)}) custom-call(s32[2,8]{1,0:T(2,128)S(1)} %bitcast.6, bf16[1024,576]{1,0:T(8,128)(2,1)S(1)} %get-tuple-element.30.keys_ref, bf16[5,256,1024]{2,1,0:T(8,128)(2,1)} %get-tuple-element.31.ds_hbm, bf16[16,128,512]{2,1,0:T(8,128)(2,1)} %w_uk_hbm.1, ...), custom_call_target="tpu_custom_call" | custom-call | flops 1509949440 | bytes 8388608 | tf_op jit(solution)/shard_map/query_grads/pallas_call | solution.py:581
  46.7 1.0 %collective-permute-done.10.refs_2_ = bf16[576,128]{1,0:T(8,128)(2,1)S(1)} collective-permute-done((bf16[576,128]{1,0:T(8,128)(2,1)S(1)}, bf16[576,128]{1,0:T(8,128)(2,1)S(1)}, u32[]{:S(2)}, u32[]{:S(2)}) %collective-permute-start.10) | collective-permute-done | bytes 147488 | tf_op jit(solution)/shard_map/ppermute | solution.py:472
  47.7 1.3 %collective-permute-start.12 = (bf16[144,128]{1,0:T(8,128)(2,1)S(1)}, bf16[144,128]{1,0:T(8,128)(2,1)S(1)}, u32[]{:S(2)}, u32[]{:S(2)}) collective-permute-start(bf16[144,128]{1,0:T(8,128)(2,1)S(1)} %get-tuple-element.42), channel_id=1, source_target_pairs={{0,8},{4,12},{8,0},{12,4},{16,24},{20,28},{24,16},{28,20},{1,9},{5... | collective-permute-start | bytes 110600 | tf_op jit(solution)/shard_map/ppermute | solution.py:469
  49.1 2.9 %collective-permute-start.13 = (bf16[144,128]{1,0:T(8,128)(2,1)S(1)}, bf16[144,128]{1,0:T(8,128)(2,1)S(1)}, u32[]{:S(2)}, u32[]{:S(2)}) collective-permute-start(bf16[144,128]{1,0:T(8,128)(2,1)S(1)} %get-tuple-element.43), channel_id=1, source_target_pairs={{0,16},{4,20},{8,24},{12,28},{16,0},{20,4},{24,8},{28,12},{1,17},{... | collective-permute-start | bytes 110600 | tf_op jit(solution)/shard_map/ppermute | solution.py:469
  52.2 2.1 %collective-permute-done.13.refs_2_ = bf16[144,128]{1,0:T(8,128)(2,1)S(1)} collective-permute-done((bf16[144,128]{1,0:T(8,128)(2,1)S(1)}, bf16[144,128]{1,0:T(8,128)(2,1)S(1)}, u32[]{:S(2)}, u32[]{:S(2)}) %collective-permute-start.13) | collective-permute-done | bytes 36896 | tf_op jit(solution)/shard_map/ppermute | solution.py:469
  54.3 3.4 %collective-permute-done.14.refs_3_ = bf16[144,128]{1,0:T(8,128)(2,1)S(1)} collective-permute-done((bf16[144,128]{1,0:T(8,128)(2,1)S(1)}, bf16[144,128]{1,0:T(8,128)(2,1)S(1)}, u32[]{:S(2)}, u32[]{:S(2)}) %collective-permute-start.14) | collective-permute-done | bytes 36896 | tf_op jit(solution)/shard_map/ppermute | solution.py:469
  57.8 1.7 %collective-permute-start.17 = (bf16[144,128]{1,0:T(8,128)(2,1)S(1)}, bf16[144,128]{1,0:T(8,128)(2,1)S(1)}, u32[]{:S(2)}, u32[]{:S(2)}) collective-permute-start(bf16[144,128]{1,0:T(8,128)(2,1)S(1)} %chip_sum.1.refs_0_), channel_id=1, source_target_pairs={{0,3},{1,2},{2,1},{3,0},{4,7},{5,6},{6,5},{7,4},{8,11},{9,10},{10,... | collective-permute-start | bytes 110600 | tf_op jit(solution)/shard_map/ppermute | solution.py:472
  59.5 1.1 %collective-permute-start.16 = (bf16[144,128]{1,0:T(8,128)(2,1)S(1)}, bf16[144,128]{1,0:T(8,128)(2,1)S(1)}, u32[]{:S(2)}, u32[]{:S(2)}) collective-permute-start(bf16[144,128]{1,0:T(8,128)(2,1)S(1)} %chip_sum.1.refs_0_), channel_id=1, source_target_pairs={{0,2},{1,3},{2,0},{3,1},{4,6},{5,7},{6,4},{7,5},{8,10},{9,11},{10,... | collective-permute-start | bytes 110600 | tf_op jit(solution)/shard_map/ppermute | solution.py:472
  60.5 0.8 %collective-permute-start.15 = (bf16[144,128]{1,0:T(8,128)(2,1)S(1)}, bf16[144,128]{1,0:T(8,128)(2,1)S(1)}, u32[]{:S(2)}, u32[]{:S(2)}) collective-permute-start(bf16[144,128]{1,0:T(8,128)(2,1)S(1)} %chip_sum.1.refs_0_), channel_id=1, source_target_pairs={{0,1},{1,0},{2,3},{3,2},{4,5},{5,4},{6,7},{7,6},{8,9},{9,8},{10,11... | collective-permute-start | bytes 110600 | tf_op jit(solution)/shard_map/ppermute | solution.py:472
  61.3 1.4 %collective-permute-done.17.refs_3_ = bf16[144,128]{1,0:T(8,128)(2,1)S(1)} collective-permute-done((bf16[144,128]{1,0:T(8,128)(2,1)S(1)}, bf16[144,128]{1,0:T(8,128)(2,1)S(1)}, u32[]{:S(2)}, u32[]{:S(2)}) %collective-permute-start.17) | collective-permute-done | bytes 36896 | tf_op jit(solution)/shard_map/ppermute | solution.py:472
  62.7 0.7 %collective-permute-done.16.refs_2_ = bf16[144,128]{1,0:T(8,128)(2,1)S(1)} collective-permute-done((bf16[144,128]{1,0:T(8,128)(2,1)S(1)}, bf16[144,128]{1,0:T(8,128)(2,1)S(1)}, u32[]{:S(2)}, u32[]{:S(2)}) %collective-permute-start.16) | collective-permute-done | bytes 36896 | tf_op jit(solution)/shard_map/ppermute | solution.py:472
  63.4 1.1 %collective-permute-done.15.refs_1_ = bf16[144,128]{1,0:T(8,128)(2,1)S(1)} collective-permute-done((bf16[144,128]{1,0:T(8,128)(2,1)S(1)}, bf16[144,128]{1,0:T(8,128)(2,1)S(1)}, u32[]{:S(2)}, u32[]{:S(2)}) %collective-permute-start.15) | collective-permute-done | bytes 36896 | tf_op jit(solution)/shard_map/ppermute | solution.py:472
  64.5 1.0 %norm_back.1 = f32[576,128]{1,0:T(8,128)} custom-call(bf16[576,128]{1,0:T(8,128)(2,1)S(1)} %bitcast.4, bf16[512]{0:T(512)(128)(2,1)S(1)} %copy-done.1, bf16[144,128]{1,0:T(8,128)(2,1)S(1)} %chip_sum.1.refs_0_, bf16[144,128]{1,0:T(8,128)(2,1)S(1)} %collective-permute-done.15.refs_1_, bf16[144,128]{1,0:T(8,128)(2,1)S(1)} %collective-permute-done.16.refs_2_, ...), custom_call_target="tpu_custom_call" | custom-call | tf_op jit(solution)/shard_map/norm_back/pallas_call | solution.py:620
  (33 shorter events, 2.6 us)
Async XLA Ops:
  2.6 10.5 %collective-permute-start.3 = (bf16[144,128]{1,0:T(8,128)(2,1)}, bf16[144,128]{1,0:T(8,128)(2,1)S(1)}, u32[]{:S(2)}, u32[]{:S(2)}) collective-permute-start(bf16[144,128]{1,0:T(8,128)(2,1)} %get-tuple-element.26.refs_3_), channel_id=1, source_target_pairs={{0,24},{4,28},{8,16},{12,20},{16,8},{20,12},{24,0},{28,4},{1,25},{... | collective-permute-start | bytes 110600 | tf_op jit(solution)/shard_map/ppermute | solution.py:469
  7.7 5.4 %collective-permute-start.2 = (bf16[144,128]{1,0:T(8,128)(2,1)}, bf16[144,128]{1,0:T(8,128)(2,1)S(1)}, u32[]{:S(2)}, u32[]{:S(2)}) collective-permute-start(bf16[144,128]{1,0:T(8,128)(2,1)} %get-tuple-element.26.refs_3_), channel_id=1, source_target_pairs={{0,16},{4,20},{8,24},{12,28},{16,0},{20,4},{24,8},{28,12},{1,17},{... | collective-permute-start | bytes 110600 | tf_op jit(solution)/shard_map/ppermute | solution.py:469
  7.7 5.4 %collective-permute-start.1 = (bf16[144,128]{1,0:T(8,128)(2,1)}, bf16[144,128]{1,0:T(8,128)(2,1)S(1)}, u32[]{:S(2)}, u32[]{:S(2)}) collective-permute-start(bf16[144,128]{1,0:T(8,128)(2,1)} %get-tuple-element.26.refs_3_), channel_id=1, source_target_pairs={{0,8},{4,12},{8,0},{12,4},{16,24},{20,28},{24,16},{28,20},{1,9},{5... | collective-permute-start | bytes 110600 | tf_op jit(solution)/shard_map/ppermute | solution.py:469
  13.1 8.4 %collective-permute-start.6 = (bf16[432,128]{1,0:T(8,128)(2,1)S(1)}, bf16[432,128]{1,0:T(8,128)(2,1)S(1)}, u32[]{:S(2)}, u32[]{:S(2)}) collective-permute-start(bf16[432,128]{1,0:T(8,128)(2,1)S(1)} %get-tuple-element.27.refs_0_), channel_id=1, source_target_pairs={{0,3},{1,2},{2,1},{3,0},{4,7},{5,6},{6,5},{7,4},{8,11},{9,10},{10,... | collective-permute-start | bytes 331784 | tf_op jit(solution)/shard_map/ppermute | solution.py:472
  15.8 5.7 %collective-permute-start.5 = (bf16[432,128]{1,0:T(8,128)(2,1)S(1)}, bf16[432,128]{1,0:T(8,128)(2,1)S(1)}, u32[]{:S(2)}, u32[]{:S(2)}) collective-permute-start(bf16[432,128]{1,0:T(8,128)(2,1)S(1)} %get-tuple-element.27.refs_0_), channel_id=1, source_target_pairs={{0,2},{1,3},{2,0},{3,1},{4,6},{5,7},{6,4},{7,5},{8,10},{9,11},{10,... | collective-permute-start | bytes 331784 | tf_op jit(solution)/shard_map/ppermute | solution.py:472
  16.3 5.2 %collective-permute-start.4 = (bf16[432,128]{1,0:T(8,128)(2,1)S(1)}, bf16[432,128]{1,0:T(8,128)(2,1)S(1)}, u32[]{:S(2)}, u32[]{:S(2)}) collective-permute-start(bf16[432,128]{1,0:T(8,128)(2,1)S(1)} %get-tuple-element.27.refs_0_), channel_id=1, source_target_pairs={{0,1},{1,0},{2,3},{3,2},{4,5},{5,4},{6,7},{7,6},{8,9},{9,8},{10,11... | collective-permute-start | bytes 331784 | tf_op jit(solution)/shard_map/ppermute | solution.py:472
  16.7 5.0 %copy-start.4 = (bf16[576,128]{1,0:T(8,128)(2,1)S(1)}, bf16[576,128]{1,0:T(8,128)(2,1)}, u32[]{:S(2)}) copy-start(bf16[576,128]{1,0:T(8,128)(2,1)} %get-tuple-element.25) | copy-start | bytes 442372
  16.7 7.0 %copy-start.2 = (s32[8,2]{0,1:T(2,128)S(1)}, s32[8,2]{0,1:T(2,128)}, u32[]{:S(2)}) copy-start(s32[8,2]{0,1:T(2,128)} %param.17) | copy-start | bytes 196
  16.7 7.0 %copy-start.3 = (bf16[128,576]{1,0:T(8,128)(2,1)S(1)}, bf16[128,576]{1,0:T(8,128)(2,1)}, u32[]{:S(2)}) copy-start(bf16[128,576]{1,0:T(8,128)(2,1)} %get-tuple-element.24.refs_1_) | copy-start | bytes 442372
  21.6 2.1 %collective-permute-start.7 = (bf16[1728,128]{1,0:T(8,128)(2,1)S(1)}, bf16[1728,128]{1,0:T(8,128)(2,1)S(1)}, u32[]{:S(2)}, u32[]{:S(2)}) collective-permute-start(bf16[1728,128]{1,0:T(8,128)(2,1)S(1)} %get-tuple-element.29.refs_3_), channel_id=1, source_target_pairs={{0,4},{4,0},{8,12},{12,8},{16,20},{20,16},{24,28},{28,24},{1,5},{5... | collective-permute-start | bytes 1327112 | tf_op jit(solution)/shard_map/ppermute | solution.py:466
  21.7 2.0 %collective-permute-start = (bf16[576,128]{1,0:T(8,128)(2,1)S(1)}, bf16[576,128]{1,0:T(8,128)(2,1)S(1)}, u32[]{:S(2)}, u32[]{:S(2)}) collective-permute-start(bf16[576,128]{1,0:T(8,128)(2,1)S(1)} %copy-done.4), channel_id=1, source_target_pairs={{0,4},{4,0},{8,12},{12,8},{16,20},{20,16},{24,28},{28,24},{1,5},{5... | collective-permute-start | bytes 442376 | tf_op jit(solution)/shard_map/ppermute | solution.py:466
  35.0 2.1 %collective-permute-start.8 = (bf16[2304,128]{1,0:T(8,128)(2,1)S(1)}, bf16[2304,128]{1,0:T(8,128)(2,1)S(1)}, u32[]{:S(2)}, u32[]{:S(2)}) collective-permute-start(bf16[2304,128]{1,0:T(8,128)(2,1)S(1)} %get-tuple-element.33), channel_id=1, source_target_pairs={{0,4},{4,0},{8,12},{12,8},{16,20},{20,16},{24,28},{28,24},{1,5},{5... | collective-permute-start | bytes 1769480 | tf_op jit(solution)/shard_map/ppermute | solution.py:466
  37.2 9.5 %collective-permute-start.9 = (bf16[576,128]{1,0:T(8,128)(2,1)S(1)}, bf16[576,128]{1,0:T(8,128)(2,1)S(1)}, u32[]{:S(2)}, u32[]{:S(2)}) collective-permute-start(bf16[576,128]{1,0:T(8,128)(2,1)S(1)} %get-tuple-element.37), channel_id=1, source_target_pairs={{0,1},{1,0},{2,3},{3,2},{4,5},{5,4},{6,7},{7,6},{8,9},{9,8},{10,11... | collective-permute-start | bytes 442376 | tf_op jit(solution)/shard_map/ppermute | solution.py:472
  38.8 8.8 %collective-permute-start.10 = (bf16[576,128]{1,0:T(8,128)(2,1)S(1)}, bf16[576,128]{1,0:T(8,128)(2,1)S(1)}, u32[]{:S(2)}, u32[]{:S(2)}) collective-permute-start(bf16[576,128]{1,0:T(8,128)(2,1)S(1)} %get-tuple-element.38), channel_id=1, source_target_pairs={{0,2},{1,3},{2,0},{3,1},{4,6},{5,7},{6,4},{7,5},{8,10},{9,11},{10,... | collective-permute-start | bytes 442376 | tf_op jit(solution)/shard_map/ppermute | solution.py:472
  40.4 7.2 %collective-permute-start.11 = (bf16[576,128]{1,0:T(8,128)(2,1)S(1)}, bf16[576,128]{1,0:T(8,128)(2,1)S(1)}, u32[]{:S(2)}, u32[]{:S(2)}) collective-permute-start(bf16[576,128]{1,0:T(8,128)(2,1)S(1)} %get-tuple-element.39), channel_id=1, source_target_pairs={{0,3},{1,2},{2,1},{3,0},{4,7},{5,6},{6,5},{7,4},{8,11},{9,10},{10,... | collective-permute-start | bytes 442376 | tf_op jit(solution)/shard_map/ppermute | solution.py:472
  40.7 23.8 %copy-start = (bf16[128,576]{0,1:T(8,128)(2,1)S(1)}, bf16[128,576]{0,1:T(8,128)(2,1)}, u32[]{:S(2)}) copy-start(bf16[128,576]{0,1:T(8,128)(2,1)} %param.11) | copy-start | bytes 442372
  40.7 23.8 %copy-start.1 = (bf16[512]{0:T(512)(128)(2,1)S(1)}, bf16[512]{0:T(512)(128)(2,1)}, u32[]{:S(2)}) copy-start(bf16[512]{0:T(512)(128)(2,1)} %gain_ref.3) | copy-start | bytes 3076
  47.7 4.5 %collective-permute-start.12 = (bf16[144,128]{1,0:T(8,128)(2,1)S(1)}, bf16[144,128]{1,0:T(8,128)(2,1)S(1)}, u32[]{:S(2)}, u32[]{:S(2)}) collective-permute-start(bf16[144,128]{1,0:T(8,128)(2,1)S(1)} %get-tuple-element.42), channel_id=1, source_target_pairs={{0,8},{4,12},{8,0},{12,4},{16,24},{20,28},{24,16},{28,20},{1,9},{5... | collective-permute-start | bytes 110600 | tf_op jit(solution)/shard_map/ppermute | solution.py:469
  49.1 5.3 %collective-permute-start.13 = (bf16[144,128]{1,0:T(8,128)(2,1)S(1)}, bf16[144,128]{1,0:T(8,128)(2,1)S(1)}, u32[]{:S(2)}, u32[]{:S(2)}) collective-permute-start(bf16[144,128]{1,0:T(8,128)(2,1)S(1)} %get-tuple-element.43), channel_id=1, source_target_pairs={{0,16},{4,20},{8,24},{12,28},{16,0},{20,4},{24,8},{28,12},{1,17},{... | collective-permute-start | bytes 110600 | tf_op jit(solution)/shard_map/ppermute | solution.py:469
  52.0 5.8 %collective-permute-start.14 = (bf16[144,128]{1,0:T(8,128)(2,1)S(1)}, bf16[144,128]{1,0:T(8,128)(2,1)S(1)}, u32[]{:S(2)}, u32[]{:S(2)}) collective-permute-start(bf16[144,128]{1,0:T(8,128)(2,1)S(1)} %get-tuple-element.44), channel_id=1, source_target_pairs={{0,24},{4,28},{8,16},{12,20},{16,8},{20,12},{24,0},{28,4},{1,25},{... | collective-permute-start | bytes 110600 | tf_op jit(solution)/shard_map/ppermute | solution.py:469
  57.8 4.9 %collective-permute-start.17 = (bf16[144,128]{1,0:T(8,128)(2,1)S(1)}, bf16[144,128]{1,0:T(8,128)(2,1)S(1)}, u32[]{:S(2)}, u32[]{:S(2)}) collective-permute-start(bf16[144,128]{1,0:T(8,128)(2,1)S(1)} %chip_sum.1.refs_0_), channel_id=1, source_target_pairs={{0,3},{1,2},{2,1},{3,0},{4,7},{5,6},{6,5},{7,4},{8,11},{9,10},{10,... | collective-permute-start | bytes 110600 | tf_op jit(solution)/shard_map/ppermute | solution.py:472
  59.5 4.0 %collective-permute-start.16 = (bf16[144,128]{1,0:T(8,128)(2,1)S(1)}, bf16[144,128]{1,0:T(8,128)(2,1)S(1)}, u32[]{:S(2)}, u32[]{:S(2)}) collective-permute-start(bf16[144,128]{1,0:T(8,128)(2,1)S(1)} %chip_sum.1.refs_0_), channel_id=1, source_target_pairs={{0,2},{1,3},{2,0},{3,1},{4,6},{5,7},{6,4},{7,5},{8,10},{9,11},{10,... | collective-permute-start | bytes 110600 | tf_op jit(solution)/shard_map/ppermute | solution.py:472
  60.5 4.0 %collective-permute-start.15 = (bf16[144,128]{1,0:T(8,128)(2,1)S(1)}, bf16[144,128]{1,0:T(8,128)(2,1)S(1)}, u32[]{:S(2)}, u32[]{:S(2)}) collective-permute-start(bf16[144,128]{1,0:T(8,128)(2,1)S(1)} %chip_sum.1.refs_0_), channel_id=1, source_target_pairs={{0,1},{1,0},{2,3},{3,2},{4,5},{5,4},{6,7},{7,6},{8,9},{9,8},{10,11... | collective-permute-start | bytes 110600 | tf_op jit(solution)/shard_map/ppermute | solution.py:472

commit v2 on v1

v2 whole, which is shorter than its diff:
```python
import functools

import jax
import jax.numpy as jnp
from jax import lax
from jax.experimental import pallas as pl
from jax.experimental.pallas import tpu as pltpu
from jax.sharding import PartitionSpec as P

neg_big = -1e30
eps_norm = 1e-06
log2_e = 1.4426950408889634
key_tile = 128
mib = 1024 * 1024
piece_mib = 53.8
query_mib = 16
attend_mib = 36
project_mib = 12
window_flops = 8 * 10**9
delta_rows = 16
row_chunk = 256
f32 = jnp.float32
bf16 = jnp.bfloat16
in_vmem = pl.BlockSpec(memory_space=pltpu.VMEM)
in_hbm = pl.BlockSpec(memory_space=pltpu.HBM)
in_any = pl.BlockSpec(memory_space=pl.ANY)
in_smem = pl.BlockSpec(memory_space=pltpu.SMEM)


def dot_nn(left, right):
    return lax.dot_general(left, right, (((1,), (0,)), ((), ())), preferred_element_type=f32)


def dot_nt(left, right):
    return lax.dot_general(left, right, (((1,), (1,)), ((), ())), preferred_element_type=f32)


def dot_tn(left, right):
    return lax.dot_general(left, right, (((0,), (0,)), ((), ())), preferred_element_type=f32)


def fold(block, on):
    if not on:
        return block
    rows, width = block.shape
    whole = width // 128
    half = rows // 2
    last = jnp.concatenate([block[:half, whole * 128 :], block[half:, whole * 128 :]], axis=1)
    return jnp.concatenate([block[:, j * 128 : (j + 1) * 128] for j in range(whole)] + [last], axis=0)


def unfold(block, width, on):
    if not on:
        return block
    rows = block.shape[0] * 128 // width
    whole = width // 128
    last = block[whole * rows :]
    edge = jnp.concatenate([last[:, : width - whole * 128], last[:, width - whole * 128 :]], axis=0)
    return jnp.concatenate([block[j * rows : (j + 1) * rows] for j in range(whole)] + [edge], axis=1)


def folded(rows, width, on):
    return (rows * width // 128, 128) if on else (rows, width)


def params(size):
    return pltpu.CompilerParams(vmem_limit_bytes=int(size * mib))


def piece_kernel(cache_t_hbm, piece_ref, cache_scr, rows_scr, sem):
    copy = pltpu.make_async_copy(cache_t_hbm, cache_scr, sem)
    copy.start()
    copy.wait()
    rows_scr[...] = jnp.transpose(cache_scr[...].astype(f32))
    rows = rows_scr.shape[0] // lax.axis_size("head")
    start = pl.multiple_of(lax.axis_index("head") * rows, rows)
    piece_ref[...] = fold(rows_scr[pl.ds(start, rows), :], rows % 32 == 0).astype(bf16)


def normalised(rows, gain):
    width = gain.shape[1]
    latent = rows[:, :width]
    inverse = lax.rsqrt(jnp.mean(latent * latent, axis=1, keepdims=True) + eps_norm)
    return jnp.concatenate([latent * inverse * gain, rows[:, width:]], axis=1)


def own_kernel(on, cache_t_ref, gain_ref, out_ref):
    rows = jnp.transpose(cache_t_ref[...].astype(f32))
    out_ref[...] = fold(normalised(rows, gain_ref[...].astype(f32)[None, :]), on).astype(bf16)


def join_chips_kernel(on, width, gain_ref, *refs):
    gain = gain_ref[...].astype(f32)[None, :]
    rows = jnp.concatenate([unfold(ref[...].astype(f32), width, on) for ref in refs[:-1]], axis=0)
    rows = normalised(rows, gain)
    size = rows.shape[0] // (len(refs) - 1)
    parts = [fold(rows[i * size : (i + 1) * size], on) for i in range(len(refs) - 1)]
    refs[-1][...] = jnp.concatenate(parts, axis=0).astype(bf16)


def project_kernel(
    factor, nope_ref, rope_ref, w_uk_ref, grad_ref, out_ref, w_uv_ref, unused_ref, q_ref, dl_ref, delta_scr
):
    heads, lat_width, value_width = w_uv_ref.shape
    nope_width = w_uk_ref.shape[1]
    span = grad_ref.shape[0] // 2
    rope_width = rope_ref.shape[1] // heads
    row_count = heads * span
    pairs = heads // 2
    ones = jnp.ones((8, value_width), bf16)
    for i in range(pairs):
        rope = (rope_ref[:, 2 * i * rope_width : 2 * (i + 1) * rope_width].astype(f32) * factor).astype(bf16)
        wide = slice(2 * i * value_width, 2 * (i + 1) * value_width)
        products = grad_ref[:, wide].astype(f32) * out_ref[:, wide].astype(f32)
        for p in range(2):
            head = 2 * i + p
            rows = slice(head * span, (head + 1) * span)
            q_lat = dot_nn(nope_ref[:, head * nope_width : (head + 1) * nope_width], w_uk_ref[head])
            q_lat = (q_lat * factor).astype(bf16)
            d_lat = dot_nt(grad_ref[:, head * value_width : (head + 1) * value_width], w_uv_ref[head]).astype(bf16)
            for s in range(2):
                tokens = slice(s * span, (s + 1) * span)
                q_ref[s, rows, :lat_width] = q_lat[tokens]
                q_ref[s, rows, lat_width:] = rope[tokens, p * rope_width : (p + 1) * rope_width]
                dl_ref[s, rows, :] = d_lat[tokens]
        for s in range(2):
            tokens = slice(s * span, (s + 1) * span)
            product = jnp.concatenate([products[tokens, :value_width], products[tokens, value_width:]], axis=0)
            high = product.astype(bf16)
            low = (product - high.astype(f32)).astype(bf16)
            delta_scr[i, s] = dot_nt(ones, high) + dot_nt(ones, low)

    per_row = min(lat_width // (2 * span), pairs)
    for s in range(2):
        rows = []
        for start in range(0, pairs, per_row):
            rows.append(jnp.concatenate([delta_scr[i, s, :1] for i in range(start, start + per_row)], axis=1))
        width = rows[0].shape[1]
        full = jnp.concatenate(rows + [jnp.zeros((8 - len(rows), width), f32)], axis=0)
        high = full.astype(bf16).astype(f32)
        both = jnp.concatenate([high, full - high], axis=0)
        if width < lat_width:
            both = jnp.concatenate([both, jnp.zeros((delta_rows, lat_width - width), f32)], axis=1)
        dl_ref[s, row_count:, :] = both.astype(bf16)


def join_kernel(*refs):
    if any(ref.shape[0] % 16 for ref in refs):
        refs[-1][...] = jnp.concatenate([ref[...].astype(f32) for ref in refs[:-1]], axis=0).astype(bf16)
        return
    start = 0
    for ref in refs[:-1]:
        size = ref.shape[0]
        refs[-1][start : start + size, :] = ref[...]
        start += size


def tile_groups(tile_count):
    pairs = [(u, u + 2) for u in range(0, tile_count // 2, 2)]
    return pairs + [(u, u + 1) for u in range(tile_count // 2, tile_count + 1)]


def tile_place(u, tile_count, span, lower_block):
    per_tile = key_tile // span
    upper_count = (tile_count * per_tile - 1 - lower_block) // per_tile + 1
    if u <= tile_count // 2:
        return True, u
    if u == tile_count:
        return False, 0
    is_upper = u < upper_count
    return is_upper, jnp.where(is_upper, u, tile_count - u)


def pick(is_upper, upper, lower):
    if isinstance(is_upper, bool):
        return upper if is_upper else lower
    return jnp.where(is_upper, upper, lower)


def half_of(is_upper):
    return int(is_upper) if isinstance(is_upper, bool) else is_upper.astype(jnp.int32)


def tile_rows(kt, count=1):
    if isinstance(kt, int):
        return slice(kt * key_tile, (kt + count) * key_tile)
    return pl.ds(pl.multiple_of(kt * key_tile, key_tile), key_tile)


def attend_kernel(head_count, *refs):
    span_ref, own_pieces, sib_pieces, q_ref, dl_ref, keys_ref, ds_ref, keep_ref, send_ref = refs[:-5]
    e_scr, score_part, prob_part, prob_scr, raw = refs[-5:]
    half_count, row_count, cat_width = q_ref.shape
    lat_width = dl_ref.shape[2]
    total = keys_ref.shape[0]
    tile_count = total // key_tile
    z_count = lax.axis_size("ctx") // 2
    tok_rows = total // z_count // 2
    span = tok_rows // 2
    piece_rows = tok_rows // head_count
    per_span = span // piece_rows
    me, head = lax.axis_index("ctx"), lax.axis_index("head")
    z, core = me // 2, lax.rem(me, 2)
    on = piece_rows % 32 == 0
    own_size = folded(tok_rows, cat_width, on)[0]
    piece_size = folded(piece_rows, cat_width, on)[0]

    def place(owner, quarter):
        block = span_ref[quarter // per_span, owner]
        start = block * span + lax.rem(quarter, per_span) * piece_rows
        return pl.ds(pl.multiple_of(start, piece_rows), piece_rows)

    stage = keys_ref if piece_rows % 16 == 0 else raw
    for side, ref in enumerate((own_pieces, sib_pieces)):
        source = ref if piece_rows % 16 == 0 else ref[...].astype(f32)
        rows = unfold(source[:own_size, :], cat_width, on)
        for s in range(2):
            start = pl.multiple_of(span_ref[s, 2 * z + lax.rem(core + side, 2)] * span, span)
            stage[pl.ds(start, span), :] = rows[s * span : (s + 1) * span, :]
        start = own_size
        for m in range(head_count):
            for k in range(1, z_count):
                owner = 2 * (z ^ k) + lax.rem(core + side, 2)
                stage[place(owner, head ^ m), :] = unfold(source[start : start + piece_size, :], cat_width, on)
                start += piece_size
    if stage is raw:
        keys_ref[...] = raw[...].astype(bf16)

    my_lower, my_upper = span_ref[0, me], span_ref[1, me]
    chunks = [slice(n, n + min(row_chunk, row_count)) for n in range(0, row_count, row_chunk)]
    groups = tile_groups(tile_count)
    counts = [last - first for first, last in groups]
    tiles = [slice(first * key_tile, last * key_tile) for first, last in groups]
    places = [tile_place(first, tile_count, span, my_lower) for first, last in groups]
    work = [(g, chunk) for g in range(len(groups)) for chunk in chunks]
    step_shape = (key_tile, min(row_chunk, row_count))
    key_step = lax.broadcasted_iota(jnp.int32, step_shape, 0)
    row_step = lax.rem(lax.broadcasted_iota(jnp.int32, step_shape, 1), span)
    step = row_step - key_step

    def score_dot(u, chunk):
        is_upper, kt = places[u]
        return dot_nt(keys_ref[tile_rows(kt, counts[u]), :], q_ref[half_of(is_upper), chunk])

    top_parts, sum_parts = {}, {}
    ahead = score_dot(*work[0])
    for i, (u, chunk) in enumerate(work):
        scores = ahead
        if i + 1 < len(work):
            ahead = score_dot(*work[i + 1])
        is_upper, kt = places[u]
        if groups[u][0] >= tile_count // 2:
            base = kt * key_tile - pick(is_upper, my_upper, my_lower) * span
            scores = jnp.where(step >= base, scores, neg_big)
        top = jnp.max(scores, axis=0, keepdims=True)
        weights = jnp.exp2(scores - top)
        e_scr[tiles[u], chunk] = weights
        top_parts.setdefault(u, []).append(top)
        sum_parts.setdefault(u, []).append(jnp.sum(weights, axis=0, keepdims=True))
    tops = [jnp.concatenate(top_parts[u], axis=1) for u in range(len(groups))]
    sums = [jnp.concatenate(sum_parts[u], axis=1) for u in range(len(groups))]

    def prob_dot(u, chunk):
        is_upper, kt = places[u]
        return dot_nt(keys_ref[tile_rows(kt, counts[u]), :lat_width], dl_ref[half_of(is_upper), chunk])

    ahead = prob_dot(*work[0])
    row_top, row_sum = [], []
    for s in range(2):
        kept = [jnp.where(half_of(is_upper) == s, top, neg_big) for (is_upper, kt), top in zip(places, tops)]
        best = functools.reduce(jnp.maximum, kept)
        row_top.append(best)
        row_sum.append(functools.reduce(jnp.add, [jnp.exp2(top - best) * add for top, add in zip(kept, sums)]))
    inverse = [1.0 / part for part in row_sum]
    factors = []
    for (is_upper, kt), top in zip(places, tops):
        best = pick(is_upper, row_top[1], row_top[0])
        factors.append(jnp.exp2(top - best) * pick(is_upper, inverse[1], inverse[0]))
    deltas = []
    for s in range(2):
        parts = dl_ref[s, row_count:, :].astype(f32)
        width = min(lat_width, row_count)
        rows = [parts[j : j + 1, :width] + parts[8 + j : 9 + j, :width] for j in range(row_count // width)]
        deltas.append(jnp.concatenate(rows, axis=1))
    sure = (tile_count // 2 + 1) * key_tile
    score_part[sure:, :] = jnp.zeros((total - sure, cat_width), f32)
    prob_part[sure:, :] = jnp.zeros((total - sure, lat_width), f32)

    def key_grads(u, source, target, rhs, first, last):
        is_upper, kt = places[u]
        part = dot_nn(source[...], rhs[half_of(is_upper), :row_count, first:last])
        if groups[u][0] <= tile_count // 2:
            target[tile_rows(kt, counts[u]), first:last] = part
        else:
            target[tile_rows(kt, counts[u]), first:last] += part

    def key_steps(u):
        widths = [(first, min(first + 256, cat_width)) for first in range(0, cat_width, 256)]
        steps = []
        for first, last in widths:
            steps.append(functools.partial(key_grads, u, ds_ref.at[tiles[u]], score_part, q_ref, first, last))
            if last <= lat_width:
                steps.append(functools.partial(key_grads, u, prob_scr.at[u % 2, : counts[u] * key_tile], prob_part, dl_ref, first, last))
        return steps

    pending = []
    for i, (u, chunk) in enumerate(work):
        d_prob = ahead
        if i + 1 < len(work):
            ahead = prob_dot(*work[i + 1])
        left = len(chunks) - i % len(chunks)
        for j in range(-(-len(pending) // left)):
            pending.pop(0)()
        is_upper, kt = places[u]
        delta = pick(is_upper, deltas[1], deltas[0])
        prob = e_scr[tiles[u], chunk] * factors[u][:, chunk]
        ds_ref[tiles[u], chunk] = (prob * (d_prob - delta[:, chunk])).astype(bf16)
        prob_scr[u % 2, : counts[u] * key_tile, chunk] = prob.astype(bf16)
        if left == 1:
            pending = key_steps(u)
    for key_step in pending:
        key_step()

    for side, ref in ((0, keep_ref), (1, send_ref)):
        for quarter in range(head_count):
            rows = []
            for other in range(z_count):
                here = place(2 * other + lax.rem(core + side, 2), jnp.int32(quarter))
                block = score_part[here, :] * (1.0 / log2_e)
                latent = block[:, :lat_width] + prob_part[here, :]
                rows.append(fold(jnp.concatenate([latent, block[:, lat_width:]], axis=1), on))
            size = z_count * piece_size
            ref[quarter * size : (quarter + 1) * size, :] = jnp.concatenate(rows, axis=0).astype(bf16)


def query_kernel(
    scale, span_ref, keys_ref, ds_ref, w_uk_ref, nope_ref, rope_ref, dq_scr
):
    tile_total, row_count = ds_ref.shape[0] // key_tile, ds_ref.shape[1]
    tile_count = tile_total - 1
    heads, nope_width, lat_width = w_uk_ref.shape
    span = row_count // heads
    cat_width = keys_ref.shape[1]
    my_lower = span_ref[0, lax.axis_index("ctx")]
    places = [tile_place(u, tile_count, span, my_lower) for u in range(tile_total)]
    sure = tile_count // 2 + 1
    dq_scr[1] = dot_tn(keys_ref[: sure * key_tile, :], ds_ref[: sure * key_tile, :])
    dq_scr[0] = dot_tn(keys_ref[:key_tile, :], ds_ref[tile_count * key_tile :, :])
    for u, (is_upper, kt) in enumerate(places):
        if not isinstance(is_upper, bool):
            dq_scr[half_of(is_upper)] += dot_tn(keys_ref[tile_rows(kt), :], ds_ref[tile_rows(u), :])
    for pair in range(heads // 2):
        wide = slice(pair * 2 * span, (pair + 1) * 2 * span)
        turned = [jnp.transpose(dq_scr[s, :, wide]) * scale for s in range(2)]
        for p in range(2):
            head = 2 * pair + p
            rows = jnp.concatenate([t[p * span : (p + 1) * span, :lat_width] for t in turned], axis=0)
            nope_ref[:, head * nope_width : (head + 1) * nope_width] = dot_nt(
                rows.astype(bf16), w_uk_ref[head]
            ).astype(bf16)
        rope = [
            jnp.concatenate([t[p * span : (p + 1) * span, lat_width:] for t in turned], axis=0) for p in range(2)
        ]
        width = 2 * (cat_width - lat_width)
        rope_ref[:, pair * width : (pair + 1) * width] = jnp.concatenate(rope, axis=1).astype(bf16)


def pair_sum_kernel(keep_ref, recv_ref, own_ref, *send_refs):
    head = lax.axis_index("head")
    share = own_ref.shape[0]

    def both(target):
        rows = pl.ds(pl.multiple_of(target * share, share), share)
        return keep_ref[rows, :].astype(f32) + recv_ref[rows, :].astype(f32)

    own_ref[...] = both(head)
    for m, ref in zip(range(len(send_refs), 0, -1), send_refs):
        ref[...] = both(head ^ m).astype(bf16)


def head_sum_kernel(*refs):
    z_count = refs[0].shape[0] // refs[-2].shape[0]
    head_count = len(refs) - 1 - z_count
    terms, own_ref, send_refs, total = refs[:head_count], refs[head_count], refs[head_count + 1 : -1], refs[-1]
    total[...] = functools.reduce(jnp.add, [ref[...].astype(f32) for ref in terms])
    rows = own_ref.shape[0]
    z = lax.axis_index("ctx") // 2

    def share(k):
        return total[pl.ds(pl.multiple_of((z ^ k) * rows, rows), rows), :]

    own_ref[...] = share(0)
    for k, ref in zip(range(len(send_refs), 0, -1), send_refs):
        ref[...] = share(k).astype(bf16)


def chip_sum_kernel(*refs):
    refs[-1][...] = functools.reduce(jnp.add, [ref[...].astype(f32) for ref in refs[:-1]]).astype(bf16)


def norm_back_kernel(cache_t_ref, gain_ref, *refs):
    shares, out_ref, total = refs[:-2], refs[-2], refs[-1]
    head = lax.axis_index("head")
    rows = total.shape[0] // len(shares)
    lat_width = gain_ref.shape[0]
    for m, ref in enumerate(shares):
        total[pl.ds(pl.multiple_of((head ^ m) * rows, rows), rows), :] = unfold(
            ref[...].astype(f32), total.shape[1], rows % 32 == 0
        )
    values = cache_t_ref[:lat_width, :].astype(f32)
    inverse = lax.rsqrt(jnp.mean(values * values, axis=0, keepdims=True) + eps_norm)
    scaled = jnp.transpose(total[:, :lat_width] * gain_ref[...].astype(f32)[None, :])
    inner = jnp.mean(values * scaled, axis=0, keepdims=True)
    out_ref[:lat_width, :] = inverse * scaled - values * (inverse * inverse * inverse * inner)
    out_ref[lat_width:, :] = jnp.transpose(total[:, lat_width:])


def local(q_nope, q_rope, kv_cache, kv_gain, w_uk, w_uv, attn_out, d_out, span_table):
    shape = jax.ShapeDtypeStruct
    tok_rows, cat_width = kv_cache.shape
    heads, nope_width, lat_width = w_uk.shape
    value_width = w_uv.shape[2]
    rope_width = q_rope.shape[1] // heads
    span = tok_rows // 2
    row_count = span * heads
    scale = float(nope_width + rope_width) ** (-0.5)
    ctx_count, head_count = lax.axis_size("ctx"), lax.axis_size("head")
    z_count = ctx_count // 2
    total = ctx_count * tok_rows
    tile_total = total // key_tile + 1
    piece_rows = tok_rows // head_count
    cache_t = kv_cache.T
    spans = span_table.T

    def to_core(rows):
        return lax.ppermute(rows, "ctx", [(i, i ^ 1) for i in range(ctx_count)])

    def to_chip(rows, k):
        return lax.ppermute(rows, "ctx", [(i, i ^ (2 * k)) for i in range(ctx_count)])

    def to_head(rows, m):
        return lax.ppermute(rows, "head", [(j, j ^ m) for j in range(head_count)])

    on = piece_rows % 32 == 0
    piece = pl.pallas_call(
        piece_kernel,
        out_shape=shape(folded(piece_rows, cat_width, on), bf16),
        in_specs=[in_any],
        out_specs=in_vmem,
        scratch_shapes=[
            pltpu.VMEM((cat_width, tok_rows), bf16),
            pltpu.VMEM((tok_rows, cat_width), f32),
            pltpu.SemaphoreType.DMA,
        ],
        compiler_params=params(piece_mib),
        name="piece",
    )(cache_t)
    pieces = [to_chip(piece, k) for k in range(1, z_count)]
    keys_own = pl.pallas_call(
        functools.partial(own_kernel, on),
        out_shape=shape(folded(tok_rows, cat_width, on), bf16),
        in_specs=[in_vmem] * 2,
        out_specs=in_vmem,
        compiler_params=params(8),
        cost_estimate=pl.CostEstimate(flops=window_flops, bytes_accessed=mib, transcendentals=0),
        name="own_keys",
    )(cache_t, kv_gain)
    *pieces, keys_own = lax.optimization_barrier((*pieces, keys_own))
    pieces = pl.pallas_call(
        functools.partial(join_chips_kernel, on, cat_width),
        out_shape=shape(((z_count - 1) * piece.shape[0], piece.shape[1]), bf16),
        in_specs=[in_vmem] * z_count,
        out_specs=in_vmem,
        compiler_params=params(8),
        name="join_chips",
    )(kv_gain, *pieces)

    def join(rows, name):
        return pl.pallas_call(
            join_kernel,
            out_shape=shape((sum(r.shape[0] for r in rows), rows[0].shape[1]), bf16),
            in_specs=[in_vmem] * len(rows),
            out_specs=in_vmem,
            compiler_params=params(4),
            name=name,
        )(*rows)

    queries, d_latent = pl.pallas_call(
        functools.partial(project_kernel, scale * log2_e),
        out_shape=(shape((2, row_count, cat_width), bf16), shape((2, row_count + delta_rows, lat_width), bf16)),
        in_specs=[in_vmem] * 6 + [in_any],
        out_specs=(in_vmem,) * 2,
        scratch_shapes=[pltpu.VMEM((heads // 2, 2, 8, 2 * span), f32)],
        compiler_params=params(project_mib),
        cost_estimate=pl.CostEstimate(
            flops=8 * row_count * nope_width * lat_width, bytes_accessed=12 * mib, transcendentals=0
        ),
        name="project",
    )(q_nope, q_rope, w_uk, d_out, attn_out, w_uv, pieces)
    pieces = [pieces] + [to_head(pieces, m) for m in range(1, head_count)]
    *pieces, queries, d_latent = lax.optimization_barrier((*pieces, queries, d_latent))
    pieces = join([keys_own] + pieces, "join_heads")
    sib_pieces = to_core(pieces)

    piece_shape = piece.shape
    share_shape = (z_count * piece_shape[0], piece_shape[1])
    all_shape = (head_count * share_shape[0], piece_shape[1])
    keys, d_score, keep, send = pl.pallas_call(
        functools.partial(attend_kernel, head_count),
        out_shape=(
            shape((total, cat_width), bf16),
            shape((tile_total * key_tile, row_count), bf16),
            shape(all_shape, bf16),
            shape(all_shape, bf16),
        ),
        in_specs=[in_smem] + [in_vmem] * 4,
        out_specs=(in_vmem,) * 4,
        scratch_shapes=[
            pltpu.VMEM((tile_total * key_tile, row_count), f32),
            pltpu.VMEM((total, cat_width), f32),
            pltpu.VMEM((total, lat_width), f32),
            pltpu.VMEM((2, 2 * key_tile, row_count), bf16),
            pltpu.VMEM((8, 128) if piece_rows % 16 == 0 else (total, cat_width), f32),
        ],
        compiler_params=params(attend_mib if total <= 2048 else 56),
        cost_estimate=pl.CostEstimate(
            flops=2 * tile_total * key_tile * row_count * (2 * cat_width + 2 * lat_width),
            bytes_accessed=12 * mib,
            transcendentals=tile_total * key_tile * row_count,
        ),
        name="attend",
    )(spans, pieces, sib_pieces, queries, d_latent)

    recv = to_core(send)
    sums = pl.pallas_call(
        pair_sum_kernel,
        out_shape=(shape(share_shape, f32),) + (shape(share_shape, bf16),) * (head_count - 1),
        in_specs=[in_vmem] * 2,
        out_specs=(in_vmem,) * head_count,
        compiler_params=params(4),
        name="pair_sum",
    )(keep, recv)
    *sums, d_score = lax.optimization_barrier((*sums, d_score))
    d_q_nope, d_q_rope = pl.pallas_call(
        functools.partial(query_kernel, scale),
        out_shape=(shape(q_nope.shape, bf16), shape(q_rope.shape, bf16)),
        in_specs=[in_smem] + [in_vmem] * 3,
        out_specs=(in_vmem,) * 2,
        scratch_shapes=[pltpu.VMEM((2, cat_width, row_count), f32)],
        compiler_params=params(query_mib),
        cost_estimate=pl.CostEstimate(
            flops=2 * tile_total * key_tile * row_count * cat_width,
            bytes_accessed=8 * mib,
            transcendentals=0,
        ),
        name="query_grads",
    )(spans, keys, d_score, w_uk)
    terms = [sums[0]] + [to_head(rows, m) for m, rows in zip(range(head_count - 1, 0, -1), sums[1:])]
    *terms, d_q_nope, d_q_rope = lax.optimization_barrier((*terms, d_q_nope, d_q_rope))
    sums = pl.pallas_call(
        head_sum_kernel,
        out_shape=(shape(piece_shape, f32),) + (shape(piece_shape, bf16),) * (z_count - 1),
        in_specs=[in_vmem] * head_count,
        out_specs=(in_vmem,) * z_count,
        scratch_shapes=[pltpu.VMEM(share_shape, f32)],
        compiler_params=params(4),
        name="head_sum",
    )(*terms)
    terms = [sums[0]] + [to_chip(rows, k) for k, rows in zip(range(z_count - 1, 0, -1), sums[1:])]
    share = pl.pallas_call(
        chip_sum_kernel,
        out_shape=shape(piece_shape, bf16),
        in_specs=[in_vmem] * z_count,
        out_specs=in_vmem,
        compiler_params=params(4),
        name="chip_sum",
    )(*terms)
    shares = [share] + [to_head(share, m) for m in range(1, head_count)]
    d_cache_t = pl.pallas_call(
        norm_back_kernel,
        out_shape=shape((cat_width, tok_rows), f32),
        in_specs=[in_vmem] * (2 + head_count),
        out_specs=in_vmem,
        scratch_shapes=[pltpu.VMEM((tok_rows, cat_width), f32)],
        compiler_params=params(8),
        name="norm_back",
    )(cache_t, kv_gain, *shares)
    return (d_q_nope, d_q_rope, d_cache_t.T)


def solution(mesh):
    in_specs = (
        P("ctx", "head"),
        P("ctx", "head"),
        P("ctx", None),
        P(),
        P("head", None, None),
        P("head", None, None),
        P("ctx", "head"),
        P("ctx", "head"),
        P(),
    )
    out_specs = (P("ctx", "head"), P("ctx", "head"), P("ctx", None))
    return jax.shard_map(local, mesh=mesh, in_specs=in_specs, out_specs=out_specs, check_vma=False)
```

time: 65.9 us -> 59.1 us (0.90)
  Pallas kernels: 30 us -> 20.7 us
  local copies, waits for them, and re-layouts: 0.02 us -> 1.63 us
  waiting for transfers between devices: 13.1 us -> 14.7 us
    pallas_call x7, Pallas kernels: 28.8 us -> 19.4 us  [the longest x1 10.3 us: local(): pl.pallas_call(functools.partial(attend_kernel, head_count), out_shape=(s...]
    ppermute x9, waiting for transfers between devices: 4.12 us -> 6.06 us  [to_head(): return lax.ppermute(rows, 'head', [(j, j ^ m) for j in range(head_count)])]
    unnamed x10 -> x22, local copies, waits for them, and re-layouts: 0.02 us -> 1.63 us
    ppermute x6, waiting for transfers between devices: 5.57 us -> 4.74 us  [to_chip(): return lax.ppermute(rows, 'ctx', [(i, i ^ 2 * k) for i in range(ctx_count)])]
    ppermute x3 -> x2, waiting for transfers between devices: 3.39 us -> 3.86 us  [to_core(): return lax.ppermute(rows, 'ctx', [(i, i ^ 1) for i in range(ctx_count)])]
  transfers between devices with their start and end apart: 18 -> 17, of which waited for: 8 -> 14; matrix products, arithmetic and copies ran while one was open for 0% -> 0% of each run, Pallas kernels for 23% -> 13%
where the time goes in v2:
time: 59.1 us; the launch traced here: 58.9 us
  starting transfers between devices  21.1 us (36%)
  Pallas kernels  20.7 us (35%)
  waiting for transfers between devices  14.7 us (25%)
  local copies, waits for them, and re-layouts  1.63 us (3%)
  between operations  0.76 us (1%)
    ppermute x9, starting transfers between devices, to_head(): return lax.ppermute(rows, 'head', [(j, j ^ m) for j in range(head_count)])  10.7 us
    pallas_call x1, Pallas kernels, local(): pl.pallas_call(functools.partial(attend_kernel, head_count), out_shape=(s...  10.3 us
    ppermute x6, starting transfers between devices, to_chip(): return lax.ppermute(rows, 'ctx', [(i, i ^ 2 * k) for i in range(ctx_count)])  10.2 us
    ppermute x9, waiting for transfers between devices, to_head(): return lax.ppermute(rows, 'head', [(j, j ^ m) for j in range(head_count)])  6.06 us
    pallas_call x1, Pallas kernels, local(): pl.pallas_call(functools.partial(query_kernel, scale), out_shape=(shape(q...  5.63 us
    ppermute x6, waiting for transfers between devices, to_chip(): return lax.ppermute(rows, 'ctx', [(i, i ^ 2 * k) for i in range(ctx_count)])  4.74 us
    ppermute x2, waiting for transfers between devices, to_core(): return lax.ppermute(rows, 'ctx', [(i, i ^ 1) for i in range(ctx_count)])  3.86 us
    pallas_call x1, Pallas kernels, local(): pl.pallas_call(functools.partial(project_kernel, scale * log2_e), out_sha...  1.9 us
  transfers between devices with their start and end apart: 17, of which 14 were waited for; matrix products, arithmetic and copies ran while one was open for 0% of the time, Pallas kernels for 13%

profile of v2, /device:TPU:0, one launch (start us, length us, event | category | flops | bytes accessed | tf_op | source)
XLA Modules:
  0.0 58.9 jit_solution(15950689178322355583)
XLA Ops:
  0.6 1.1 %piece.1 = bf16[144,128]{1,0:T(8,128)(2,1)S(1)} custom-call(bf16[576,128]{1,0:T(8,128)(2,1)} %bitcast.3), custom_call_target="tpu_custom_call" | custom-call | tf_op jit(solution)/shard_map/piece/pallas_call | solution.py:445
  1.8 5.1 %collective-permute-start.2 = (bf16[144,128]{1,0:T(8,128)(2,1)S(1)}, bf16[144,128]{1,0:T(8,128)(2,1)S(1)}, u32[]{:S(2)}, u32[]{:S(2)}) collective-permute-start(bf16[144,128]{1,0:T(8,128)(2,1)S(1)} %piece.1), channel_id=1, source_target_pairs={{0,24},{4,28},{8,16},{12,20},{16,8},{20,12},{24,0},{28,4},{1,25},{... | collective-permute-start | bytes 110600 | tf_op jit(solution)/shard_map/ppermute | solution.py:439
  7.5 0.9 %copy-done.2 = bf16[128,576]{0,1:T(8,128)(2,1)S(1)} copy-done((bf16[128,576]{0,1:T(8,128)(2,1)S(1)}, bf16[128,576]{0,1:T(8,128)(2,1)}, u32[]{:S(2)}) %copy-start.2) | copy-done | bytes 147480
  9.4 2.3 %collective-permute-done.1.refs_1_ = bf16[144,128]{1,0:T(8,128)(2,1)S(1)} collective-permute-done((bf16[144,128]{1,0:T(8,128)(2,1)S(1)}, bf16[144,128]{1,0:T(8,128)(2,1)S(1)}, u32[]{:S(2)}, u32[]{:S(2)}) %collective-permute-start.1) | collective-permute-done | bytes 36896 | tf_op jit(solution)/shard_map/ppermute | solution.py:439
  11.9 2.5 %collective-permute-start.5 = (bf16[432,128]{1,0:T(8,128)(2,1)S(1)}, bf16[432,128]{1,0:T(8,128)(2,1)S(1)}, u32[]{:S(2)}, u32[]{:S(2)}) collective-permute-start(bf16[432,128]{1,0:T(8,128)(2,1)S(1)} %join_chips.1.unused_ref.refs_1_), channel_id=1, source_target_pairs={{0,3},{1,2},{2,1},{3,0},{4,7},{5,6},{6,5},{7,4},{8,11},{9,10},{10,... | collective-permute-start | bytes 331784 | tf_op jit(solution)/shard_map/ppermute | solution.py:442
  15.5 1.9 %project.1 = (bf16[2,1024,576]{2,1,0:T(8,128)(2,1)S(1)}, bf16[2,1040,512]{2,1,0:T(8,128)(2,1)S(1)}) custom-call(bf16[128,2048]{1,0:T(8,128)(2,1)S(1)} %copy-done.4, bf16[128,1024]{1,0:T(8,128)(2,1)S(1)} %copy-done.7, bf16[16,128,512]{2,1,0:T(8,128)(2,1)S(1)} %copy-done, bf16[128,2048]{1,0:T(8,128)(2,1)S(1)} %copy-done.5, bf16[128,2048]{1,0:T(8,128)(2,1)S(1)} %copy-done.6, ...), custom_call_target="tpu_custom_call" | custom-call | flops 536870912 | bytes 12582912 | tf_op jit(solution)/shard_map/project/pallas_call | solution.py:488
  17.4 1.4 %collective-permute-done.5.refs_4_ = bf16[432,128]{1,0:T(8,128)(2,1)S(1)} collective-permute-done((bf16[432,128]{1,0:T(8,128)(2,1)S(1)}, bf16[432,128]{1,0:T(8,128)(2,1)S(1)}, u32[]{:S(2)}, u32[]{:S(2)}) %collective-permute-start.5) | collective-permute-done | bytes 110624 | tf_op jit(solution)/shard_map/ppermute | solution.py:442
  18.8 0.8 %collective-permute-done.4.refs_3_ = bf16[432,128]{1,0:T(8,128)(2,1)S(1)} collective-permute-done((bf16[432,128]{1,0:T(8,128)(2,1)S(1)}, bf16[432,128]{1,0:T(8,128)(2,1)S(1)}, u32[]{:S(2)}, u32[]{:S(2)}) %collective-permute-start.4) | collective-permute-done | bytes 110624 | tf_op jit(solution)/shard_map/ppermute | solution.py:442
  19.8 2.0 %collective-permute-done.6.refs_2_ = bf16[2304,128]{1,0:T(8,128)(2,1)S(1)} collective-permute-done((bf16[2304,128]{1,0:T(8,128)(2,1)S(1)}, bf16[2304,128]{1,0:T(8,128)(2,1)S(1)}, u32[]{:S(2)}, u32[]{:S(2)}) %collective-permute-start.6) | collective-permute-done | bytes 589856 | tf_op jit(solution)/shard_map/ppermute | solution.py:436
  21.8 10.3 %attend.1 = (bf16[1024,576]{1,0:T(8,128)(2,1)S(1)}, bf16[1152,1024]{1,0:T(8,128)(2,1)S(1)}, bf16[2304,128]{1,0:T(8,128)(2,1)S(1)}, bf16[2304,128]{1,0:T(8,128)(2,1)S(1)}) custom-call(s32[2,8]{1,0:T(2,128)S(1)} %bitcast.6, bf16[2304,128]{1,0:T(8,128)(2,1)S(1)} %join_heads.1.refs_1_, bf16[2304,128]{1,0:T(8,128)(2,1)S(1)} %collective-permute-done.6.refs_2_, ...), custom_call_target="tpu_custom_call" | custom-call | flops 5133828096 | bytes 12582912 | tf_op jit(solution)/shard_map/attend/pallas_call | solution.py:508
  32.4 1.9 %collective-permute-done.7.recv_ref = bf16[2304,128]{1,0:T(8,128)(2,1)S(1)} collective-permute-done((bf16[2304,128]{1,0:T(8,128)(2,1)S(1)}, bf16[2304,128]{1,0:T(8,128)(2,1)S(1)}, u32[]{:S(2)}, u32[]{:S(2)}) %collective-permute-start.7) | collective-permute-done | bytes 589856 | tf_op jit(solution)/shard_map/ppermute | solution.py:436
  34.3 1.6 %collective-permute-start.8 = (bf16[576,128]{1,0:T(8,128)(2,1)S(1)}, bf16[576,128]{1,0:T(8,128)(2,1)S(1)}, u32[]{:S(2)}, u32[]{:S(2)}) collective-permute-start(bf16[576,128]{1,0:T(8,128)(2,1)S(1)} %get-tuple-element.60), channel_id=1, source_target_pairs={{0,3},{1,2},{2,1},{3,0},{4,7},{5,6},{6,5},{7,4},{8,11},{9,10},{10,... | collective-permute-start | bytes 442376 | tf_op jit(solution)/shard_map/ppermute | solution.py:442
  36.6 1.3 %collective-permute-start.10 = (bf16[576,128]{1,0:T(8,128)(2,1)S(1)}, bf16[576,128]{1,0:T(8,128)(2,1)S(1)}, u32[]{:S(2)}, u32[]{:S(2)}) collective-permute-start(bf16[576,128]{1,0:T(8,128)(2,1)S(1)} %get-tuple-element.62), channel_id=1, source_target_pairs={{0,1},{1,0},{2,3},{3,2},{4,5},{5,4},{6,7},{7,6},{8,9},{9,8},{10,11... | collective-permute-start | bytes 442376 | tf_op jit(solution)/shard_map/ppermute | solution.py:442
  37.9 5.6 %query_grads.1 = (bf16[128,2048]{1,0:T(8,128)(2,1)}, bf16[128,1024]{1,0:T(8,128)(2,1)}) custom-call(s32[2,8]{1,0:T(2,128)S(1)} %bitcast.7, bf16[1024,576]{1,0:T(8,128)(2,1)S(1)} %get-tuple-element.63.keys_ref, bf16[1152,1024]{1,0:T(8,128)(2,1)S(1)} %get-tuple-element.64.ds_ref, bf16[16,128,512]{2,1,0:T(8,128)(2,1)S(1)} %copy-done), custom_call_target="tpu_custom_call" | custom-call | flops 1358954496 | bytes 8388608 | tf_op jit(solution)/shard_map/query_grads/pallas_call | solution.py:544
  43.5 0.8 %collective-permute-done.9.refs_2_ = bf16[576,128]{1,0:T(8,128)(2,1)S(1)} collective-permute-done((bf16[576,128]{1,0:T(8,128)(2,1)S(1)}, bf16[576,128]{1,0:T(8,128)(2,1)S(1)}, u32[]{:S(2)}, u32[]{:S(2)}) %collective-permute-start.9) | collective-permute-done | bytes 147488 | tf_op jit(solution)/shard_map/ppermute | solution.py:442
  44.6 1.5 %collective-permute-start.11 = (bf16[144,128]{1,0:T(8,128)(2,1)S(1)}, bf16[144,128]{1,0:T(8,128)(2,1)S(1)}, u32[]{:S(2)}, u32[]{:S(2)}) collective-permute-start(bf16[144,128]{1,0:T(8,128)(2,1)S(1)} %get-tuple-element.74), channel_id=1, source_target_pairs={{0,24},{4,28},{8,16},{12,20},{16,8},{20,12},{24,0},{28,4},{1,25},{... | collective-permute-start | bytes 110600 | tf_op jit(solution)/shard_map/ppermute | solution.py:439
  46.8 2.3 %collective-permute-start.13 = (bf16[144,128]{1,0:T(8,128)(2,1)S(1)}, bf16[144,128]{1,0:T(8,128)(2,1)S(1)}, u32[]{:S(2)}, u32[]{:S(2)}) collective-permute-start(bf16[144,128]{1,0:T(8,128)(2,1)S(1)} %get-tuple-element.76), channel_id=1, source_target_pairs={{0,8},{4,12},{8,0},{12,4},{16,24},{20,28},{24,16},{28,20},{1,9},{5... | collective-permute-start | bytes 110600 | tf_op jit(solution)/shard_map/ppermute | solution.py:439
  49.0 1.7 %collective-permute-done.11.refs_1_ = bf16[144,128]{1,0:T(8,128)(2,1)S(1)} collective-permute-done((bf16[144,128]{1,0:T(8,128)(2,1)S(1)}, bf16[144,128]{1,0:T(8,128)(2,1)S(1)}, u32[]{:S(2)}, u32[]{:S(2)}) %collective-permute-start.11) | collective-permute-done | bytes 36896 | tf_op jit(solution)/shard_map/ppermute | solution.py:439
  51.5 1.5 %collective-permute-start.16 = (bf16[144,128]{1,0:T(8,128)(2,1)S(1)}, bf16[144,128]{1,0:T(8,128)(2,1)S(1)}, u32[]{:S(2)}, u32[]{:S(2)}) collective-permute-start(bf16[144,128]{1,0:T(8,128)(2,1)S(1)} %chip_sum.1.refs_0_), channel_id=1, source_target_pairs={{0,3},{1,2},{2,1},{3,0},{4,7},{5,6},{6,5},{7,4},{8,11},{9,10},{10,... | collective-permute-start | bytes 110600 | tf_op jit(solution)/shard_map/ppermute | solution.py:442
  53.0 1.0 %collective-permute-start.15 = (bf16[144,128]{1,0:T(8,128)(2,1)S(1)}, bf16[144,128]{1,0:T(8,128)(2,1)S(1)}, u32[]{:S(2)}, u32[]{:S(2)}) collective-permute-start(bf16[144,128]{1,0:T(8,128)(2,1)S(1)} %chip_sum.1.refs_0_), channel_id=1, source_target_pairs={{0,2},{1,3},{2,0},{3,1},{4,6},{5,7},{6,4},{7,5},{8,10},{9,11},{10,... | collective-permute-start | bytes 110600 | tf_op jit(solution)/shard_map/ppermute | solution.py:442
  53.9 1.1 %collective-permute-start.14 = (bf16[144,128]{1,0:T(8,128)(2,1)S(1)}, bf16[144,128]{1,0:T(8,128)(2,1)S(1)}, u32[]{:S(2)}, u32[]{:S(2)}) collective-permute-start(bf16[144,128]{1,0:T(8,128)(2,1)S(1)} %chip_sum.1.refs_0_), channel_id=1, source_target_pairs={{0,1},{1,0},{2,3},{3,2},{4,5},{5,4},{6,7},{7,6},{8,9},{9,8},{10,11... | collective-permute-start | bytes 110600 | tf_op jit(solution)/shard_map/ppermute | solution.py:442
  55.0 1.4 %collective-permute-done.16.refs_3_ = bf16[144,128]{1,0:T(8,128)(2,1)S(1)} collective-permute-done((bf16[144,128]{1,0:T(8,128)(2,1)S(1)}, bf16[144,128]{1,0:T(8,128)(2,1)S(1)}, u32[]{:S(2)}, u32[]{:S(2)}) %collective-permute-start.16) | collective-permute-done | bytes 36896 | tf_op jit(solution)/shard_map/ppermute | solution.py:442
  56.9 1.0 %collective-permute-done.14.refs_1_ = bf16[144,128]{1,0:T(8,128)(2,1)S(1)} collective-permute-done((bf16[144,128]{1,0:T(8,128)(2,1)S(1)}, bf16[144,128]{1,0:T(8,128)(2,1)S(1)}, u32[]{:S(2)}, u32[]{:S(2)}) %collective-permute-start.14) | collective-permute-done | bytes 36896 | tf_op jit(solution)/shard_map/ppermute | solution.py:442
  57.9 1.0 %norm_back.1 = f32[576,128]{1,0:T(8,128)} custom-call(bf16[576,128]{1,0:T(8,128)(2,1)S(1)} %bitcast.5, bf16[512]{0:T(512)(128)(2,1)S(1)} %copy-done.9, bf16[144,128]{1,0:T(8,128)(2,1)S(1)} %chip_sum.1.refs_0_, bf16[144,128]{1,0:T(8,128)(2,1)S(1)} %collective-permute-done.14.refs_1_, bf16[144,128]{1,0:T(8,128)(2,1)S(1)} %collective-permute-done.15.refs_2_, ...), custom_call_target="tpu_custom_call" | custom-call | tf_op jit(solution)/shard_map/norm_back/pallas_call | solution.py:579
  (43 shorter events, 6.2 us)
Async XLA Ops:
  0.6 11.1 %copy-start.9 = (bf16[512]{0:T(512)(128)(2,1)S(1)}, bf16[512]{0:T(512)(128)(2,1)}, u32[]{:S(2)}) copy-start(bf16[512]{0:T(512)(128)(2,1)} %gain_ref.5) | copy-start | bytes 3076
  1.8 13.7 %copy-start = (bf16[16,128,512]{2,1,0:T(8,128)(2,1)S(1)}, bf16[16,128,512]{2,1,0:T(8,128)(2,1)}, u32[]{:S(2)}) copy-start(bf16[16,128,512]{2,1,0:T(8,128)(2,1)} %w_uk_ref.3) | copy-start | bytes 6291460
  1.8 13.7 %copy-start.1 = (bf16[16,512,128]{2,1,0:T(8,128)(2,1)S(1)}, bf16[16,512,128]{2,1,0:T(8,128)(2,1)}, u32[]{:S(2)}) copy-start(bf16[16,512,128]{2,1,0:T(8,128)(2,1)} %w_uv_ref.1) | copy-start | bytes 6291460
  1.8 7.7 %collective-permute-start.2 = (bf16[144,128]{1,0:T(8,128)(2,1)S(1)}, bf16[144,128]{1,0:T(8,128)(2,1)S(1)}, u32[]{:S(2)}, u32[]{:S(2)}) collective-permute-start(bf16[144,128]{1,0:T(8,128)(2,1)S(1)} %piece.1), channel_id=1, source_target_pairs={{0,24},{4,28},{8,16},{12,20},{16,8},{20,12},{24,0},{28,4},{1,25},{... | collective-permute-start | bytes 110600 | tf_op jit(solution)/shard_map/ppermute | solution.py:439
  6.9 4.9 %collective-permute-start.1 = (bf16[144,128]{1,0:T(8,128)(2,1)S(1)}, bf16[144,128]{1,0:T(8,128)(2,1)S(1)}, u32[]{:S(2)}, u32[]{:S(2)}) collective-permute-start(bf16[144,128]{1,0:T(8,128)(2,1)S(1)} %piece.1), channel_id=1, source_target_pairs={{0,16},{4,20},{8,24},{12,28},{16,0},{20,4},{24,8},{28,12},{1,17},{... | collective-permute-start | bytes 110600 | tf_op jit(solution)/shard_map/ppermute | solution.py:439
  6.9 4.9 %collective-permute-start = (bf16[144,128]{1,0:T(8,128)(2,1)S(1)}, bf16[144,128]{1,0:T(8,128)(2,1)S(1)}, u32[]{:S(2)}, u32[]{:S(2)}) collective-permute-start(bf16[144,128]{1,0:T(8,128)(2,1)S(1)} %piece.1), channel_id=1, source_target_pairs={{0,8},{4,12},{8,0},{12,4},{16,24},{20,28},{24,16},{28,20},{1,9},{5... | collective-permute-start | bytes 110600 | tf_op jit(solution)/shard_map/ppermute | solution.py:439
  9.1 6.4 %copy-start.6 = (bf16[128,2048]{1,0:T(8,128)(2,1)S(1)}, bf16[128,2048]{1,0:T(8,128)(2,1)}, u32[]{:S(2)}) copy-start(bf16[128,2048]{1,0:T(8,128)(2,1)} %out_ref.1) | copy-start | bytes 1572868
  9.1 6.4 %copy-start.7 = (bf16[128,1024]{1,0:T(8,128)(2,1)S(1)}, bf16[128,1024]{1,0:T(8,128)(2,1)}, u32[]{:S(2)}) copy-start(bf16[128,1024]{1,0:T(8,128)(2,1)} %rope_ref.1) | copy-start | bytes 786436
  11.9 9.9 %copy-start.10 = (s32[8,2]{0,1:T(2,128)S(1)}, s32[8,2]{0,1:T(2,128)}, u32[]{:S(2)}) copy-start(s32[8,2]{0,1:T(2,128)} %param.17) | copy-start | bytes 196
  11.9 6.9 %collective-permute-start.5 = (bf16[432,128]{1,0:T(8,128)(2,1)S(1)}, bf16[432,128]{1,0:T(8,128)(2,1)S(1)}, u32[]{:S(2)}, u32[]{:S(2)}) collective-permute-start(bf16[432,128]{1,0:T(8,128)(2,1)S(1)} %join_chips.1.unused_ref.refs_1_), channel_id=1, source_target_pairs={{0,3},{1,2},{2,1},{3,0},{4,7},{5,6},{6,5},{7,4},{8,11},{9,10},{10,... | collective-permute-start | bytes 331784 | tf_op jit(solution)/shard_map/ppermute | solution.py:442
  14.4 5.2 %collective-permute-start.4 = (bf16[432,128]{1,0:T(8,128)(2,1)S(1)}, bf16[432,128]{1,0:T(8,128)(2,1)S(1)}, u32[]{:S(2)}, u32[]{:S(2)}) collective-permute-start(bf16[432,128]{1,0:T(8,128)(2,1)S(1)} %join_chips.1.unused_ref.refs_1_), channel_id=1, source_target_pairs={{0,2},{1,3},{2,0},{3,1},{4,6},{5,7},{6,4},{7,5},{8,10},{9,11},{10,... | collective-permute-start | bytes 331784 | tf_op jit(solution)/shard_map/ppermute | solution.py:442
  14.9 4.7 %collective-permute-start.3 = (bf16[432,128]{1,0:T(8,128)(2,1)S(1)}, bf16[432,128]{1,0:T(8,128)(2,1)S(1)}, u32[]{:S(2)}, u32[]{:S(2)}) collective-permute-start(bf16[432,128]{1,0:T(8,128)(2,1)S(1)} %join_chips.1.unused_ref.refs_1_), channel_id=1, source_target_pairs={{0,1},{1,0},{2,3},{3,2},{4,5},{5,4},{6,7},{7,6},{8,9},{9,8},{10,11... | collective-permute-start | bytes 331784 | tf_op jit(solution)/shard_map/ppermute | solution.py:442
  19.7 2.1 %collective-permute-start.6 = (bf16[2304,128]{1,0:T(8,128)(2,1)S(1)}, bf16[2304,128]{1,0:T(8,128)(2,1)S(1)}, u32[]{:S(2)}, u32[]{:S(2)}) collective-permute-start(bf16[2304,128]{1,0:T(8,128)(2,1)S(1)} %join_heads.1.refs_1_), channel_id=1, source_target_pairs={{0,4},{4,0},{8,12},{12,8},{16,20},{20,16},{24,28},{28,24},{1,5},{5... | collective-permute-start | bytes 1769480 | tf_op jit(solution)/shard_map/ppermute | solution.py:436
  32.1 2.1 %collective-permute-start.7 = (bf16[2304,128]{1,0:T(8,128)(2,1)S(1)}, bf16[2304,128]{1,0:T(8,128)(2,1)S(1)}, u32[]{:S(2)}, u32[]{:S(2)}) collective-permute-start(bf16[2304,128]{1,0:T(8,128)(2,1)S(1)} %get-tuple-element.53), channel_id=1, source_target_pairs={{0,4},{4,0},{8,12},{12,8},{16,20},{20,16},{24,28},{28,24},{1,5},{5... | collective-permute-start | bytes 1769480 | tf_op jit(solution)/shard_map/ppermute | solution.py:436
  34.3 9.2 %collective-permute-start.8 = (bf16[576,128]{1,0:T(8,128)(2,1)S(1)}, bf16[576,128]{1,0:T(8,128)(2,1)S(1)}, u32[]{:S(2)}, u32[]{:S(2)}) collective-permute-start(bf16[576,128]{1,0:T(8,128)(2,1)S(1)} %get-tuple-element.60), channel_id=1, source_target_pairs={{0,3},{1,2},{2,1},{3,0},{4,7},{5,6},{6,5},{7,4},{8,11},{9,10},{10,... | collective-permute-start | bytes 442376 | tf_op jit(solution)/shard_map/ppermute | solution.py:442
  35.9 8.5 %collective-permute-start.9 = (bf16[576,128]{1,0:T(8,128)(2,1)S(1)}, bf16[576,128]{1,0:T(8,128)(2,1)S(1)}, u32[]{:S(2)}, u32[]{:S(2)}) collective-permute-start(bf16[576,128]{1,0:T(8,128)(2,1)S(1)} %get-tuple-element.61), channel_id=1, source_target_pairs={{0,2},{1,3},{2,0},{3,1},{4,6},{5,7},{6,4},{7,5},{8,10},{9,11},{10,... | collective-permute-start | bytes 442376 | tf_op jit(solution)/shard_map/ppermute | solution.py:442
  36.6 7.9 %collective-permute-start.10 = (bf16[576,128]{1,0:T(8,128)(2,1)S(1)}, bf16[576,128]{1,0:T(8,128)(2,1)S(1)}, u32[]{:S(2)}, u32[]{:S(2)}) collective-permute-start(bf16[576,128]{1,0:T(8,128)(2,1)S(1)} %get-tuple-element.62), channel_id=1, source_target_pairs={{0,1},{1,0},{2,3},{3,2},{4,5},{5,4},{6,7},{7,6},{8,9},{9,8},{10,11... | collective-permute-start | bytes 442376 | tf_op jit(solution)/shard_map/ppermute | solution.py:442
  37.9 20.0 %copy-start.3 = (bf16[128,576]{0,1:T(8,128)(2,1)S(1)}, bf16[128,576]{0,1:T(8,128)(2,1)}, u32[]{:S(2)}) copy-start(bf16[128,576]{0,1:T(8,128)(2,1)} %param.11) | copy-start | bytes 442372
  44.6 6.2 %collective-permute-start.11 = (bf16[144,128]{1,0:T(8,128)(2,1)S(1)}, bf16[144,128]{1,0:T(8,128)(2,1)S(1)}, u32[]{:S(2)}, u32[]{:S(2)}) collective-permute-start(bf16[144,128]{1,0:T(8,128)(2,1)S(1)} %get-tuple-element.74), channel_id=1, source_target_pairs={{0,24},{4,28},{8,16},{12,20},{16,8},{20,12},{24,0},{28,4},{1,25},{... | collective-permute-start | bytes 110600 | tf_op jit(solution)/shard_map/ppermute | solution.py:439
  46.1 5.0 %collective-permute-start.12 = (bf16[144,128]{1,0:T(8,128)(2,1)S(1)}, bf16[144,128]{1,0:T(8,128)(2,1)S(1)}, u32[]{:S(2)}, u32[]{:S(2)}) collective-permute-start(bf16[144,128]{1,0:T(8,128)(2,1)S(1)} %get-tuple-element.75), channel_id=1, source_target_pairs={{0,16},{4,20},{8,24},{12,28},{16,0},{20,4},{24,8},{28,12},{1,17},{... | collective-permute-start | bytes 110600 | tf_op jit(solution)/shard_map/ppermute | solution.py:439
  46.8 4.7 %collective-permute-start.13 = (bf16[144,128]{1,0:T(8,128)(2,1)S(1)}, bf16[144,128]{1,0:T(8,128)(2,1)S(1)}, u32[]{:S(2)}, u32[]{:S(2)}) collective-permute-start(bf16[144,128]{1,0:T(8,128)(2,1)S(1)} %get-tuple-element.76), channel_id=1, source_target_pairs={{0,8},{4,12},{8,0},{12,4},{16,24},{20,28},{24,16},{28,20},{1,9},{5... | collective-permute-start | bytes 110600 | tf_op jit(solution)/shard_map/ppermute | solution.py:439
  51.5 4.9 %collective-permute-start.16 = (bf16[144,128]{1,0:T(8,128)(2,1)S(1)}, bf16[144,128]{1,0:T(8,128)(2,1)S(1)}, u32[]{:S(2)}, u32[]{:S(2)}) collective-permute-start(bf16[144,128]{1,0:T(8,128)(2,1)S(1)} %chip_sum.1.refs_0_), channel_id=1, source_target_pairs={{0,3},{1,2},{2,1},{3,0},{4,7},{5,6},{6,5},{7,4},{8,11},{9,10},{10,... | collective-permute-start | bytes 110600 | tf_op jit(solution)/shard_map/ppermute | solution.py:442
  53.0 4.0 %collective-permute-start.15 = (bf16[144,128]{1,0:T(8,128)(2,1)S(1)}, bf16[144,128]{1,0:T(8,128)(2,1)S(1)}, u32[]{:S(2)}, u32[]{:S(2)}) collective-permute-start(bf16[144,128]{1,0:T(8,128)(2,1)S(1)} %chip_sum.1.refs_0_), channel_id=1, source_target_pairs={{0,2},{1,3},{2,0},{3,1},{4,6},{5,7},{6,4},{7,5},{8,10},{9,11},{10,... | collective-permute-start | bytes 110600 | tf_op jit(solution)/shard_map/ppermute | solution.py:442
  53.9 4.0 %collective-permute-start.14 = (bf16[144,128]{1,0:T(8,128)(2,1)S(1)}, bf16[144,128]{1,0:T(8,128)(2,1)S(1)}, u32[]{:S(2)}, u32[]{:S(2)}) collective-permute-start(bf16[144,128]{1,0:T(8,128)(2,1)S(1)} %chip_sum.1.refs_0_), channel_id=1, source_target_pairs={{0,1},{1,0},{2,3},{3,2},{4,5},{5,4},{6,7},{7,6},{8,9},{9,8},{10,11... | collective-permute-start | bytes 110600 | tf_op jit(solution)/shard_map/ppermute | solution.py:442
  (4 other events, 14.3 us)

commit v3 on v2

--- a/solution.py
+++ b/solution.py
@@ -10,11 +10,11 @@
 neg_big = -1e30
 eps_norm = 1e-06
 log2_e = 1.4426950408889634
-key_tile = 128
+key_tile = 256
 mib = 1024 * 1024
 piece_mib = 53.8
 query_mib = 16
-attend_mib = 36
+attend_mib = 28
 project_mib = 12
 window_flops = 8 * 10**9
 delta_rows = 16
@@ -89,13 +89,17 @@
     out_ref[...] = fold(normalised(rows, gain_ref[...].astype(f32)[None, :]), on).astype(bf16)
 
 
-def join_chips_kernel(on, width, gain_ref, *refs):
+def join_chips_kernel(on, width, gain_ref, own_ref, *refs):
+    refs, pieces_ref, first_ref = refs[:-2], refs[-2], refs[-1]
     gain = gain_ref[...].astype(f32)[None, :]
-    rows = jnp.concatenate([unfold(ref[...].astype(f32), width, on) for ref in refs[:-1]], axis=0)
+    rows = jnp.concatenate([unfold(ref[...].astype(f32), width, on) for ref in refs], axis=0)
     rows = normalised(rows, gain)
-    size = rows.shape[0] // (len(refs) - 1)
-    parts = [fold(rows[i * size : (i + 1) * size], on) for i in range(len(refs) - 1)]
-    refs[-1][...] = jnp.concatenate(parts, axis=0).astype(bf16)
+    size = rows.shape[0] // len(refs)
+    parts = [fold(rows[i * size : (i + 1) * size], on) for i in range(len(refs))]
+    pieces = jnp.concatenate(parts, axis=0).astype(bf16)
+    pieces_ref[...] = pieces
+    first_ref[: own_ref.shape[0], :] = own_ref[...]
+    first_ref[own_ref.shape[0] :, :] = pieces
 
 
 def project_kernel(
@@ -156,8 +160,7 @@
 
 
 def tile_groups(tile_count):
-    pairs = [(u, u + 2) for u in range(0, tile_count // 2, 2)]
-    return pairs + [(u, u + 1) for u in range(tile_count // 2, tile_count + 1)]
+    return [(u, u + 1) for u in range(tile_count + 1)]
 
 
 def tile_place(u, tile_count, span, lower_block):
@@ -188,8 +191,8 @@
 
 
 def attend_kernel(head_count, *refs):
-    span_ref, own_pieces, sib_pieces, q_ref, dl_ref, keys_ref, ds_ref, keep_ref, send_ref = refs[:-5]
-    e_scr, score_part, prob_part, prob_scr, raw = refs[-5:]
+    span_ref, own_first, own_later, sib_first, sib_later, q_ref, dl_ref = refs[:7]
+    keys_ref, ds_ref, send_ref, score_part, prob_part, e_scr, prob_scr, raw = refs[7:]
     half_count, row_count, cat_width = q_ref.shape
     lat_width = dl_ref.shape[2]
     total = keys_ref.shape[0]
@@ -211,14 +214,15 @@
         return pl.ds(pl.multiple_of(start, piece_rows), piece_rows)
 
     stage = keys_ref if piece_rows % 16 == 0 else raw
-    for side, ref in enumerate((own_pieces, sib_pieces)):
-        source = ref if piece_rows % 16 == 0 else ref[...].astype(f32)
-        rows = unfold(source[:own_size, :], cat_width, on)
+    for side, parts in enumerate(((own_first, own_later), (sib_first, sib_later))):
+        first, later = parts if piece_rows % 16 == 0 else [ref[...].astype(f32) for ref in parts]
+        rows = unfold(first[:own_size, :], cat_width, on)
         for s in range(2):
             start = pl.multiple_of(span_ref[s, 2 * z + lax.rem(core + side, 2)] * span, span)
             stage[pl.ds(start, span), :] = rows[s * span : (s + 1) * span, :]
-        start = own_size
         for m in range(head_count):
+            source = later if m else first
+            start = (m - 1) * (z_count - 1) * piece_size if m else own_size
             for k in range(1, z_count):
                 owner = 2 * (z ^ k) + lax.rem(core + side, 2)
                 stage[place(owner, head ^ m), :] = unfold(source[start : start + piece_size, :], cat_width, on)
@@ -321,16 +325,29 @@
     for key_step in pending:
         key_step()
 
-    for side, ref in ((0, keep_ref), (1, send_ref)):
-        for quarter in range(head_count):
-            rows = []
-            for other in range(z_count):
-                here = place(2 * other + lax.rem(core + side, 2), jnp.int32(quarter))
-                block = score_part[here, :] * (1.0 / log2_e)
-                latent = block[:, :lat_width] + prob_part[here, :]
-                rows.append(fold(jnp.concatenate([latent, block[:, lat_width:]], axis=1), on))
-            size = z_count * piece_size
-            ref[quarter * size : (quarter + 1) * size, :] = jnp.concatenate(rows, axis=0).astype(bf16)
+    pack(1, head_count, span_ref, score_part, prob_part, send_ref)
+
+
+def pack(side, head_count, span_ref, score_part, prob_part, out_ref):
+    total, cat_width = score_part.shape
+    lat_width = prob_part.shape[1]
+    z_count = lax.axis_size("ctx") // 2
+    piece_rows = total // z_count // 2 // head_count
+    span = total // z_count // 4
+    per_span = span // piece_rows
+    on = piece_rows % 32 == 0
+    size = z_count * folded(piece_rows, cat_width, on)[0]
+    owner_core = lax.rem(lax.axis_index("ctx") + side, 2)
+    for quarter in range(head_count):
+        rows = []
+        for other in range(z_count):
+            block = span_ref[quarter // per_span, 2 * other + owner_core]
+            start = block * span + quarter % per_span * piece_rows
+            here = pl.ds(pl.multiple_of(start, piece_rows), piece_rows)
+            terms = score_part[here, :] * (1.0 / log2_e)
+            latent = terms[:, :lat_width] + prob_part[here, :]
+            rows.append(fold(jnp.concatenate([latent, terms[:, lat_width:]], axis=1), on))
+        out_ref[quarter * size : (quarter + 1) * size, :] = jnp.concatenate(rows, axis=0).astype(bf16)
 
 
 def query_kernel(
@@ -399,7 +416,7 @@
 
 
 def norm_back_kernel(cache_t_ref, gain_ref, *refs):
-    shares, out_ref, total = refs[:-2], refs[-2], refs[-1]
+    shares, (out_hbm, total, out_ref, sems) = refs[:-4], refs[-4:]
     head = lax.axis_index("head")
     rows = total.shape[0] // len(shares)
     lat_width = gain_ref.shape[0]
@@ -407,12 +424,20 @@
         total[pl.ds(pl.multiple_of((head ^ m) * rows, rows), rows), :] = unfold(
             ref[...].astype(f32), total.shape[1], rows % 32 == 0
         )
+    blocks = [slice(j, min(j + 128, total.shape[1])) for j in range(0, total.shape[1], 128)]
+    copies = [pltpu.make_async_copy(out_ref.at[b], out_hbm.at[b], sems.at[j]) for j, b in enumerate(blocks)]
     values = cache_t_ref[:lat_width, :].astype(f32)
     inverse = lax.rsqrt(jnp.mean(values * values, axis=0, keepdims=True) + eps_norm)
+    out_ref[lat_width:, :] = jnp.transpose(total[:, lat_width:])
+    copies[-1].start()
     scaled = jnp.transpose(total[:, :lat_width] * gain_ref[...].astype(f32)[None, :])
     inner = jnp.mean(values * scaled, axis=0, keepdims=True)
-    out_ref[:lat_width, :] = inverse * scaled - values * (inverse * inverse * inverse * inner)
-    out_ref[lat_width:, :] = jnp.transpose(total[:, lat_width:])
+    factor = inverse * inverse * inverse * inner
+    for block, copy in zip(blocks[:-1], copies):
+        out_ref[block, :] = inverse * scaled[block] - values[block] * factor
+        copy.start()
+    for copy in copies:
+        copy.wait()
 
 
 def local(q_nope, q_rope, kv_cache, kv_gain, w_uk, w_uv, attn_out, d_out, span_table):
@@ -466,14 +491,19 @@
         name="own_keys",
     )(cache_t, kv_gain)
     *pieces, keys_own = lax.optimization_barrier((*pieces, keys_own))
-    pieces = pl.pallas_call(
+    piece_total = (z_count - 1) * piece.shape[0]
+    pieces, first = pl.pallas_call(
         functools.partial(join_chips_kernel, on, cat_width),
-        out_shape=shape(((z_count - 1) * piece.shape[0], piece.shape[1]), bf16),
-        in_specs=[in_vmem] * z_count,
-        out_specs=in_vmem,
+        out_shape=(
+            shape((piece_total, piece.shape[1]), bf16),
+            shape((keys_own.shape[0] + piece_total, piece.shape[1]), bf16),
+        ),
+        in_specs=[in_vmem] * (z_count + 1),
+        out_specs=(in_vmem,) * 2,
         compiler_params=params(8),
         name="join_chips",
-    )(kv_gain, *pieces)
+    )(kv_gain, keys_own, *pieces)
+    sib_first = to_core(first)
 
     def join(rows, name):
         return pl.pallas_call(
@@ -497,29 +527,28 @@
         ),
         name="project",
     )(q_nope, q_rope, w_uk, d_out, attn_out, w_uv, pieces)
-    pieces = [pieces] + [to_head(pieces, m) for m in range(1, head_count)]
-    *pieces, queries, d_latent = lax.optimization_barrier((*pieces, queries, d_latent))
-    pieces = join([keys_own] + pieces, "join_heads")
-    sib_pieces = to_core(pieces)
+    pieces = [to_head(pieces, m) for m in range(1, head_count)]
+    *pieces, sib_first, queries, d_latent = lax.optimization_barrier((*pieces, sib_first, queries, d_latent))
+    later = join(pieces, "join_heads")
+    sib_later = to_core(later)
 
     piece_shape = piece.shape
     share_shape = (z_count * piece_shape[0], piece_shape[1])
     all_shape = (head_count * share_shape[0], piece_shape[1])
-    keys, d_score, keep, send = pl.pallas_call(
+    keys, d_score, send, score_part, prob_part = pl.pallas_call(
         functools.partial(attend_kernel, head_count),
         out_shape=(
             shape((total, cat_width), bf16),
             shape((tile_total * key_tile, row_count), bf16),
             shape(all_shape, bf16),
-            shape(all_shape, bf16),
+            shape((total, cat_width), f32),
+            shape((total, lat_width), f32),
         ),
-        in_specs=[in_smem] + [in_vmem] * 4,
-        out_specs=(in_vmem,) * 4,
+        in_specs=[in_smem] + [in_vmem] * 6,
+        out_specs=(in_vmem,) * 5,
         scratch_shapes=[
             pltpu.VMEM((tile_total * key_tile, row_count), f32),
-            pltpu.VMEM((total, cat_width), f32),
-            pltpu.VMEM((total, lat_width), f32),
-            pltpu.VMEM((2, 2 * key_tile, row_count), bf16),
+            pltpu.VMEM((2, key_tile, row_count), bf16),
             pltpu.VMEM((8, 128) if piece_rows % 16 == 0 else (total, cat_width), f32),
         ],
         compiler_params=params(attend_mib if total <= 2048 else 56),
@@ -529,9 +558,17 @@
             transcendentals=tile_total * key_tile * row_count,
         ),
         name="attend",
-    )(spans, pieces, sib_pieces, queries, d_latent)
+    )(spans, first, later, sib_first, sib_later, queries, d_latent)
 
     recv = to_core(send)
+    keep = pl.pallas_call(
+        functools.partial(pack, 0, head_count),
+        out_shape=shape(all_shape, bf16),
+        in_specs=[in_smem] + [in_vmem] * 2,
+        out_specs=in_vmem,
+        compiler_params=params(6),
+        name="pack_keep",
+    )(spans, score_part, prob_part)
     sums = pl.pallas_call(
         pair_sum_kernel,
         out_shape=(shape(share_shape, f32),) + (shape(share_shape, bf16),) * (head_count - 1),
@@ -580,8 +617,12 @@
         norm_back_kernel,
         out_shape=shape((cat_width, tok_rows), f32),
         in_specs=[in_vmem] * (2 + head_count),
-        out_specs=in_vmem,
-        scratch_shapes=[pltpu.VMEM((tok_rows, cat_width), f32)],
+        out_specs=in_any,
+        scratch_shapes=[
+            pltpu.VMEM((tok_rows, cat_width), f32),
+            pltpu.VMEM((cat_width, tok_rows), f32),
+            pltpu.SemaphoreType.DMA((-(-cat_width // 128),)),
+        ],
         compiler_params=params(8),
         name="norm_back",
     )(cache_t, kv_gain, *shares)

time: 59.1 us -> 59.1 us (level)
  Pallas kernels: 20.7 us -> 19.4 us
  waiting for transfers between devices: 14.7 us -> 15.9 us
    ppermute x9, waiting for transfers between devices: 6.06 us -> 8.47 us  [to_head(): return lax.ppermute(rows, 'head', [(j, j ^ m) for j in range(head_count)])]
    pallas_call x1, Pallas kernels: 10.3 us -> 9.15 us  [local(): pl.pallas_call(functools.partial(attend_kernel, head_count), out_shape=(s...]
    ppermute x2 -> x3, waiting for transfers between devices: 3.86 us -> 2.72 us  [to_core(): return lax.ppermute(rows, 'ctx', [(i, i ^ 1) for i in range(ctx_count)])]
    pallas_call x1, Pallas kernels: 5.63 us -> 4.75 us  [local(): pl.pallas_call(functools.partial(query_kernel, scale), out_shape=(shape(q...]
    pallas_call x0 -> x1, Pallas kernels: none -> 0.76 us  [local(): pl.pallas_call(functools.partial(pack, 0, head_count), out_shape=shape(al...]
  transfers between devices with their start and end apart: 17 -> 18, of which waited for: 14 -> 13; matrix products, arithmetic and copies ran while one was open for 0% -> 0% of each run, Pallas kernels for 13% -> 13%
where the time goes in v3:
time: 59.1 us; the launch traced here: 59 us
  starting transfers between devices  21.2 us (36%)
  Pallas kernels  19.4 us (33%)
  waiting for transfers between devices  15.9 us (27%)
  local copies, waits for them, and re-layouts  1.63 us (3%)
  between operations  0.77 us (1%)
    ppermute x9, starting transfers between devices, to_head(): return lax.ppermute(rows, 'head', [(j, j ^ m) for j in range(head_count)])  10.7 us
    ppermute x6, starting transfers between devices, to_chip(): return lax.ppermute(rows, 'ctx', [(i, i ^ 2 * k) for i in range(ctx_count)])  10.2 us
    pallas_call x1, Pallas kernels, local(): pl.pallas_call(functools.partial(attend_kernel, head_count), out_shape=(s...  9.15 us
    ppermute x9, waiting for transfers between devices, to_head(): return lax.ppermute(rows, 'head', [(j, j ^ m) for j in range(head_count)])  8.47 us
    ppermute x6, waiting for transfers between devices, to_chip(): return lax.ppermute(rows, 'ctx', [(i, i ^ 2 * k) for i in range(ctx_count)])  4.76 us
    pallas_call x1, Pallas kernels, local(): pl.pallas_call(functools.partial(query_kernel, scale), out_shape=(shape(q...  4.75 us
    ppermute x3, waiting for transfers between devices, to_core(): return lax.ppermute(rows, 'ctx', [(i, i ^ 1) for i in range(ctx_count)])  2.72 us
    pallas_call x1, Pallas kernels, local(): pl.pallas_call(functools.partial(project_kernel, scale * log2_e), out_sha...  1.91 us
  transfers between devices with their start and end apart: 18, of which 13 were waited for; matrix products, arithmetic and copies ran while one was open for 0% of the time, Pallas kernels for 13%

profile of v3, /device:TPU:0, one launch (start us, length us, event | category | flops | bytes accessed | tf_op | source)
XLA Modules:
  0.0 59.0 jit_solution(16969036073643444177)
XLA Ops:
  0.6 1.1 %piece.1 = bf16[144,128]{1,0:T(8,128)(2,1)S(1)} custom-call(bf16[576,128]{1,0:T(8,128)(2,1)} %bitcast.3), custom_call_target="tpu_custom_call" | custom-call | tf_op jit(solution)/shard_map/piece/pallas_call | solution.py:470
  1.8 5.1 %collective-permute-start.2 = (bf16[144,128]{1,0:T(8,128)(2,1)S(1)}, bf16[144,128]{1,0:T(8,128)(2,1)S(1)}, u32[]{:S(2)}, u32[]{:S(2)}) collective-permute-start(bf16[144,128]{1,0:T(8,128)(2,1)S(1)} %piece.1), channel_id=1, source_target_pairs={{0,24},{4,28},{8,16},{12,20},{16,8},{20,12},{24,0},{28,4},{1,25},{... | collective-permute-start | bytes 110600 | tf_op jit(solution)/shard_map/ppermute | solution.py:464
  7.5 0.9 %copy-done.2 = bf16[128,576]{0,1:T(8,128)(2,1)S(1)} copy-done((bf16[128,576]{0,1:T(8,128)(2,1)S(1)}, bf16[128,576]{0,1:T(8,128)(2,1)}, u32[]{:S(2)}) %copy-start.2) | copy-done | bytes 147480
  9.4 2.3 %collective-permute-done.1.refs_1_ = bf16[144,128]{1,0:T(8,128)(2,1)S(1)} collective-permute-done((bf16[144,128]{1,0:T(8,128)(2,1)S(1)}, bf16[144,128]{1,0:T(8,128)(2,1)S(1)}, u32[]{:S(2)}, u32[]{:S(2)}) %collective-permute-start.1) | collective-permute-done | bytes 36896 | tf_op jit(solution)/shard_map/ppermute | solution.py:464
  12.0 2.5 %collective-permute-start.5 = (bf16[432,128]{1,0:T(8,128)(2,1)S(1)}, bf16[432,128]{1,0:T(8,128)(2,1)S(1)}, u32[]{:S(2)}, u32[]{:S(2)}) collective-permute-start(bf16[432,128]{1,0:T(8,128)(2,1)S(1)} %get-tuple-element.48.unused_ref), channel_id=1, source_target_pairs={{0,3},{1,2},{2,1},{3,0},{4,7},{5,6},{6,5},{7,4},{8,11},{9,10},{10,... | collective-permute-start | bytes 331784 | tf_op jit(solution)/shard_map/ppermute | solution.py:467
  15.6 1.9 %project.1 = (bf16[2,1024,576]{2,1,0:T(8,128)(2,1)S(1)}, bf16[2,1040,512]{2,1,0:T(8,128)(2,1)S(1)}) custom-call(bf16[128,2048]{1,0:T(8,128)(2,1)S(1)} %copy-done.4, bf16[128,1024]{1,0:T(8,128)(2,1)S(1)} %copy-done.7, bf16[16,128,512]{2,1,0:T(8,128)(2,1)S(1)} %copy-done, bf16[128,2048]{1,0:T(8,128)(2,1)S(1)} %copy-done.5, bf16[128,2048]{1,0:T(8,128)(2,1)S(1)} %copy-done.6, ...), custom_call_target="tpu_custom_call" | custom-call | flops 536870912 | bytes 12582912 | tf_op jit(solution)/shard_map/project/pallas_call | solution.py:518
  17.5 1.0 %collective-permute-done.5.refs_2_ = bf16[432,128]{1,0:T(8,128)(2,1)S(1)} collective-permute-done((bf16[432,128]{1,0:T(8,128)(2,1)S(1)}, bf16[432,128]{1,0:T(8,128)(2,1)S(1)}, u32[]{:S(2)}, u32[]{:S(2)}) %collective-permute-start.5) | collective-permute-done | bytes 110624 | tf_op jit(solution)/shard_map/ppermute | solution.py:467
  18.4 2.3 %collective-permute-done.4.refs_1_ = bf16[432,128]{1,0:T(8,128)(2,1)S(1)} collective-permute-done((bf16[432,128]{1,0:T(8,128)(2,1)S(1)}, bf16[432,128]{1,0:T(8,128)(2,1)S(1)}, u32[]{:S(2)}, u32[]{:S(2)}) %collective-permute-start.4) | collective-permute-done | bytes 110624 | tf_op jit(solution)/shard_map/ppermute | solution.py:467
  20.9 1.6 %collective-permute-done.7.refs_4_ = bf16[1296,128]{1,0:T(8,128)(2,1)S(1)} collective-permute-done((bf16[1296,128]{1,0:T(8,128)(2,1)S(1)}, bf16[1296,128]{1,0:T(8,128)(2,1)S(1)}, u32[]{:S(2)}, u32[]{:S(2)}) %collective-permute-start.7) | collective-permute-done | bytes 331808 | tf_op jit(solution)/shard_map/ppermute | solution.py:461
  22.5 9.1 %attend.1 = (bf16[1024,576]{1,0:T(8,128)(2,1)S(1)}, bf16[1280,1024]{1,0:T(8,128)(2,1)S(1)}, bf16[2304,128]{1,0:T(8,128)(2,1)S(1)}, f32[1024,576]{1,0:T(8,128)S(1)}, f32[1024,512]{1,0:T(8,128)S(1)}) custom-call(s32[2,8]{1,0:T(2,128)S(1)} %bitcast.6, bf16[1008,128]{1,0:T(8,128)(2,1)S(1)} %get-tuple-element.47.refs_1_, ...), custom_call_target="tpu_custom_call" | custom-call | flops 5704253440 | bytes 12582912 | tf_op jit(solution)/shard_map/attend/pallas_call | solution.py:538
  31.9 0.8 %pack_keep.1.keep_ref = bf16[2304,128]{1,0:T(8,128)(2,1)S(1)} custom-call(s32[2,8]{1,0:T(2,128)S(1)} %bitcast.7, f32[1024,576]{1,0:T(8,128)S(1)} %get-tuple-element.57.score_part, f32[1024,512]{1,0:T(8,128)S(1)} %get-tuple-element.58.prob_part), custom_call_target="tpu_custom_call" | custom-call | tf_op jit(solution)/shard_map/pack_keep/pallas_call | solution.py:564
  32.6 1.1 %collective-permute-done.8.recv_ref = bf16[2304,128]{1,0:T(8,128)(2,1)S(1)} collective-permute-done((bf16[2304,128]{1,0:T(8,128)(2,1)S(1)}, bf16[2304,128]{1,0:T(8,128)(2,1)S(1)}, u32[]{:S(2)}, u32[]{:S(2)}) %collective-permute-start.8) | collective-permute-done | bytes 589856 | tf_op jit(solution)/shard_map/ppermute | solution.py:461
  33.9 1.7 %collective-permute-start.9 = (bf16[576,128]{1,0:T(8,128)(2,1)S(1)}, bf16[576,128]{1,0:T(8,128)(2,1)S(1)}, u32[]{:S(2)}, u32[]{:S(2)}) collective-permute-start(bf16[576,128]{1,0:T(8,128)(2,1)S(1)} %get-tuple-element.66), channel_id=1, source_target_pairs={{0,3},{1,2},{2,1},{3,0},{4,7},{5,6},{6,5},{7,4},{8,11},{9,10},{10,... | collective-permute-start | bytes 442376 | tf_op jit(solution)/shard_map/ppermute | solution.py:467
  35.6 1.3 %collective-permute-start.10 = (bf16[576,128]{1,0:T(8,128)(2,1)S(1)}, bf16[576,128]{1,0:T(8,128)(2,1)S(1)}, u32[]{:S(2)}, u32[]{:S(2)}) collective-permute-start(bf16[576,128]{1,0:T(8,128)(2,1)S(1)} %get-tuple-element.67), channel_id=1, source_target_pairs={{0,2},{1,3},{2,0},{3,1},{4,6},{5,7},{6,4},{7,5},{8,10},{9,11},{10,... | collective-permute-start | bytes 442376 | tf_op jit(solution)/shard_map/ppermute | solution.py:467
  37.4 4.7 %query_grads.1 = (bf16[128,2048]{1,0:T(8,128)(2,1)}, bf16[128,1024]{1,0:T(8,128)(2,1)}) custom-call(s32[2,8]{1,0:T(2,128)S(1)} %bitcast.8, bf16[1024,576]{1,0:T(8,128)(2,1)S(1)} %get-tuple-element.69.keys_ref, bf16[1280,1024]{1,0:T(8,128)(2,1)S(1)} %get-tuple-element.70.ds_ref, bf16[16,128,512]{2,1,0:T(8,128)(2,1)S(1)} %copy-done), custom_call_target="tpu_custom_call" | custom-call | flops 1509949440 | bytes 8388608 | tf_op jit(solution)/shard_map/query_grads/pallas_call | solution.py:581
  42.2 1.7 %collective-permute-done.10.refs_2_ = bf16[576,128]{1,0:T(8,128)(2,1)S(1)} collective-permute-done((bf16[576,128]{1,0:T(8,128)(2,1)S(1)}, bf16[576,128]{1,0:T(8,128)(2,1)S(1)}, u32[]{:S(2)}, u32[]{:S(2)}) %collective-permute-start.10) | collective-permute-done | bytes 147488 | tf_op jit(solution)/shard_map/ppermute | solution.py:467
  44.0 1.5 %collective-permute-start.12 = (bf16[144,128]{1,0:T(8,128)(2,1)S(1)}, bf16[144,128]{1,0:T(8,128)(2,1)S(1)}, u32[]{:S(2)}, u32[]{:S(2)}) collective-permute-start(bf16[144,128]{1,0:T(8,128)(2,1)S(1)} %get-tuple-element.80), channel_id=1, source_target_pairs={{0,24},{4,28},{8,16},{12,20},{16,8},{20,12},{24,0},{28,4},{1,25},{... | collective-permute-start | bytes 110600 | tf_op jit(solution)/shard_map/ppermute | solution.py:464
  46.2 2.3 %collective-permute-start.14 = (bf16[144,128]{1,0:T(8,128)(2,1)S(1)}, bf16[144,128]{1,0:T(8,128)(2,1)S(1)}, u32[]{:S(2)}, u32[]{:S(2)}) collective-permute-start(bf16[144,128]{1,0:T(8,128)(2,1)S(1)} %get-tuple-element.82), channel_id=1, source_target_pairs={{0,8},{4,12},{8,0},{12,4},{16,24},{20,28},{24,16},{28,20},{1,9},{5... | collective-permute-start | bytes 110600 | tf_op jit(solution)/shard_map/ppermute | solution.py:464
  48.5 1.8 %collective-permute-done.12.refs_1_ = bf16[144,128]{1,0:T(8,128)(2,1)S(1)} collective-permute-done((bf16[144,128]{1,0:T(8,128)(2,1)S(1)}, bf16[144,128]{1,0:T(8,128)(2,1)S(1)}, u32[]{:S(2)}, u32[]{:S(2)}) %collective-permute-start.12) | collective-permute-done | bytes 36896 | tf_op jit(solution)/shard_map/ppermute | solution.py:464
  51.0 1.7 %collective-permute-start.17 = (bf16[144,128]{1,0:T(8,128)(2,1)S(1)}, bf16[144,128]{1,0:T(8,128)(2,1)S(1)}, u32[]{:S(2)}, u32[]{:S(2)}) collective-permute-start(bf16[144,128]{1,0:T(8,128)(2,1)S(1)} %chip_sum.1.refs_0_), channel_id=1, source_target_pairs={{0,3},{1,2},{2,1},{3,0},{4,7},{5,6},{6,5},{7,4},{8,11},{9,10},{10,... | collective-permute-start | bytes 110600 | tf_op jit(solution)/shard_map/ppermute | solution.py:467
  52.7 1.3 %collective-permute-start.16 = (bf16[144,128]{1,0:T(8,128)(2,1)S(1)}, bf16[144,128]{1,0:T(8,128)(2,1)S(1)}, u32[]{:S(2)}, u32[]{:S(2)}) collective-permute-start(bf16[144,128]{1,0:T(8,128)(2,1)S(1)} %chip_sum.1.refs_0_), channel_id=1, source_target_pairs={{0,2},{1,3},{2,0},{3,1},{4,6},{5,7},{6,4},{7,5},{8,10},{9,11},{10,... | collective-permute-start | bytes 110600 | tf_op jit(solution)/shard_map/ppermute | solution.py:467
  54.5 1.6 %collective-permute-done.17.refs_3_ = bf16[144,128]{1,0:T(8,128)(2,1)S(1)} collective-permute-done((bf16[144,128]{1,0:T(8,128)(2,1)S(1)}, bf16[144,128]{1,0:T(8,128)(2,1)S(1)}, u32[]{:S(2)}, u32[]{:S(2)}) %collective-permute-start.17) | collective-permute-done | bytes 36896 | tf_op jit(solution)/shard_map/ppermute | solution.py:467
  56.6 1.3 %collective-permute-done.15.refs_1_ = bf16[144,128]{1,0:T(8,128)(2,1)S(1)} collective-permute-done((bf16[144,128]{1,0:T(8,128)(2,1)S(1)}, bf16[144,128]{1,0:T(8,128)(2,1)S(1)}, u32[]{:S(2)}, u32[]{:S(2)}) %collective-permute-start.15) | collective-permute-done | bytes 36896 | tf_op jit(solution)/shard_map/ppermute | solution.py:467
  58.0 1.0 %norm_back.1 = f32[576,128]{1,0:T(8,128)} custom-call(bf16[576,128]{1,0:T(8,128)(2,1)S(1)} %bitcast.5, bf16[512]{0:T(512)(128)(2,1)S(1)} %copy-done.10, bf16[144,128]{1,0:T(8,128)(2,1)S(1)} %chip_sum.1.refs_0_, bf16[144,128]{1,0:T(8,128)(2,1)S(1)} %collective-permute-done.15.refs_1_, bf16[144,128]{1,0:T(8,128)(2,1)S(1)} %collective-permute-done.16.refs_2_, ...), custom_call_target="tpu_custom_call" | custom-call | tf_op jit(solution)/shard_map/norm_back/pallas_call | solution.py:616
  (46 shorter events, 6.5 us)
Async XLA Ops:
  1.7 13.8 %copy-start = (bf16[16,128,512]{2,1,0:T(8,128)(2,1)S(1)}, bf16[16,128,512]{2,1,0:T(8,128)(2,1)}, u32[]{:S(2)}) copy-start(bf16[16,128,512]{2,1,0:T(8,128)(2,1)} %w_uk_ref.3) | copy-start | bytes 6291460
  1.8 13.8 %copy-start.1 = (bf16[16,512,128]{2,1,0:T(8,128)(2,1)S(1)}, bf16[16,512,128]{2,1,0:T(8,128)(2,1)}, u32[]{:S(2)}) copy-start(bf16[16,512,128]{2,1,0:T(8,128)(2,1)} %w_uv_ref.1) | copy-start | bytes 6291460
  1.8 7.7 %collective-permute-start.2 = (bf16[144,128]{1,0:T(8,128)(2,1)S(1)}, bf16[144,128]{1,0:T(8,128)(2,1)S(1)}, u32[]{:S(2)}, u32[]{:S(2)}) collective-permute-start(bf16[144,128]{1,0:T(8,128)(2,1)S(1)} %piece.1), channel_id=1, source_target_pairs={{0,24},{4,28},{8,16},{12,20},{16,8},{20,12},{24,0},{28,4},{1,25},{... | collective-permute-start | bytes 110600 | tf_op jit(solution)/shard_map/ppermute | solution.py:464
  6.9 4.9 %collective-permute-start.1 = (bf16[144,128]{1,0:T(8,128)(2,1)S(1)}, bf16[144,128]{1,0:T(8,128)(2,1)S(1)}, u32[]{:S(2)}, u32[]{:S(2)}) collective-permute-start(bf16[144,128]{1,0:T(8,128)(2,1)S(1)} %piece.1), channel_id=1, source_target_pairs={{0,16},{4,20},{8,24},{12,28},{16,0},{20,4},{24,8},{28,12},{1,17},{... | collective-permute-start | bytes 110600 | tf_op jit(solution)/shard_map/ppermute | solution.py:464
  6.9 4.9 %collective-permute-start = (bf16[144,128]{1,0:T(8,128)(2,1)S(1)}, bf16[144,128]{1,0:T(8,128)(2,1)S(1)}, u32[]{:S(2)}, u32[]{:S(2)}) collective-permute-start(bf16[144,128]{1,0:T(8,128)(2,1)S(1)} %piece.1), channel_id=1, source_target_pairs={{0,8},{4,12},{8,0},{12,4},{16,24},{20,28},{24,16},{28,20},{1,9},{5... | collective-permute-start | bytes 110600 | tf_op jit(solution)/shard_map/ppermute | solution.py:464
  9.1 6.4 %copy-start.7 = (bf16[128,1024]{1,0:T(8,128)(2,1)S(1)}, bf16[128,1024]{1,0:T(8,128)(2,1)}, u32[]{:S(2)}) copy-start(bf16[128,1024]{1,0:T(8,128)(2,1)} %rope_ref.1) | copy-start | bytes 786436
  11.9 8.9 %collective-permute-start.6 = (bf16[1008,128]{1,0:T(8,128)(2,1)S(1)}, bf16[1008,128]{1,0:T(8,128)(2,1)S(1)}, u32[]{:S(2)}, u32[]{:S(2)}) collective-permute-start(bf16[1008,128]{1,0:T(8,128)(2,1)S(1)} %get-tuple-element.47.refs_1_), channel_id=1, source_target_pairs={{0,4},{4,0},{8,12},{12,8},{16,20},{20,16},{24,28},{28,24},{1,5},{5... | collective-permute-start | bytes 774152 | tf_op jit(solution)/shard_map/ppermute | solution.py:461
  12.0 10.6 %copy-start.8 = (s32[8,2]{0,1:T(2,128)S(1)}, s32[8,2]{0,1:T(2,128)}, u32[]{:S(2)}) copy-start(s32[8,2]{0,1:T(2,128)} %param.17) | copy-start | bytes 196
  12.0 6.5 %collective-permute-start.5 = (bf16[432,128]{1,0:T(8,128)(2,1)S(1)}, bf16[432,128]{1,0:T(8,128)(2,1)S(1)}, u32[]{:S(2)}, u32[]{:S(2)}) collective-permute-start(bf16[432,128]{1,0:T(8,128)(2,1)S(1)} %get-tuple-element.48.unused_ref), channel_id=1, source_target_pairs={{0,3},{1,2},{2,1},{3,0},{4,7},{5,6},{6,5},{7,4},{8,11},{9,10},{10,... | collective-permute-start | bytes 331784 | tf_op jit(solution)/shard_map/ppermute | solution.py:467
  14.5 6.2 %collective-permute-start.4 = (bf16[432,128]{1,0:T(8,128)(2,1)S(1)}, bf16[432,128]{1,0:T(8,128)(2,1)S(1)}, u32[]{:S(2)}, u32[]{:S(2)}) collective-permute-start(bf16[432,128]{1,0:T(8,128)(2,1)S(1)} %get-tuple-element.48.unused_ref), channel_id=1, source_target_pairs={{0,2},{1,3},{2,0},{3,1},{4,6},{5,7},{6,4},{7,5},{8,10},{9,11},{10,... | collective-permute-start | bytes 331784 | tf_op jit(solution)/shard_map/ppermute | solution.py:467
  15.0 5.8 %collective-permute-start.3 = (bf16[432,128]{1,0:T(8,128)(2,1)S(1)}, bf16[432,128]{1,0:T(8,128)(2,1)S(1)}, u32[]{:S(2)}, u32[]{:S(2)}) collective-permute-start(bf16[432,128]{1,0:T(8,128)(2,1)S(1)} %get-tuple-element.48.unused_ref), channel_id=1, source_target_pairs={{0,1},{1,0},{2,3},{3,2},{4,5},{5,4},{6,7},{7,6},{8,9},{9,8},{10,11... | collective-permute-start | bytes 331784 | tf_op jit(solution)/shard_map/ppermute | solution.py:467
  20.8 1.7 %collective-permute-start.7 = (bf16[1296,128]{1,0:T(8,128)(2,1)S(1)}, bf16[1296,128]{1,0:T(8,128)(2,1)S(1)}, u32[]{:S(2)}, u32[]{:S(2)}) collective-permute-start(bf16[1296,128]{1,0:T(8,128)(2,1)S(1)} %join_heads.1.refs_2_), channel_id=1, source_target_pairs={{0,4},{4,0},{8,12},{12,8},{16,20},{20,16},{24,28},{28,24},{1,5},{5... | collective-permute-start | bytes 995336 | tf_op jit(solution)/shard_map/ppermute | solution.py:461
  31.7 2.1 %collective-permute-start.8 = (bf16[2304,128]{1,0:T(8,128)(2,1)S(1)}, bf16[2304,128]{1,0:T(8,128)(2,1)S(1)}, u32[]{:S(2)}, u32[]{:S(2)}) collective-permute-start(bf16[2304,128]{1,0:T(8,128)(2,1)S(1)} %get-tuple-element.59), channel_id=1, source_target_pairs={{0,4},{4,0},{8,12},{12,8},{16,20},{20,16},{24,28},{28,24},{1,5},{5... | collective-permute-start | bytes 1769480 | tf_op jit(solution)/shard_map/ppermute | solution.py:461
  33.9 8.3 %collective-permute-start.9 = (bf16[576,128]{1,0:T(8,128)(2,1)S(1)}, bf16[576,128]{1,0:T(8,128)(2,1)S(1)}, u32[]{:S(2)}, u32[]{:S(2)}) collective-permute-start(bf16[576,128]{1,0:T(8,128)(2,1)S(1)} %get-tuple-element.66), channel_id=1, source_target_pairs={{0,3},{1,2},{2,1},{3,0},{4,7},{5,6},{6,5},{7,4},{8,11},{9,10},{10,... | collective-permute-start | bytes 442376 | tf_op jit(solution)/shard_map/ppermute | solution.py:467
  35.6 8.3 %collective-permute-start.10 = (bf16[576,128]{1,0:T(8,128)(2,1)S(1)}, bf16[576,128]{1,0:T(8,128)(2,1)S(1)}, u32[]{:S(2)}, u32[]{:S(2)}) collective-permute-start(bf16[576,128]{1,0:T(8,128)(2,1)S(1)} %get-tuple-element.67), channel_id=1, source_target_pairs={{0,2},{1,3},{2,0},{3,1},{4,6},{5,7},{6,4},{7,5},{8,10},{9,11},{10,... | collective-permute-start | bytes 442376 | tf_op jit(solution)/shard_map/ppermute | solution.py:467
  36.9 7.0 %collective-permute-start.11 = (bf16[576,128]{1,0:T(8,128)(2,1)S(1)}, bf16[576,128]{1,0:T(8,128)(2,1)S(1)}, u32[]{:S(2)}, u32[]{:S(2)}) collective-permute-start(bf16[576,128]{1,0:T(8,128)(2,1)S(1)} %get-tuple-element.68), channel_id=1, source_target_pairs={{0,1},{1,0},{2,3},{3,2},{4,5},{5,4},{6,7},{7,6},{8,9},{9,8},{10,11... | collective-permute-start | bytes 442376 | tf_op jit(solution)/shard_map/ppermute | solution.py:467
  37.4 20.5 %copy-start.3 = (bf16[128,576]{0,1:T(8,128)(2,1)S(1)}, bf16[128,576]{0,1:T(8,128)(2,1)}, u32[]{:S(2)}) copy-start(bf16[128,576]{0,1:T(8,128)(2,1)} %param.11) | copy-start | bytes 442372
  37.4 20.5 %copy-start.10 = (bf16[512]{0:T(512)(128)(2,1)S(1)}, bf16[512]{0:T(512)(128)(2,1)}, u32[]{:S(2)}) copy-start(bf16[512]{0:T(512)(128)(2,1)} %gain_ref.5) | copy-start | bytes 3076
  44.0 6.2 %collective-permute-start.12 = (bf16[144,128]{1,0:T(8,128)(2,1)S(1)}, bf16[144,128]{1,0:T(8,128)(2,1)S(1)}, u32[]{:S(2)}, u32[]{:S(2)}) collective-permute-start(bf16[144,128]{1,0:T(8,128)(2,1)S(1)} %get-tuple-element.80), channel_id=1, source_target_pairs={{0,24},{4,28},{8,16},{12,20},{16,8},{20,12},{24,0},{28,4},{1,25},{... | collective-permute-start | bytes 110600 | tf_op jit(solution)/shard_map/ppermute | solution.py:464
  45.6 5.0 %collective-permute-start.13 = (bf16[144,128]{1,0:T(8,128)(2,1)S(1)}, bf16[144,128]{1,0:T(8,128)(2,1)S(1)}, u32[]{:S(2)}, u32[]{:S(2)}) collective-permute-start(bf16[144,128]{1,0:T(8,128)(2,1)S(1)} %get-tuple-element.81), channel_id=1, source_target_pairs={{0,16},{4,20},{8,24},{12,28},{16,0},{20,4},{24,8},{28,12},{1,17},{... | collective-permute-start | bytes 110600 | tf_op jit(solution)/shard_map/ppermute | solution.py:464
  46.2 4.7 %collective-permute-start.14 = (bf16[144,128]{1,0:T(8,128)(2,1)S(1)}, bf16[144,128]{1,0:T(8,128)(2,1)S(1)}, u32[]{:S(2)}, u32[]{:S(2)}) collective-permute-start(bf16[144,128]{1,0:T(8,128)(2,1)S(1)} %get-tuple-element.82), channel_id=1, source_target_pairs={{0,8},{4,12},{8,0},{12,4},{16,24},{20,28},{24,16},{28,20},{1,9},{5... | collective-permute-start | bytes 110600 | tf_op jit(solution)/shard_map/ppermute | solution.py:464
  51.0 5.1 %collective-permute-start.17 = (bf16[144,128]{1,0:T(8,128)(2,1)S(1)}, bf16[144,128]{1,0:T(8,128)(2,1)S(1)}, u32[]{:S(2)}, u32[]{:S(2)}) collective-permute-start(bf16[144,128]{1,0:T(8,128)(2,1)S(1)} %chip_sum.1.refs_0_), channel_id=1, source_target_pairs={{0,3},{1,2},{2,1},{3,0},{4,7},{5,6},{6,5},{7,4},{8,11},{9,10},{10,... | collective-permute-start | bytes 110600 | tf_op jit(solution)/shard_map/ppermute | solution.py:467
  52.7 4.0 %collective-permute-start.16 = (bf16[144,128]{1,0:T(8,128)(2,1)S(1)}, bf16[144,128]{1,0:T(8,128)(2,1)S(1)}, u32[]{:S(2)}, u32[]{:S(2)}) collective-permute-start(bf16[144,128]{1,0:T(8,128)(2,1)S(1)} %chip_sum.1.refs_0_), channel_id=1, source_target_pairs={{0,2},{1,3},{2,0},{3,1},{4,6},{5,7},{6,4},{7,5},{8,10},{9,11},{10,... | collective-permute-start | bytes 110600 | tf_op jit(solution)/shard_map/ppermute | solution.py:467
  54.0 4.0 %collective-permute-start.15 = (bf16[144,128]{1,0:T(8,128)(2,1)S(1)}, bf16[144,128]{1,0:T(8,128)(2,1)S(1)}, u32[]{:S(2)}, u32[]{:S(2)}) collective-permute-start(bf16[144,128]{1,0:T(8,128)(2,1)S(1)} %chip_sum.1.refs_0_), channel_id=1, source_target_pairs={{0,1},{1,0},{2,3},{3,2},{4,5},{5,4},{6,7},{7,6},{8,9},{9,8},{10,11... | collective-permute-start | bytes 110600 | tf_op jit(solution)/shard_map/ppermute | solution.py:467
  (5 other events, 20.9 us)

commit v4 on v3

--- a/solution.py
+++ b/solution.py
@@ -89,17 +89,13 @@
     out_ref[...] = fold(normalised(rows, gain_ref[...].astype(f32)[None, :]), on).astype(bf16)
 
 
-def join_chips_kernel(on, width, gain_ref, own_ref, *refs):
-    refs, pieces_ref, first_ref = refs[:-2], refs[-2], refs[-1]
+def join_chips_kernel(on, width, gain_ref, *refs):
     gain = gain_ref[...].astype(f32)[None, :]
-    rows = jnp.concatenate([unfold(ref[...].astype(f32), width, on) for ref in refs], axis=0)
+    rows = jnp.concatenate([unfold(ref[...].astype(f32), width, on) for ref in refs[:-1]], axis=0)
     rows = normalised(rows, gain)
-    size = rows.shape[0] // len(refs)
-    parts = [fold(rows[i * size : (i + 1) * size], on) for i in range(len(refs))]
-    pieces = jnp.concatenate(parts, axis=0).astype(bf16)
-    pieces_ref[...] = pieces
-    first_ref[: own_ref.shape[0], :] = own_ref[...]
-    first_ref[own_ref.shape[0] :, :] = pieces
+    size = rows.shape[0] // (len(refs) - 1)
+    parts = [fold(rows[i * size : (i + 1) * size], on) for i in range(len(refs) - 1)]
+    refs[-1][...] = jnp.concatenate(parts, axis=0).astype(bf16)
 
 
 def project_kernel(
@@ -190,45 +186,45 @@
     return pl.ds(pl.multiple_of(kt * key_tile, key_tile), key_tile)
 
 
+def place_rows(head_count, side, span_ref, source, keys_ref):
+    total, cat_width = keys_ref.shape
+    z_count = lax.axis_size("ctx") // 2
+    span = total // z_count // 4
+    piece_rows = 2 * span // head_count
+    per_span = span // piece_rows
+    on = piece_rows % 32 == 0
+    start = folded(2 * span, cat_width, on)[0]
+    size = folded(piece_rows, cat_width, on)[0]
+    me, head = lax.axis_index("ctx"), lax.axis_index("head")
+    source = source if piece_rows % 16 == 0 else source[...].astype(f32)
+    rows = unfold(source[:start, :], cat_width, on).astype(keys_ref.dtype)
+    for s in range(2):
+        row = pl.multiple_of(span_ref[s, me ^ side] * span, span)
+        keys_ref[pl.ds(row, span), :] = rows[s * span : (s + 1) * span, :]
+    for m in range(head_count):
+        quarter = head ^ m
+        for k in range(1, z_count):
+            owner = 2 * (me // 2 ^ k) + lax.rem(me + side, 2)
+            row = span_ref[quarter // per_span, owner] * span + lax.rem(quarter, per_span) * piece_rows
+            rows = unfold(source[start : start + size, :], cat_width, on)
+            keys_ref[pl.ds(pl.multiple_of(row, piece_rows), piece_rows), :] = rows.astype(keys_ref.dtype)
+            start += size
+
+
 def attend_kernel(head_count, *refs):
-    span_ref, own_first, own_later, sib_first, sib_later, q_ref, dl_ref = refs[:7]
-    keys_ref, ds_ref, send_ref, score_part, prob_part, e_scr, prob_scr, raw = refs[7:]
+    span_ref, sib_pieces, placed_ref, q_ref, dl_ref = refs[:5]
+    keys_ref, ds_ref, send_ref, score_part, prob_part, e_scr, prob_scr = refs[5:]
     half_count, row_count, cat_width = q_ref.shape
     lat_width = dl_ref.shape[2]
     total = keys_ref.shape[0]
     tile_count = total // key_tile
-    z_count = lax.axis_size("ctx") // 2
-    tok_rows = total // z_count // 2
-    span = tok_rows // 2
-    piece_rows = tok_rows // head_count
-    per_span = span // piece_rows
-    me, head = lax.axis_index("ctx"), lax.axis_index("head")
-    z, core = me // 2, lax.rem(me, 2)
-    on = piece_rows % 32 == 0
-    own_size = folded(tok_rows, cat_width, on)[0]
-    piece_size = folded(piece_rows, cat_width, on)[0]
-
-    def place(owner, quarter):
-        block = span_ref[quarter // per_span, owner]
-        start = block * span + lax.rem(quarter, per_span) * piece_rows
-        return pl.ds(pl.multiple_of(start, piece_rows), piece_rows)
-
-    stage = keys_ref if piece_rows % 16 == 0 else raw
-    for side, parts in enumerate(((own_first, own_later), (sib_first, sib_later))):
-        first, later = parts if piece_rows % 16 == 0 else [ref[...].astype(f32) for ref in parts]
-        rows = unfold(first[:own_size, :], cat_width, on)
-        for s in range(2):
-            start = pl.multiple_of(span_ref[s, 2 * z + lax.rem(core + side, 2)] * span, span)
-            stage[pl.ds(start, span), :] = rows[s * span : (s + 1) * span, :]
-        for m in range(head_count):
-            source = later if m else first
-            start = (m - 1) * (z_count - 1) * piece_size if m else own_size
-            for k in range(1, z_count):
-                owner = 2 * (z ^ k) + lax.rem(core + side, 2)
-                stage[place(owner, head ^ m), :] = unfold(source[start : start + piece_size, :], cat_width, on)
-                start += piece_size
-    if stage is raw:
-        keys_ref[...] = raw[...].astype(bf16)
+    span = total // lax.axis_size("ctx") // 2
+    me = lax.axis_index("ctx")
+    if placed_ref.dtype == keys_ref.dtype:
+        place_rows(head_count, 1, span_ref, sib_pieces, keys_ref)
+    else:
+        place_rows(head_count, 1, span_ref, sib_pieces, placed_ref)
+        keys_ref[...] = placed_ref[...].astype(bf16)
 
     my_lower, my_upper = span_ref[0, me], span_ref[1, me]
     chunks = [slice(n, n + min(row_chunk, row_count)) for n in range(0, row_count, row_chunk)]
@@ -491,19 +487,14 @@
         name="own_keys",
     )(cache_t, kv_gain)
     *pieces, keys_own = lax.optimization_barrier((*pieces, keys_own))
-    piece_total = (z_count - 1) * piece.shape[0]
-    pieces, first = pl.pallas_call(
+    pieces = pl.pallas_call(
         functools.partial(join_chips_kernel, on, cat_width),
-        out_shape=(
-            shape((piece_total, piece.shape[1]), bf16),
-            shape((keys_own.shape[0] + piece_total, piece.shape[1]), bf16),
-        ),
-        in_specs=[in_vmem] * (z_count + 1),
-        out_specs=(in_vmem,) * 2,
+        out_shape=shape(((z_count - 1) * piece.shape[0], piece.shape[1]), bf16),
+        in_specs=[in_vmem] * z_count,
+        out_specs=in_vmem,
         compiler_params=params(8),
         name="join_chips",
-    )(kv_gain, keys_own, *pieces)
-    sib_first = to_core(first)
+    )(kv_gain, *pieces)
 
     def join(rows, name):
         return pl.pallas_call(
@@ -527,10 +518,20 @@
         ),
         name="project",
     )(q_nope, q_rope, w_uk, d_out, attn_out, w_uv, pieces)
-    pieces = [to_head(pieces, m) for m in range(1, head_count)]
-    *pieces, sib_first, queries, d_latent = lax.optimization_barrier((*pieces, sib_first, queries, d_latent))
-    later = join(pieces, "join_heads")
-    sib_later = to_core(later)
+    pieces = [pieces] + [to_head(pieces, m) for m in range(1, head_count)]
+    *pieces, queries, d_latent = lax.optimization_barrier((*pieces, queries, d_latent))
+    pieces = join([keys_own] + pieces, "join_heads")
+    sib_pieces = to_core(pieces)
+    aligned = piece_rows % 16 == 0
+    placed = pl.pallas_call(
+        functools.partial(place_rows, head_count, 0),
+        out_shape=shape((total, cat_width), bf16 if aligned else f32),
+        in_specs=[in_smem, in_vmem],
+        out_specs=in_vmem,
+        compiler_params=params(8),
+        name="place",
+    )(spans, pieces)
+    sib_pieces, placed = lax.optimization_barrier((sib_pieces, placed))
 
     piece_shape = piece.shape
     share_shape = (z_count * piece_shape[0], piece_shape[1])
@@ -544,12 +545,12 @@
             shape((total, cat_width), f32),
             shape((total, lat_width), f32),
         ),
-        in_specs=[in_smem] + [in_vmem] * 6,
+        in_specs=[in_smem] + [in_vmem] * 4,
+        input_output_aliases={2: 0} if aligned else {},
         out_specs=(in_vmem,) * 5,
         scratch_shapes=[
             pltpu.VMEM((tile_total * key_tile, row_count), f32),
             pltpu.VMEM((2, key_tile, row_count), bf16),
-            pltpu.VMEM((8, 128) if piece_rows % 16 == 0 else (total, cat_width), f32),
         ],
         compiler_params=params(attend_mib if total <= 2048 else 56),
         cost_estimate=pl.CostEstimate(
@@ -558,7 +559,7 @@
             transcendentals=tile_total * key_tile * row_count,
         ),
         name="attend",
-    )(spans, first, later, sib_first, sib_later, queries, d_latent)
+    )(spans, sib_pieces, placed, queries, d_latent)
 
     recv = to_core(send)
     keep = pl.pallas_call(

time: 59.1 us -> 57.9 us (0.980)
  waiting for transfers between devices: 15.9 us -> 14.1 us
  Pallas kernels: 19.4 us -> 20.1 us
    ppermute x9, waiting for transfers between devices: 8.47 us -> 6.94 us  [to_head(): return lax.ppermute(rows, 'head', [(j, j ^ m) for j in range(head_count)])]
    pallas_call x0 -> x1, Pallas kernels: none -> 0.67 us  [local(): pl.pallas_call(functools.partial(place_rows, head_count, 0), out_shape=sh...]
    ppermute x3 -> x2, waiting for transfers between devices: 2.72 us -> 2.42 us  [to_core(): return lax.ppermute(rows, 'ctx', [(i, i ^ 1) for i in range(ctx_count)])]
  transfers between devices with their start and end apart: 18 -> 17, of which waited for: 13 -> 14; matrix products, arithmetic and copies ran while one was open for 0% -> 0% of each run, Pallas kernels for 13% -> 14%
where the time goes in v4:
time: 57.9 us; the launch traced here: 57.7 us
  starting transfers between devices  21.1 us (36%)
  Pallas kernels  20.1 us (35%)
  waiting for transfers between devices  14.1 us (24%)
  local copies, waits for them, and re-layouts  1.63 us (3%)
  between operations  0.78 us (1%)
    ppermute x9, starting transfers between devices, to_head(): return lax.ppermute(rows, 'head', [(j, j ^ m) for j in range(head_count)])  10.7 us
    ppermute x6, starting transfers between devices, to_chip(): return lax.ppermute(rows, 'ctx', [(i, i ^ 2 * k) for i in range(ctx_count)])  10.2 us
    pallas_call x1, Pallas kernels, local(): pl.pallas_call(functools.partial(attend_kernel, head_count), out_shape=(s...  9.15 us
    ppermute x9, waiting for transfers between devices, to_head(): return lax.ppermute(rows, 'head', [(j, j ^ m) for j in range(head_count)])  6.94 us
    pallas_call x1, Pallas kernels, local(): pl.pallas_call(functools.partial(query_kernel, scale), out_shape=(shape(q...  4.75 us
    ppermute x6, waiting for transfers between devices, to_chip(): return lax.ppermute(rows, 'ctx', [(i, i ^ 2 * k) for i in range(ctx_count)])  4.74 us
    ppermute x2, waiting for transfers between devices, to_core(): return lax.ppermute(rows, 'ctx', [(i, i ^ 1) for i in range(ctx_count)])  2.42 us
    pallas_call x1, Pallas kernels, local(): pl.pallas_call(functools.partial(project_kernel, scale * log2_e), out_sha...  1.89 us
  transfers between devices with their start and end apart: 17, of which 14 were waited for; matrix products, arithmetic and copies ran while one was open for 0% of the time, Pallas kernels for 14%

profile of v4, /device:TPU:0, one launch (start us, length us, event | category | flops | bytes accessed | tf_op | source)
XLA Modules:
  0.0 57.7 jit_solution(11558267926719200790)
XLA Ops:
  0.6 1.1 %piece.1 = bf16[144,128]{1,0:T(8,128)(2,1)S(1)} custom-call(bf16[576,128]{1,0:T(8,128)(2,1)} %bitcast.3), custom_call_target="tpu_custom_call" | custom-call | tf_op jit(solution)/shard_map/piece/pallas_call | solution.py:466
  1.8 5.1 %collective-permute-start.2 = (bf16[144,128]{1,0:T(8,128)(2,1)S(1)}, bf16[144,128]{1,0:T(8,128)(2,1)S(1)}, u32[]{:S(2)}, u32[]{:S(2)}) collective-permute-start(bf16[144,128]{1,0:T(8,128)(2,1)S(1)} %piece.1), channel_id=1, source_target_pairs={{0,24},{4,28},{8,16},{12,20},{16,8},{20,12},{24,0},{28,4},{1,25},{... | collective-permute-start | bytes 110600 | tf_op jit(solution)/shard_map/ppermute | solution.py:460
  7.5 0.9 %copy-done.2 = bf16[128,576]{0,1:T(8,128)(2,1)S(1)} copy-done((bf16[128,576]{0,1:T(8,128)(2,1)S(1)}, bf16[128,576]{0,1:T(8,128)(2,1)}, u32[]{:S(2)}) %copy-start.2) | copy-done | bytes 147480
  9.4 2.3 %collective-permute-done.1.refs_1_ = bf16[144,128]{1,0:T(8,128)(2,1)S(1)} collective-permute-done((bf16[144,128]{1,0:T(8,128)(2,1)S(1)}, bf16[144,128]{1,0:T(8,128)(2,1)S(1)}, u32[]{:S(2)}, u32[]{:S(2)}) %collective-permute-start.1) | collective-permute-done | bytes 36896 | tf_op jit(solution)/shard_map/ppermute | solution.py:460
  11.9 2.5 %collective-permute-start.5 = (bf16[432,128]{1,0:T(8,128)(2,1)S(1)}, bf16[432,128]{1,0:T(8,128)(2,1)S(1)}, u32[]{:S(2)}, u32[]{:S(2)}) collective-permute-start(bf16[432,128]{1,0:T(8,128)(2,1)S(1)} %join_chips.1.unused_ref.refs_1_), channel_id=1, source_target_pairs={{0,3},{1,2},{2,1},{3,0},{4,7},{5,6},{6,5},{7,4},{8,11},{9,10},{10,... | collective-permute-start | bytes 331784 | tf_op jit(solution)/shard_map/ppermute | solution.py:463
  15.5 1.9 %project.1 = (bf16[2,1024,576]{2,1,0:T(8,128)(2,1)S(1)}, bf16[2,1040,512]{2,1,0:T(8,128)(2,1)S(1)}) custom-call(bf16[128,2048]{1,0:T(8,128)(2,1)S(1)} %copy-done.4, bf16[128,1024]{1,0:T(8,128)(2,1)S(1)} %copy-done.7, bf16[16,128,512]{2,1,0:T(8,128)(2,1)S(1)} %copy-done, bf16[128,2048]{1,0:T(8,128)(2,1)S(1)} %copy-done.5, bf16[128,2048]{1,0:T(8,128)(2,1)S(1)} %copy-done.6, ...), custom_call_target="tpu_custom_call" | custom-call | flops 536870912 | bytes 12582912 | tf_op jit(solution)/shard_map/project/pallas_call | solution.py:509
  17.4 1.4 %collective-permute-done.5.refs_4_ = bf16[432,128]{1,0:T(8,128)(2,1)S(1)} collective-permute-done((bf16[432,128]{1,0:T(8,128)(2,1)S(1)}, bf16[432,128]{1,0:T(8,128)(2,1)S(1)}, u32[]{:S(2)}, u32[]{:S(2)}) %collective-permute-start.5) | collective-permute-done | bytes 110624 | tf_op jit(solution)/shard_map/ppermute | solution.py:463
  18.8 0.8 %collective-permute-done.4.refs_3_ = bf16[432,128]{1,0:T(8,128)(2,1)S(1)} collective-permute-done((bf16[432,128]{1,0:T(8,128)(2,1)S(1)}, bf16[432,128]{1,0:T(8,128)(2,1)S(1)}, u32[]{:S(2)}, u32[]{:S(2)}) %collective-permute-start.4) | collective-permute-done | bytes 110624 | tf_op jit(solution)/shard_map/ppermute | solution.py:463
  20.5 1.3 %collective-permute-done.6.refs_1_ = bf16[2304,128]{1,0:T(8,128)(2,1)S(1)} collective-permute-done((bf16[2304,128]{1,0:T(8,128)(2,1)S(1)}, bf16[2304,128]{1,0:T(8,128)(2,1)S(1)}, u32[]{:S(2)}, u32[]{:S(2)}) %collective-permute-start.6) | collective-permute-done | bytes 589856 | tf_op jit(solution)/shard_map/ppermute | solution.py:457
  21.8 9.2 %attend.1 = (bf16[1024,576]{1,0:T(8,128)(2,1)S(1)}, bf16[1280,1024]{1,0:T(8,128)(2,1)S(1)}, bf16[2304,128]{1,0:T(8,128)(2,1)S(1)}, f32[1024,576]{1,0:T(8,128)S(1)}, f32[1024,512]{1,0:T(8,128)S(1)}) custom-call(s32[2,8]{1,0:T(2,128)S(1)} %bitcast.7, bf16[2304,128]{1,0:T(8,128)(2,1)S(1)} %collective-permute-done.6.refs_1_, ...), custom_call_target="tpu_custom_call", output_to_operand_aliasing={{0}: (2, {})} | custom-call | flops 5704253440 | bytes 12582912 | tf_op jit(solution)/shard_map/attend/pallas_call | solution.py:539
  31.9 1.1 %collective-permute-done.7.recv_ref = bf16[2304,128]{1,0:T(8,128)(2,1)S(1)} collective-permute-done((bf16[2304,128]{1,0:T(8,128)(2,1)S(1)}, bf16[2304,128]{1,0:T(8,128)(2,1)S(1)}, u32[]{:S(2)}, u32[]{:S(2)}) %collective-permute-start.7) | collective-permute-done | bytes 589856 | tf_op jit(solution)/shard_map/ppermute | solution.py:457
  33.2 1.6 %collective-permute-start.8 = (bf16[576,128]{1,0:T(8,128)(2,1)S(1)}, bf16[576,128]{1,0:T(8,128)(2,1)S(1)}, u32[]{:S(2)}, u32[]{:S(2)}) collective-permute-start(bf16[576,128]{1,0:T(8,128)(2,1)S(1)} %get-tuple-element.66), channel_id=1, source_target_pairs={{0,3},{1,2},{2,1},{3,0},{4,7},{5,6},{6,5},{7,4},{8,11},{9,10},{10,... | collective-permute-start | bytes 442376 | tf_op jit(solution)/shard_map/ppermute | solution.py:463
  35.4 1.3 %collective-permute-start.10 = (bf16[576,128]{1,0:T(8,128)(2,1)S(1)}, bf16[576,128]{1,0:T(8,128)(2,1)S(1)}, u32[]{:S(2)}, u32[]{:S(2)}) collective-permute-start(bf16[576,128]{1,0:T(8,128)(2,1)S(1)} %get-tuple-element.68), channel_id=1, source_target_pairs={{0,1},{1,0},{2,3},{3,2},{4,5},{5,4},{6,7},{7,6},{8,9},{9,8},{10,11... | collective-permute-start | bytes 442376 | tf_op jit(solution)/shard_map/ppermute | solution.py:463
  36.7 4.7 %query_grads.1 = (bf16[128,2048]{1,0:T(8,128)(2,1)}, bf16[128,1024]{1,0:T(8,128)(2,1)}) custom-call(s32[2,8]{1,0:T(2,128)S(1)} %bitcast.9, bf16[1024,576]{1,0:T(8,128)(2,1)S(1)} %get-tuple-element.69.keys_ref, bf16[1280,1024]{1,0:T(8,128)(2,1)S(1)} %get-tuple-element.70.ds_ref, bf16[16,128,512]{2,1,0:T(8,128)(2,1)S(1)} %copy-done), custom_call_target="tpu_custom_call" | custom-call | flops 1509949440 | bytes 8388608 | tf_op jit(solution)/shard_map/query_grads/pallas_call | solution.py:582
  41.5 1.7 %collective-permute-done.9.refs_2_ = bf16[576,128]{1,0:T(8,128)(2,1)S(1)} collective-permute-done((bf16[576,128]{1,0:T(8,128)(2,1)S(1)}, bf16[576,128]{1,0:T(8,128)(2,1)S(1)}, u32[]{:S(2)}, u32[]{:S(2)}) %collective-permute-start.9) | collective-permute-done | bytes 147488 | tf_op jit(solution)/shard_map/ppermute | solution.py:463
  43.4 1.5 %collective-permute-start.11 = (bf16[144,128]{1,0:T(8,128)(2,1)S(1)}, bf16[144,128]{1,0:T(8,128)(2,1)S(1)}, u32[]{:S(2)}, u32[]{:S(2)}) collective-permute-start(bf16[144,128]{1,0:T(8,128)(2,1)S(1)} %get-tuple-element.80), channel_id=1, source_target_pairs={{0,24},{4,28},{8,16},{12,20},{16,8},{20,12},{24,0},{28,4},{1,25},{... | collective-permute-start | bytes 110600 | tf_op jit(solution)/shard_map/ppermute | solution.py:460
  45.6 2.3 %collective-permute-start.13 = (bf16[144,128]{1,0:T(8,128)(2,1)S(1)}, bf16[144,128]{1,0:T(8,128)(2,1)S(1)}, u32[]{:S(2)}, u32[]{:S(2)}) collective-permute-start(bf16[144,128]{1,0:T(8,128)(2,1)S(1)} %get-tuple-element.82), channel_id=1, source_target_pairs={{0,8},{4,12},{8,0},{12,4},{16,24},{20,28},{24,16},{28,20},{1,9},{5... | collective-permute-start | bytes 110600 | tf_op jit(solution)/shard_map/ppermute | solution.py:460
  47.9 1.7 %collective-permute-done.11.refs_1_ = bf16[144,128]{1,0:T(8,128)(2,1)S(1)} collective-permute-done((bf16[144,128]{1,0:T(8,128)(2,1)S(1)}, bf16[144,128]{1,0:T(8,128)(2,1)S(1)}, u32[]{:S(2)}, u32[]{:S(2)}) %collective-permute-start.11) | collective-permute-done | bytes 36896 | tf_op jit(solution)/shard_map/ppermute | solution.py:460
  50.3 1.5 %collective-permute-start.16 = (bf16[144,128]{1,0:T(8,128)(2,1)S(1)}, bf16[144,128]{1,0:T(8,128)(2,1)S(1)}, u32[]{:S(2)}, u32[]{:S(2)}) collective-permute-start(bf16[144,128]{1,0:T(8,128)(2,1)S(1)} %chip_sum.1.refs_0_), channel_id=1, source_target_pairs={{0,3},{1,2},{2,1},{3,0},{4,7},{5,6},{6,5},{7,4},{8,11},{9,10},{10,... | collective-permute-start | bytes 110600 | tf_op jit(solution)/shard_map/ppermute | solution.py:463
  51.8 1.0 %collective-permute-start.15 = (bf16[144,128]{1,0:T(8,128)(2,1)S(1)}, bf16[144,128]{1,0:T(8,128)(2,1)S(1)}, u32[]{:S(2)}, u32[]{:S(2)}) collective-permute-start(bf16[144,128]{1,0:T(8,128)(2,1)S(1)} %chip_sum.1.refs_0_), channel_id=1, source_target_pairs={{0,2},{1,3},{2,0},{3,1},{4,6},{5,7},{6,4},{7,5},{8,10},{9,11},{10,... | collective-permute-start | bytes 110600 | tf_op jit(solution)/shard_map/ppermute | solution.py:463
  52.7 1.1 %collective-permute-start.14 = (bf16[144,128]{1,0:T(8,128)(2,1)S(1)}, bf16[144,128]{1,0:T(8,128)(2,1)S(1)}, u32[]{:S(2)}, u32[]{:S(2)}) collective-permute-start(bf16[144,128]{1,0:T(8,128)(2,1)S(1)} %chip_sum.1.refs_0_), channel_id=1, source_target_pairs={{0,1},{1,0},{2,3},{3,2},{4,5},{5,4},{6,7},{7,6},{8,9},{9,8},{10,11... | collective-permute-start | bytes 110600 | tf_op jit(solution)/shard_map/ppermute | solution.py:463
  53.9 1.4 %collective-permute-done.16.refs_3_ = bf16[144,128]{1,0:T(8,128)(2,1)S(1)} collective-permute-done((bf16[144,128]{1,0:T(8,128)(2,1)S(1)}, bf16[144,128]{1,0:T(8,128)(2,1)S(1)}, u32[]{:S(2)}, u32[]{:S(2)}) %collective-permute-start.16) | collective-permute-done | bytes 36896 | tf_op jit(solution)/shard_map/ppermute | solution.py:463
  55.7 1.0 %collective-permute-done.14.refs_1_ = bf16[144,128]{1,0:T(8,128)(2,1)S(1)} collective-permute-done((bf16[144,128]{1,0:T(8,128)(2,1)S(1)}, bf16[144,128]{1,0:T(8,128)(2,1)S(1)}, u32[]{:S(2)}, u32[]{:S(2)}) %collective-permute-start.14) | collective-permute-done | bytes 36896 | tf_op jit(solution)/shard_map/ppermute | solution.py:463
  56.7 1.0 %norm_back.1 = f32[576,128]{1,0:T(8,128)} custom-call(bf16[576,128]{1,0:T(8,128)(2,1)S(1)} %bitcast.5, bf16[512]{0:T(512)(128)(2,1)S(1)} %copy-done.10, bf16[144,128]{1,0:T(8,128)(2,1)S(1)} %chip_sum.1.refs_0_, bf16[144,128]{1,0:T(8,128)(2,1)S(1)} %collective-permute-done.14.refs_1_, bf16[144,128]{1,0:T(8,128)(2,1)S(1)} %collective-permute-done.15.refs_2_, ...), custom_call_target="tpu_custom_call" | custom-call | tf_op jit(solution)/shard_map/norm_back/pallas_call | solution.py:617
  (45 shorter events, 7.6 us)
Async XLA Ops:
  0.6 11.1 %copy-start.10 = (bf16[512]{0:T(512)(128)(2,1)S(1)}, bf16[512]{0:T(512)(128)(2,1)}, u32[]{:S(2)}) copy-start(bf16[512]{0:T(512)(128)(2,1)} %gain_ref.5) | copy-start | bytes 3076
  1.8 13.7 %copy-start = (bf16[16,128,512]{2,1,0:T(8,128)(2,1)S(1)}, bf16[16,128,512]{2,1,0:T(8,128)(2,1)}, u32[]{:S(2)}) copy-start(bf16[16,128,512]{2,1,0:T(8,128)(2,1)} %w_uk_ref.3) | copy-start | bytes 6291460
  1.8 13.7 %copy-start.1 = (bf16[16,512,128]{2,1,0:T(8,128)(2,1)S(1)}, bf16[16,512,128]{2,1,0:T(8,128)(2,1)}, u32[]{:S(2)}) copy-start(bf16[16,512,128]{2,1,0:T(8,128)(2,1)} %w_uv_ref.1) | copy-start | bytes 6291460
  1.8 7.7 %collective-permute-start.2 = (bf16[144,128]{1,0:T(8,128)(2,1)S(1)}, bf16[144,128]{1,0:T(8,128)(2,1)S(1)}, u32[]{:S(2)}, u32[]{:S(2)}) collective-permute-start(bf16[144,128]{1,0:T(8,128)(2,1)S(1)} %piece.1), channel_id=1, source_target_pairs={{0,24},{4,28},{8,16},{12,20},{16,8},{20,12},{24,0},{28,4},{1,25},{... | collective-permute-start | bytes 110600 | tf_op jit(solution)/shard_map/ppermute | solution.py:460
  6.9 4.9 %collective-permute-start.1 = (bf16[144,128]{1,0:T(8,128)(2,1)S(1)}, bf16[144,128]{1,0:T(8,128)(2,1)S(1)}, u32[]{:S(2)}, u32[]{:S(2)}) collective-permute-start(bf16[144,128]{1,0:T(8,128)(2,1)S(1)} %piece.1), channel_id=1, source_target_pairs={{0,16},{4,20},{8,24},{12,28},{16,0},{20,4},{24,8},{28,12},{1,17},{... | collective-permute-start | bytes 110600 | tf_op jit(solution)/shard_map/ppermute | solution.py:460
  6.9 4.9 %collective-permute-start = (bf16[144,128]{1,0:T(8,128)(2,1)S(1)}, bf16[144,128]{1,0:T(8,128)(2,1)S(1)}, u32[]{:S(2)}, u32[]{:S(2)}) collective-permute-start(bf16[144,128]{1,0:T(8,128)(2,1)S(1)} %piece.1), channel_id=1, source_target_pairs={{0,8},{4,12},{8,0},{12,4},{16,24},{20,28},{24,16},{28,20},{1,9},{5... | collective-permute-start | bytes 110600 | tf_op jit(solution)/shard_map/ppermute | solution.py:460
  9.1 6.4 %copy-start.6 = (bf16[128,2048]{1,0:T(8,128)(2,1)S(1)}, bf16[128,2048]{1,0:T(8,128)(2,1)}, u32[]{:S(2)}) copy-start(bf16[128,2048]{1,0:T(8,128)(2,1)} %out_ref.1) | copy-start | bytes 1572868
  9.1 6.4 %copy-start.7 = (bf16[128,1024]{1,0:T(8,128)(2,1)S(1)}, bf16[128,1024]{1,0:T(8,128)(2,1)}, u32[]{:S(2)}) copy-start(bf16[128,1024]{1,0:T(8,128)(2,1)} %rope_ref.1) | copy-start | bytes 786436
  11.9 7.9 %copy-start.8 = (s32[8,2]{0,1:T(2,128)S(1)}, s32[8,2]{0,1:T(2,128)}, u32[]{:S(2)}) copy-start(s32[8,2]{0,1:T(2,128)} %param.17) | copy-start | bytes 196
  11.9 6.9 %collective-permute-start.5 = (bf16[432,128]{1,0:T(8,128)(2,1)S(1)}, bf16[432,128]{1,0:T(8,128)(2,1)S(1)}, u32[]{:S(2)}, u32[]{:S(2)}) collective-permute-start(bf16[432,128]{1,0:T(8,128)(2,1)S(1)} %join_chips.1.unused_ref.refs_1_), channel_id=1, source_target_pairs={{0,3},{1,2},{2,1},{3,0},{4,7},{5,6},{6,5},{7,4},{8,11},{9,10},{10,... | collective-permute-start | bytes 331784 | tf_op jit(solution)/shard_map/ppermute | solution.py:463
  14.4 5.2 %collective-permute-start.4 = (bf16[432,128]{1,0:T(8,128)(2,1)S(1)}, bf16[432,128]{1,0:T(8,128)(2,1)S(1)}, u32[]{:S(2)}, u32[]{:S(2)}) collective-permute-start(bf16[432,128]{1,0:T(8,128)(2,1)S(1)} %join_chips.1.unused_ref.refs_1_), channel_id=1, source_target_pairs={{0,2},{1,3},{2,0},{3,1},{4,6},{5,7},{6,4},{7,5},{8,10},{9,11},{10,... | collective-permute-start | bytes 331784 | tf_op jit(solution)/shard_map/ppermute | solution.py:463
  14.9 4.7 %collective-permute-start.3 = (bf16[432,128]{1,0:T(8,128)(2,1)S(1)}, bf16[432,128]{1,0:T(8,128)(2,1)S(1)}, u32[]{:S(2)}, u32[]{:S(2)}) collective-permute-start(bf16[432,128]{1,0:T(8,128)(2,1)S(1)} %join_chips.1.unused_ref.refs_1_), channel_id=1, source_target_pairs={{0,1},{1,0},{2,3},{3,2},{4,5},{5,4},{6,7},{7,6},{8,9},{9,8},{10,11... | collective-permute-start | bytes 331784 | tf_op jit(solution)/shard_map/ppermute | solution.py:463
  19.7 2.1 %collective-permute-start.6 = (bf16[2304,128]{1,0:T(8,128)(2,1)S(1)}, bf16[2304,128]{1,0:T(8,128)(2,1)S(1)}, u32[]{:S(2)}, u32[]{:S(2)}) collective-permute-start(bf16[2304,128]{1,0:T(8,128)(2,1)S(1)} %join_heads.1.source), channel_id=1, source_target_pairs={{0,4},{4,0},{8,12},{12,8},{16,20},{20,16},{24,28},{28,24},{1,5},{5... | collective-permute-start | bytes 1769480 | tf_op jit(solution)/shard_map/ppermute | solution.py:457
  31.0 2.1 %collective-permute-start.7 = (bf16[2304,128]{1,0:T(8,128)(2,1)S(1)}, bf16[2304,128]{1,0:T(8,128)(2,1)S(1)}, u32[]{:S(2)}, u32[]{:S(2)}) collective-permute-start(bf16[2304,128]{1,0:T(8,128)(2,1)S(1)} %get-tuple-element.59), channel_id=1, source_target_pairs={{0,4},{4,0},{8,12},{12,8},{16,20},{20,16},{24,28},{28,24},{1,5},{5... | collective-permute-start | bytes 1769480 | tf_op jit(solution)/shard_map/ppermute | solution.py:457
  33.2 8.3 %collective-permute-start.8 = (bf16[576,128]{1,0:T(8,128)(2,1)S(1)}, bf16[576,128]{1,0:T(8,128)(2,1)S(1)}, u32[]{:S(2)}, u32[]{:S(2)}) collective-permute-start(bf16[576,128]{1,0:T(8,128)(2,1)S(1)} %get-tuple-element.66), channel_id=1, source_target_pairs={{0,3},{1,2},{2,1},{3,0},{4,7},{5,6},{6,5},{7,4},{8,11},{9,10},{10,... | collective-permute-start | bytes 442376 | tf_op jit(solution)/shard_map/ppermute | solution.py:463
  34.7 8.5 %collective-permute-start.9 = (bf16[576,128]{1,0:T(8,128)(2,1)S(1)}, bf16[576,128]{1,0:T(8,128)(2,1)S(1)}, u32[]{:S(2)}, u32[]{:S(2)}) collective-permute-start(bf16[576,128]{1,0:T(8,128)(2,1)S(1)} %get-tuple-element.67), channel_id=1, source_target_pairs={{0,2},{1,3},{2,0},{3,1},{4,6},{5,7},{6,4},{7,5},{8,10},{9,11},{10,... | collective-permute-start | bytes 442376 | tf_op jit(solution)/shard_map/ppermute | solution.py:463
  35.4 7.8 %collective-permute-start.10 = (bf16[576,128]{1,0:T(8,128)(2,1)S(1)}, bf16[576,128]{1,0:T(8,128)(2,1)S(1)}, u32[]{:S(2)}, u32[]{:S(2)}) collective-permute-start(bf16[576,128]{1,0:T(8,128)(2,1)S(1)} %get-tuple-element.68), channel_id=1, source_target_pairs={{0,1},{1,0},{2,3},{3,2},{4,5},{5,4},{6,7},{7,6},{8,9},{9,8},{10,11... | collective-permute-start | bytes 442376 | tf_op jit(solution)/shard_map/ppermute | solution.py:463
  36.7 20.0 %copy-start.3 = (bf16[128,576]{0,1:T(8,128)(2,1)S(1)}, bf16[128,576]{0,1:T(8,128)(2,1)}, u32[]{:S(2)}) copy-start(bf16[128,576]{0,1:T(8,128)(2,1)} %param.11) | copy-start | bytes 442372
  43.4 6.2 %collective-permute-start.11 = (bf16[144,128]{1,0:T(8,128)(2,1)S(1)}, bf16[144,128]{1,0:T(8,128)(2,1)S(1)}, u32[]{:S(2)}, u32[]{:S(2)}) collective-permute-start(bf16[144,128]{1,0:T(8,128)(2,1)S(1)} %get-tuple-element.80), channel_id=1, source_target_pairs={{0,24},{4,28},{8,16},{12,20},{16,8},{20,12},{24,0},{28,4},{1,25},{... | collective-permute-start | bytes 110600 | tf_op jit(solution)/shard_map/ppermute | solution.py:460
  44.9 5.0 %collective-permute-start.12 = (bf16[144,128]{1,0:T(8,128)(2,1)S(1)}, bf16[144,128]{1,0:T(8,128)(2,1)S(1)}, u32[]{:S(2)}, u32[]{:S(2)}) collective-permute-start(bf16[144,128]{1,0:T(8,128)(2,1)S(1)} %get-tuple-element.81), channel_id=1, source_target_pairs={{0,16},{4,20},{8,24},{12,28},{16,0},{20,4},{24,8},{28,12},{1,17},{... | collective-permute-start | bytes 110600 | tf_op jit(solution)/shard_map/ppermute | solution.py:460
  45.6 4.7 %collective-permute-start.13 = (bf16[144,128]{1,0:T(8,128)(2,1)S(1)}, bf16[144,128]{1,0:T(8,128)(2,1)S(1)}, u32[]{:S(2)}, u32[]{:S(2)}) collective-permute-start(bf16[144,128]{1,0:T(8,128)(2,1)S(1)} %get-tuple-element.82), channel_id=1, source_target_pairs={{0,8},{4,12},{8,0},{12,4},{16,24},{20,28},{24,16},{28,20},{1,9},{5... | collective-permute-start | bytes 110600 | tf_op jit(solution)/shard_map/ppermute | solution.py:460
  50.3 4.9 %collective-permute-start.16 = (bf16[144,128]{1,0:T(8,128)(2,1)S(1)}, bf16[144,128]{1,0:T(8,128)(2,1)S(1)}, u32[]{:S(2)}, u32[]{:S(2)}) collective-permute-start(bf16[144,128]{1,0:T(8,128)(2,1)S(1)} %chip_sum.1.refs_0_), channel_id=1, source_target_pairs={{0,3},{1,2},{2,1},{3,0},{4,7},{5,6},{6,5},{7,4},{8,11},{9,10},{10,... | collective-permute-start | bytes 110600 | tf_op jit(solution)/shard_map/ppermute | solution.py:463
  51.8 4.0 %collective-permute-start.15 = (bf16[144,128]{1,0:T(8,128)(2,1)S(1)}, bf16[144,128]{1,0:T(8,128)(2,1)S(1)}, u32[]{:S(2)}, u32[]{:S(2)}) collective-permute-start(bf16[144,128]{1,0:T(8,128)(2,1)S(1)} %chip_sum.1.refs_0_), channel_id=1, source_target_pairs={{0,2},{1,3},{2,0},{3,1},{4,6},{5,7},{6,4},{7,5},{8,10},{9,11},{10,... | collective-permute-start | bytes 110600 | tf_op jit(solution)/shard_map/ppermute | solution.py:463
  52.7 4.0 %collective-permute-start.14 = (bf16[144,128]{1,0:T(8,128)(2,1)S(1)}, bf16[144,128]{1,0:T(8,128)(2,1)S(1)}, u32[]{:S(2)}, u32[]{:S(2)}) collective-permute-start(bf16[144,128]{1,0:T(8,128)(2,1)S(1)} %chip_sum.1.refs_0_), channel_id=1, source_target_pairs={{0,1},{1,0},{2,3},{3,2},{4,5},{5,4},{6,7},{7,6},{8,9},{9,8},{10,11... | collective-permute-start | bytes 110600 | tf_op jit(solution)/shard_map/ppermute | solution.py:463
  (4 other events, 14.3 us)

commit v5 on v4

--- a/solution.py
+++ b/solution.py
@@ -18,7 +18,7 @@
 project_mib = 12
 window_flops = 8 * 10**9
 delta_rows = 16
-row_chunk = 256
+row_chunk = 512
 f32 = jnp.float32
 bf16 = jnp.bfloat16
 in_vmem = pl.BlockSpec(memory_space=pltpu.VMEM)

time: 57.9 us -> 57.9 us (level)
  no operation moved by 1% of the time
where the time goes in v5:
time: 57.9 us; the launch traced here: 57.8 us
  starting transfers between devices  21.1 us (36%)
  Pallas kernels  20.1 us (35%)
  waiting for transfers between devices  14.1 us (24%)
  local copies, waits for them, and re-layouts  1.63 us (3%)
  between operations  0.78 us (1%)
    ppermute x9, starting transfers between devices, to_head(): return lax.ppermute(rows, 'head', [(j, j ^ m) for j in range(head_count)])  10.7 us
    ppermute x6, starting transfers between devices, to_chip(): return lax.ppermute(rows, 'ctx', [(i, i ^ 2 * k) for i in range(ctx_count)])  10.2 us
    pallas_call x1, Pallas kernels, local(): pl.pallas_call(functools.partial(attend_kernel, head_count), out_shape=(s...  9.17 us
    ppermute x9, waiting for transfers between devices, to_head(): return lax.ppermute(rows, 'head', [(j, j ^ m) for j in range(head_count)])  6.98 us
    pallas_call x1, Pallas kernels, local(): pl.pallas_call(functools.partial(query_kernel, scale), out_shape=(shape(q...  4.74 us
    ppermute x6, waiting for transfers between devices, to_chip(): return lax.ppermute(rows, 'ctx', [(i, i ^ 2 * k) for i in range(ctx_count)])  4.73 us
    ppermute x2, waiting for transfers between devices, to_core(): return lax.ppermute(rows, 'ctx', [(i, i ^ 1) for i in range(ctx_count)])  2.41 us
    pallas_call x1, Pallas kernels, local(): pl.pallas_call(functools.partial(project_kernel, scale * log2_e), out_sha...  1.89 us
  transfers between devices with their start and end apart: 17, of which 14 were waited for; matrix products, arithmetic and copies ran while one was open for 0% of the time, Pallas kernels for 14%

profile of v5, /device:TPU:0, one launch (start us, length us, event | category | flops | bytes accessed | tf_op | source)
XLA Modules:
  0.0 57.8 jit_solution(16314907237581880687)
XLA Ops:
  0.6 1.1 %piece.1 = bf16[144,128]{1,0:T(8,128)(2,1)S(1)} custom-call(bf16[576,128]{1,0:T(8,128)(2,1)} %bitcast.3), custom_call_target="tpu_custom_call" | custom-call | tf_op jit(solution)/shard_map/piece/pallas_call | solution.py:466
  1.8 5.1 %collective-permute-start.2 = (bf16[144,128]{1,0:T(8,128)(2,1)S(1)}, bf16[144,128]{1,0:T(8,128)(2,1)S(1)}, u32[]{:S(2)}, u32[]{:S(2)}) collective-permute-start(bf16[144,128]{1,0:T(8,128)(2,1)S(1)} %piece.1), channel_id=1, source_target_pairs={{0,24},{4,28},{8,16},{12,20},{16,8},{20,12},{24,0},{28,4},{1,25},{... | collective-permute-start | bytes 110600 | tf_op jit(solution)/shard_map/ppermute | solution.py:460
  7.5 0.9 %copy-done.2 = bf16[128,576]{0,1:T(8,128)(2,1)S(1)} copy-done((bf16[128,576]{0,1:T(8,128)(2,1)S(1)}, bf16[128,576]{0,1:T(8,128)(2,1)}, u32[]{:S(2)}) %copy-start.2) | copy-done | bytes 147480
  9.4 2.3 %collective-permute-done.1.refs_1_ = bf16[144,128]{1,0:T(8,128)(2,1)S(1)} collective-permute-done((bf16[144,128]{1,0:T(8,128)(2,1)S(1)}, bf16[144,128]{1,0:T(8,128)(2,1)S(1)}, u32[]{:S(2)}, u32[]{:S(2)}) %collective-permute-start.1) | collective-permute-done | bytes 36896 | tf_op jit(solution)/shard_map/ppermute | solution.py:460
  11.9 2.5 %collective-permute-start.5 = (bf16[432,128]{1,0:T(8,128)(2,1)S(1)}, bf16[432,128]{1,0:T(8,128)(2,1)S(1)}, u32[]{:S(2)}, u32[]{:S(2)}) collective-permute-start(bf16[432,128]{1,0:T(8,128)(2,1)S(1)} %join_chips.1.unused_ref.refs_1_), channel_id=1, source_target_pairs={{0,3},{1,2},{2,1},{3,0},{4,7},{5,6},{6,5},{7,4},{8,11},{9,10},{10,... | collective-permute-start | bytes 331784 | tf_op jit(solution)/shard_map/ppermute | solution.py:463
  15.5 1.9 %project.1 = (bf16[2,1024,576]{2,1,0:T(8,128)(2,1)S(1)}, bf16[2,1040,512]{2,1,0:T(8,128)(2,1)S(1)}) custom-call(bf16[128,2048]{1,0:T(8,128)(2,1)S(1)} %copy-done.4, bf16[128,1024]{1,0:T(8,128)(2,1)S(1)} %copy-done.7, bf16[16,128,512]{2,1,0:T(8,128)(2,1)S(1)} %copy-done, bf16[128,2048]{1,0:T(8,128)(2,1)S(1)} %copy-done.5, bf16[128,2048]{1,0:T(8,128)(2,1)S(1)} %copy-done.6, ...), custom_call_target="tpu_custom_call" | custom-call | flops 536870912 | bytes 12582912 | tf_op jit(solution)/shard_map/project/pallas_call | solution.py:509
  17.4 1.4 %collective-permute-done.5.refs_4_ = bf16[432,128]{1,0:T(8,128)(2,1)S(1)} collective-permute-done((bf16[432,128]{1,0:T(8,128)(2,1)S(1)}, bf16[432,128]{1,0:T(8,128)(2,1)S(1)}, u32[]{:S(2)}, u32[]{:S(2)}) %collective-permute-start.5) | collective-permute-done | bytes 110624 | tf_op jit(solution)/shard_map/ppermute | solution.py:463
  18.8 0.8 %collective-permute-done.4.refs_3_ = bf16[432,128]{1,0:T(8,128)(2,1)S(1)} collective-permute-done((bf16[432,128]{1,0:T(8,128)(2,1)S(1)}, bf16[432,128]{1,0:T(8,128)(2,1)S(1)}, u32[]{:S(2)}, u32[]{:S(2)}) %collective-permute-start.4) | collective-permute-done | bytes 110624 | tf_op jit(solution)/shard_map/ppermute | solution.py:463
  20.5 1.3 %collective-permute-done.6.refs_1_ = bf16[2304,128]{1,0:T(8,128)(2,1)S(1)} collective-permute-done((bf16[2304,128]{1,0:T(8,128)(2,1)S(1)}, bf16[2304,128]{1,0:T(8,128)(2,1)S(1)}, u32[]{:S(2)}, u32[]{:S(2)}) %collective-permute-start.6) | collective-permute-done | bytes 589856 | tf_op jit(solution)/shard_map/ppermute | solution.py:457
  21.8 9.2 %attend.1 = (bf16[1024,576]{1,0:T(8,128)(2,1)S(1)}, bf16[1280,1024]{1,0:T(8,128)(2,1)S(1)}, bf16[2304,128]{1,0:T(8,128)(2,1)S(1)}, f32[1024,576]{1,0:T(8,128)S(1)}, f32[1024,512]{1,0:T(8,128)S(1)}) custom-call(s32[2,8]{1,0:T(2,128)S(1)} %bitcast.7, bf16[2304,128]{1,0:T(8,128)(2,1)S(1)} %collective-permute-done.6.refs_1_, ...), custom_call_target="tpu_custom_call", output_to_operand_aliasing={{0}: (2, {})} | custom-call | flops 5704253440 | bytes 12582912 | tf_op jit(solution)/shard_map/attend/pallas_call | solution.py:539
  31.9 1.1 %collective-permute-done.7.recv_ref = bf16[2304,128]{1,0:T(8,128)(2,1)S(1)} collective-permute-done((bf16[2304,128]{1,0:T(8,128)(2,1)S(1)}, bf16[2304,128]{1,0:T(8,128)(2,1)S(1)}, u32[]{:S(2)}, u32[]{:S(2)}) %collective-permute-start.7) | collective-permute-done | bytes 589856 | tf_op jit(solution)/shard_map/ppermute | solution.py:457
  33.2 1.6 %collective-permute-start.8 = (bf16[576,128]{1,0:T(8,128)(2,1)S(1)}, bf16[576,128]{1,0:T(8,128)(2,1)S(1)}, u32[]{:S(2)}, u32[]{:S(2)}) collective-permute-start(bf16[576,128]{1,0:T(8,128)(2,1)S(1)} %get-tuple-element.66), channel_id=1, source_target_pairs={{0,3},{1,2},{2,1},{3,0},{4,7},{5,6},{6,5},{7,4},{8,11},{9,10},{10,... | collective-permute-start | bytes 442376 | tf_op jit(solution)/shard_map/ppermute | solution.py:463
  35.5 1.3 %collective-permute-start.10 = (bf16[576,128]{1,0:T(8,128)(2,1)S(1)}, bf16[576,128]{1,0:T(8,128)(2,1)S(1)}, u32[]{:S(2)}, u32[]{:S(2)}) collective-permute-start(bf16[576,128]{1,0:T(8,128)(2,1)S(1)} %get-tuple-element.68), channel_id=1, source_target_pairs={{0,1},{1,0},{2,3},{3,2},{4,5},{5,4},{6,7},{7,6},{8,9},{9,8},{10,11... | collective-permute-start | bytes 442376 | tf_op jit(solution)/shard_map/ppermute | solution.py:463
  36.7 4.7 %query_grads.1 = (bf16[128,2048]{1,0:T(8,128)(2,1)}, bf16[128,1024]{1,0:T(8,128)(2,1)}) custom-call(s32[2,8]{1,0:T(2,128)S(1)} %bitcast.9, bf16[1024,576]{1,0:T(8,128)(2,1)S(1)} %get-tuple-element.69.keys_ref, bf16[1280,1024]{1,0:T(8,128)(2,1)S(1)} %get-tuple-element.70.ds_ref, bf16[16,128,512]{2,1,0:T(8,128)(2,1)S(1)} %copy-done), custom_call_target="tpu_custom_call" | custom-call | flops 1509949440 | bytes 8388608 | tf_op jit(solution)/shard_map/query_grads/pallas_call | solution.py:582
  41.5 1.7 %collective-permute-done.9.refs_2_ = bf16[576,128]{1,0:T(8,128)(2,1)S(1)} collective-permute-done((bf16[576,128]{1,0:T(8,128)(2,1)S(1)}, bf16[576,128]{1,0:T(8,128)(2,1)S(1)}, u32[]{:S(2)}, u32[]{:S(2)}) %collective-permute-start.9) | collective-permute-done | bytes 147488 | tf_op jit(solution)/shard_map/ppermute | solution.py:463
  43.4 1.5 %collective-permute-start.11 = (bf16[144,128]{1,0:T(8,128)(2,1)S(1)}, bf16[144,128]{1,0:T(8,128)(2,1)S(1)}, u32[]{:S(2)}, u32[]{:S(2)}) collective-permute-start(bf16[144,128]{1,0:T(8,128)(2,1)S(1)} %get-tuple-element.80), channel_id=1, source_target_pairs={{0,24},{4,28},{8,16},{12,20},{16,8},{20,12},{24,0},{28,4},{1,25},{... | collective-permute-start | bytes 110600 | tf_op jit(solution)/shard_map/ppermute | solution.py:460
  45.6 2.3 %collective-permute-start.13 = (bf16[144,128]{1,0:T(8,128)(2,1)S(1)}, bf16[144,128]{1,0:T(8,128)(2,1)S(1)}, u32[]{:S(2)}, u32[]{:S(2)}) collective-permute-start(bf16[144,128]{1,0:T(8,128)(2,1)S(1)} %get-tuple-element.82), channel_id=1, source_target_pairs={{0,8},{4,12},{8,0},{12,4},{16,24},{20,28},{24,16},{28,20},{1,9},{5... | collective-permute-start | bytes 110600 | tf_op jit(solution)/shard_map/ppermute | solution.py:460
  47.9 1.7 %collective-permute-done.11.refs_1_ = bf16[144,128]{1,0:T(8,128)(2,1)S(1)} collective-permute-done((bf16[144,128]{1,0:T(8,128)(2,1)S(1)}, bf16[144,128]{1,0:T(8,128)(2,1)S(1)}, u32[]{:S(2)}, u32[]{:S(2)}) %collective-permute-start.11) | collective-permute-done | bytes 36896 | tf_op jit(solution)/shard_map/ppermute | solution.py:460
  50.3 1.5 %collective-permute-start.16 = (bf16[144,128]{1,0:T(8,128)(2,1)S(1)}, bf16[144,128]{1,0:T(8,128)(2,1)S(1)}, u32[]{:S(2)}, u32[]{:S(2)}) collective-permute-start(bf16[144,128]{1,0:T(8,128)(2,1)S(1)} %chip_sum.1.refs_0_), channel_id=1, source_target_pairs={{0,3},{1,2},{2,1},{3,0},{4,7},{5,6},{6,5},{7,4},{8,11},{9,10},{10,... | collective-permute-start | bytes 110600 | tf_op jit(solution)/shard_map/ppermute | solution.py:463
  51.8 1.0 %collective-permute-start.15 = (bf16[144,128]{1,0:T(8,128)(2,1)S(1)}, bf16[144,128]{1,0:T(8,128)(2,1)S(1)}, u32[]{:S(2)}, u32[]{:S(2)}) collective-permute-start(bf16[144,128]{1,0:T(8,128)(2,1)S(1)} %chip_sum.1.refs_0_), channel_id=1, source_target_pairs={{0,2},{1,3},{2,0},{3,1},{4,6},{5,7},{6,4},{7,5},{8,10},{9,11},{10,... | collective-permute-start | bytes 110600 | tf_op jit(solution)/shard_map/ppermute | solution.py:463
  52.8 1.1 %collective-permute-start.14 = (bf16[144,128]{1,0:T(8,128)(2,1)S(1)}, bf16[144,128]{1,0:T(8,128)(2,1)S(1)}, u32[]{:S(2)}, u32[]{:S(2)}) collective-permute-start(bf16[144,128]{1,0:T(8,128)(2,1)S(1)} %chip_sum.1.refs_0_), channel_id=1, source_target_pairs={{0,1},{1,0},{2,3},{3,2},{4,5},{5,4},{6,7},{7,6},{8,9},{9,8},{10,11... | collective-permute-start | bytes 110600 | tf_op jit(solution)/shard_map/ppermute | solution.py:463
  53.9 1.4 %collective-permute-done.16.refs_3_ = bf16[144,128]{1,0:T(8,128)(2,1)S(1)} collective-permute-done((bf16[144,128]{1,0:T(8,128)(2,1)S(1)}, bf16[144,128]{1,0:T(8,128)(2,1)S(1)}, u32[]{:S(2)}, u32[]{:S(2)}) %collective-permute-start.16) | collective-permute-done | bytes 36896 | tf_op jit(solution)/shard_map/ppermute | solution.py:463
  55.8 1.0 %collective-permute-done.14.refs_1_ = bf16[144,128]{1,0:T(8,128)(2,1)S(1)} collective-permute-done((bf16[144,128]{1,0:T(8,128)(2,1)S(1)}, bf16[144,128]{1,0:T(8,128)(2,1)S(1)}, u32[]{:S(2)}, u32[]{:S(2)}) %collective-permute-start.14) | collective-permute-done | bytes 36896 | tf_op jit(solution)/shard_map/ppermute | solution.py:463
  56.7 1.0 %norm_back.1 = f32[576,128]{1,0:T(8,128)} custom-call(bf16[576,128]{1,0:T(8,128)(2,1)S(1)} %bitcast.5, bf16[512]{0:T(512)(128)(2,1)S(1)} %copy-done.10, bf16[144,128]{1,0:T(8,128)(2,1)S(1)} %chip_sum.1.refs_0_, bf16[144,128]{1,0:T(8,128)(2,1)S(1)} %collective-permute-done.14.refs_1_, bf16[144,128]{1,0:T(8,128)(2,1)S(1)} %collective-permute-done.15.refs_2_, ...), custom_call_target="tpu_custom_call" | custom-call | tf_op jit(solution)/shard_map/norm_back/pallas_call | solution.py:617
  (45 shorter events, 7.6 us)
Async XLA Ops:
  0.6 11.1 %copy-start.10 = (bf16[512]{0:T(512)(128)(2,1)S(1)}, bf16[512]{0:T(512)(128)(2,1)}, u32[]{:S(2)}) copy-start(bf16[512]{0:T(512)(128)(2,1)} %gain_ref.5) | copy-start | bytes 3076
  1.8 13.7 %copy-start = (bf16[16,128,512]{2,1,0:T(8,128)(2,1)S(1)}, bf16[16,128,512]{2,1,0:T(8,128)(2,1)}, u32[]{:S(2)}) copy-start(bf16[16,128,512]{2,1,0:T(8,128)(2,1)} %w_uk_ref.3) | copy-start | bytes 6291460
  1.8 13.7 %copy-start.1 = (bf16[16,512,128]{2,1,0:T(8,128)(2,1)S(1)}, bf16[16,512,128]{2,1,0:T(8,128)(2,1)}, u32[]{:S(2)}) copy-start(bf16[16,512,128]{2,1,0:T(8,128)(2,1)} %w_uv_ref.1) | copy-start | bytes 6291460
  1.8 7.7 %collective-permute-start.2 = (bf16[144,128]{1,0:T(8,128)(2,1)S(1)}, bf16[144,128]{1,0:T(8,128)(2,1)S(1)}, u32[]{:S(2)}, u32[]{:S(2)}) collective-permute-start(bf16[144,128]{1,0:T(8,128)(2,1)S(1)} %piece.1), channel_id=1, source_target_pairs={{0,24},{4,28},{8,16},{12,20},{16,8},{20,12},{24,0},{28,4},{1,25},{... | collective-permute-start | bytes 110600 | tf_op jit(solution)/shard_map/ppermute | solution.py:460
  6.9 4.9 %collective-permute-start.1 = (bf16[144,128]{1,0:T(8,128)(2,1)S(1)}, bf16[144,128]{1,0:T(8,128)(2,1)S(1)}, u32[]{:S(2)}, u32[]{:S(2)}) collective-permute-start(bf16[144,128]{1,0:T(8,128)(2,1)S(1)} %piece.1), channel_id=1, source_target_pairs={{0,16},{4,20},{8,24},{12,28},{16,0},{20,4},{24,8},{28,12},{1,17},{... | collective-permute-start | bytes 110600 | tf_op jit(solution)/shard_map/ppermute | solution.py:460
  6.9 4.9 %collective-permute-start = (bf16[144,128]{1,0:T(8,128)(2,1)S(1)}, bf16[144,128]{1,0:T(8,128)(2,1)S(1)}, u32[]{:S(2)}, u32[]{:S(2)}) collective-permute-start(bf16[144,128]{1,0:T(8,128)(2,1)S(1)} %piece.1), channel_id=1, source_target_pairs={{0,8},{4,12},{8,0},{12,4},{16,24},{20,28},{24,16},{28,20},{1,9},{5... | collective-permute-start | bytes 110600 | tf_op jit(solution)/shard_map/ppermute | solution.py:460
  9.1 6.4 %copy-start.6 = (bf16[128,2048]{1,0:T(8,128)(2,1)S(1)}, bf16[128,2048]{1,0:T(8,128)(2,1)}, u32[]{:S(2)}) copy-start(bf16[128,2048]{1,0:T(8,128)(2,1)} %out_ref.1) | copy-start | bytes 1572868
  9.1 6.4 %copy-start.7 = (bf16[128,1024]{1,0:T(8,128)(2,1)S(1)}, bf16[128,1024]{1,0:T(8,128)(2,1)}, u32[]{:S(2)}) copy-start(bf16[128,1024]{1,0:T(8,128)(2,1)} %rope_ref.1) | copy-start | bytes 786436
  11.9 7.9 %copy-start.8 = (s32[8,2]{0,1:T(2,128)S(1)}, s32[8,2]{0,1:T(2,128)}, u32[]{:S(2)}) copy-start(s32[8,2]{0,1:T(2,128)} %param.17) | copy-start | bytes 196
  11.9 6.9 %collective-permute-start.5 = (bf16[432,128]{1,0:T(8,128)(2,1)S(1)}, bf16[432,128]{1,0:T(8,128)(2,1)S(1)}, u32[]{:S(2)}, u32[]{:S(2)}) collective-permute-start(bf16[432,128]{1,0:T(8,128)(2,1)S(1)} %join_chips.1.unused_ref.refs_1_), channel_id=1, source_target_pairs={{0,3},{1,2},{2,1},{3,0},{4,7},{5,6},{6,5},{7,4},{8,11},{9,10},{10,... | collective-permute-start | bytes 331784 | tf_op jit(solution)/shard_map/ppermute | solution.py:463
  14.4 5.2 %collective-permute-start.4 = (bf16[432,128]{1,0:T(8,128)(2,1)S(1)}, bf16[432,128]{1,0:T(8,128)(2,1)S(1)}, u32[]{:S(2)}, u32[]{:S(2)}) collective-permute-start(bf16[432,128]{1,0:T(8,128)(2,1)S(1)} %join_chips.1.unused_ref.refs_1_), channel_id=1, source_target_pairs={{0,2},{1,3},{2,0},{3,1},{4,6},{5,7},{6,4},{7,5},{8,10},{9,11},{10,... | collective-permute-start | bytes 331784 | tf_op jit(solution)/shard_map/ppermute | solution.py:463
  14.9 4.7 %collective-permute-start.3 = (bf16[432,128]{1,0:T(8,128)(2,1)S(1)}, bf16[432,128]{1,0:T(8,128)(2,1)S(1)}, u32[]{:S(2)}, u32[]{:S(2)}) collective-permute-start(bf16[432,128]{1,0:T(8,128)(2,1)S(1)} %join_chips.1.unused_ref.refs_1_), channel_id=1, source_target_pairs={{0,1},{1,0},{2,3},{3,2},{4,5},{5,4},{6,7},{7,6},{8,9},{9,8},{10,11... | collective-permute-start | bytes 331784 | tf_op jit(solution)/shard_map/ppermute | solution.py:463
  19.7 2.1 %collective-permute-start.6 = (bf16[2304,128]{1,0:T(8,128)(2,1)S(1)}, bf16[2304,128]{1,0:T(8,128)(2,1)S(1)}, u32[]{:S(2)}, u32[]{:S(2)}) collective-permute-start(bf16[2304,128]{1,0:T(8,128)(2,1)S(1)} %join_heads.1.source), channel_id=1, source_target_pairs={{0,4},{4,0},{8,12},{12,8},{16,20},{20,16},{24,28},{28,24},{1,5},{5... | collective-permute-start | bytes 1769480 | tf_op jit(solution)/shard_map/ppermute | solution.py:457
  31.0 2.1 %collective-permute-start.7 = (bf16[2304,128]{1,0:T(8,128)(2,1)S(1)}, bf16[2304,128]{1,0:T(8,128)(2,1)S(1)}, u32[]{:S(2)}, u32[]{:S(2)}) collective-permute-start(bf16[2304,128]{1,0:T(8,128)(2,1)S(1)} %get-tuple-element.59), channel_id=1, source_target_pairs={{0,4},{4,0},{8,12},{12,8},{16,20},{20,16},{24,28},{28,24},{1,5},{5... | collective-permute-start | bytes 1769480 | tf_op jit(solution)/shard_map/ppermute | solution.py:457
  33.2 8.3 %collective-permute-start.8 = (bf16[576,128]{1,0:T(8,128)(2,1)S(1)}, bf16[576,128]{1,0:T(8,128)(2,1)S(1)}, u32[]{:S(2)}, u32[]{:S(2)}) collective-permute-start(bf16[576,128]{1,0:T(8,128)(2,1)S(1)} %get-tuple-element.66), channel_id=1, source_target_pairs={{0,3},{1,2},{2,1},{3,0},{4,7},{5,6},{6,5},{7,4},{8,11},{9,10},{10,... | collective-permute-start | bytes 442376 | tf_op jit(solution)/shard_map/ppermute | solution.py:463
  34.7 8.5 %collective-permute-start.9 = (bf16[576,128]{1,0:T(8,128)(2,1)S(1)}, bf16[576,128]{1,0:T(8,128)(2,1)S(1)}, u32[]{:S(2)}, u32[]{:S(2)}) collective-permute-start(bf16[576,128]{1,0:T(8,128)(2,1)S(1)} %get-tuple-element.67), channel_id=1, source_target_pairs={{0,2},{1,3},{2,0},{3,1},{4,6},{5,7},{6,4},{7,5},{8,10},{9,11},{10,... | collective-permute-start | bytes 442376 | tf_op jit(solution)/shard_map/ppermute | solution.py:463
  35.5 7.9 %collective-permute-start.10 = (bf16[576,128]{1,0:T(8,128)(2,1)S(1)}, bf16[576,128]{1,0:T(8,128)(2,1)S(1)}, u32[]{:S(2)}, u32[]{:S(2)}) collective-permute-start(bf16[576,128]{1,0:T(8,128)(2,1)S(1)} %get-tuple-element.68), channel_id=1, source_target_pairs={{0,1},{1,0},{2,3},{3,2},{4,5},{5,4},{6,7},{7,6},{8,9},{9,8},{10,11... | collective-permute-start | bytes 442376 | tf_op jit(solution)/shard_map/ppermute | solution.py:463
  36.7 20.0 %copy-start.3 = (bf16[128,576]{0,1:T(8,128)(2,1)S(1)}, bf16[128,576]{0,1:T(8,128)(2,1)}, u32[]{:S(2)}) copy-start(bf16[128,576]{0,1:T(8,128)(2,1)} %param.11) | copy-start | bytes 442372
  43.4 6.2 %collective-permute-start.11 = (bf16[144,128]{1,0:T(8,128)(2,1)S(1)}, bf16[144,128]{1,0:T(8,128)(2,1)S(1)}, u32[]{:S(2)}, u32[]{:S(2)}) collective-permute-start(bf16[144,128]{1,0:T(8,128)(2,1)S(1)} %get-tuple-element.80), channel_id=1, source_target_pairs={{0,24},{4,28},{8,16},{12,20},{16,8},{20,12},{24,0},{28,4},{1,25},{... | collective-permute-start | bytes 110600 | tf_op jit(solution)/shard_map/ppermute | solution.py:460
  45.0 5.0 %collective-permute-start.12 = (bf16[144,128]{1,0:T(8,128)(2,1)S(1)}, bf16[144,128]{1,0:T(8,128)(2,1)S(1)}, u32[]{:S(2)}, u32[]{:S(2)}) collective-permute-start(bf16[144,128]{1,0:T(8,128)(2,1)S(1)} %get-tuple-element.81), channel_id=1, source_target_pairs={{0,16},{4,20},{8,24},{12,28},{16,0},{20,4},{24,8},{28,12},{1,17},{... | collective-permute-start | bytes 110600 | tf_op jit(solution)/shard_map/ppermute | solution.py:460
  45.6 4.7 %collective-permute-start.13 = (bf16[144,128]{1,0:T(8,128)(2,1)S(1)}, bf16[144,128]{1,0:T(8,128)(2,1)S(1)}, u32[]{:S(2)}, u32[]{:S(2)}) collective-permute-start(bf16[144,128]{1,0:T(8,128)(2,1)S(1)} %get-tuple-element.82), channel_id=1, source_target_pairs={{0,8},{4,12},{8,0},{12,4},{16,24},{20,28},{24,16},{28,20},{1,9},{5... | collective-permute-start | bytes 110600 | tf_op jit(solution)/shard_map/ppermute | solution.py:460
  50.3 4.9 %collective-permute-start.16 = (bf16[144,128]{1,0:T(8,128)(2,1)S(1)}, bf16[144,128]{1,0:T(8,128)(2,1)S(1)}, u32[]{:S(2)}, u32[]{:S(2)}) collective-permute-start(bf16[144,128]{1,0:T(8,128)(2,1)S(1)} %chip_sum.1.refs_0_), channel_id=1, source_target_pairs={{0,3},{1,2},{2,1},{3,0},{4,7},{5,6},{6,5},{7,4},{8,11},{9,10},{10,... | collective-permute-start | bytes 110600 | tf_op jit(solution)/shard_map/ppermute | solution.py:463
  51.8 4.0 %collective-permute-start.15 = (bf16[144,128]{1,0:T(8,128)(2,1)S(1)}, bf16[144,128]{1,0:T(8,128)(2,1)S(1)}, u32[]{:S(2)}, u32[]{:S(2)}) collective-permute-start(bf16[144,128]{1,0:T(8,128)(2,1)S(1)} %chip_sum.1.refs_0_), channel_id=1, source_target_pairs={{0,2},{1,3},{2,0},{3,1},{4,6},{5,7},{6,4},{7,5},{8,10},{9,11},{10,... | collective-permute-start | bytes 110600 | tf_op jit(solution)/shard_map/ppermute | solution.py:463
  52.8 4.0 %collective-permute-start.14 = (bf16[144,128]{1,0:T(8,128)(2,1)S(1)}, bf16[144,128]{1,0:T(8,128)(2,1)S(1)}, u32[]{:S(2)}, u32[]{:S(2)}) collective-permute-start(bf16[144,128]{1,0:T(8,128)(2,1)S(1)} %chip_sum.1.refs_0_), channel_id=1, source_target_pairs={{0,1},{1,0},{2,3},{3,2},{4,5},{5,4},{6,7},{7,6},{8,9},{9,8},{10,11... | collective-permute-start | bytes 110600 | tf_op jit(solution)/shard_map/ppermute | solution.py:463
  (4 other events, 14.3 us)

commit v6 on v4

--- a/solution.py
+++ b/solution.py
@@ -19,6 +19,7 @@
 window_flops = 8 * 10**9
 delta_rows = 16
 row_chunk = 256
+dots_ahead = 2
 f32 = jnp.float32
 bf16 = jnp.bfloat16
 in_vmem = pl.BlockSpec(memory_space=pltpu.VMEM)
@@ -243,11 +244,11 @@
         return dot_nt(keys_ref[tile_rows(kt, counts[u]), :], q_ref[half_of(is_upper), chunk])
 
     top_parts, sum_parts = {}, {}
-    ahead = score_dot(*work[0])
+    ahead = [score_dot(*item) for item in work[:dots_ahead]]
     for i, (u, chunk) in enumerate(work):
-        scores = ahead
-        if i + 1 < len(work):
-            ahead = score_dot(*work[i + 1])
+        scores = ahead.pop(0)
+        if i + dots_ahead < len(work):
+            ahead.append(score_dot(*work[i + dots_ahead]))
         is_upper, kt = places[u]
         if groups[u][0] >= tile_count // 2:
             base = kt * key_tile - pick(is_upper, my_upper, my_lower) * span
@@ -264,7 +265,7 @@
         is_upper, kt = places[u]
         return dot_nt(keys_ref[tile_rows(kt, counts[u]), :lat_width], dl_ref[half_of(is_upper), chunk])
 
-    ahead = prob_dot(*work[0])
+    ahead = [prob_dot(*item) for item in work[:dots_ahead]]
     row_top, row_sum = [], []
     for s in range(2):
         kept = [jnp.where(half_of(is_upper) == s, top, neg_big) for (is_upper, kt), top in zip(places, tops)]
@@ -305,9 +306,9 @@
 
     pending = []
     for i, (u, chunk) in enumerate(work):
-        d_prob = ahead
-        if i + 1 < len(work):
-            ahead = prob_dot(*work[i + 1])
+        d_prob = ahead.pop(0)
+        if i + dots_ahead < len(work):
+            ahead.append(prob_dot(*work[i + dots_ahead]))
         left = len(chunks) - i % len(chunks)
         for j in range(-(-len(pending) // left)):
             pending.pop(0)()

time: 57.9 us -> 57.9 us (level)
  no operation moved by 1% of the time
where the time goes in v6:
time: 57.9 us; the launch traced here: 57.7 us
  starting transfers between devices  21.1 us (36%)
  Pallas kernels  20.1 us (35%)
  waiting for transfers between devices  14.1 us (24%)
  local copies, waits for them, and re-layouts  1.63 us (3%)
  between operations  0.78 us (1%)
    ppermute x9, starting transfers between devices, to_head(): return lax.ppermute(rows, 'head', [(j, j ^ m) for j in range(head_count)])  10.7 us
    ppermute x6, starting transfers between devices, to_chip(): return lax.ppermute(rows, 'ctx', [(i, i ^ 2 * k) for i in range(ctx_count)])  10.2 us
    pallas_call x1, Pallas kernels, local(): pl.pallas_call(functools.partial(attend_kernel, head_count), out_shape=(s...  9.17 us
    ppermute x9, waiting for transfers between devices, to_head(): return lax.ppermute(rows, 'head', [(j, j ^ m) for j in range(head_count)])  6.96 us
    ppermute x6, waiting for transfers between devices, to_chip(): return lax.ppermute(rows, 'ctx', [(i, i ^ 2 * k) for i in range(ctx_count)])  4.74 us
    pallas_call x1, Pallas kernels, local(): pl.pallas_call(functools.partial(query_kernel, scale), out_shape=(shape(q...  4.73 us
    ppermute x2, waiting for transfers between devices, to_core(): return lax.ppermute(rows, 'ctx', [(i, i ^ 1) for i in range(ctx_count)])  2.42 us
    pallas_call x1, Pallas kernels, local(): pl.pallas_call(functools.partial(project_kernel, scale * log2_e), out_sha...  1.89 us
  transfers between devices with their start and end apart: 17, of which 14 were waited for; matrix products, arithmetic and copies ran while one was open for 0% of the time, Pallas kernels for 14%

profile of v6, /device:TPU:0, one launch (start us, length us, event | category | flops | bytes accessed | tf_op | source)
XLA Modules:
  0.0 57.7 jit_solution(4731425908029535097)
XLA Ops:
  0.6 1.1 %piece.1 = bf16[144,128]{1,0:T(8,128)(2,1)S(1)} custom-call(bf16[576,128]{1,0:T(8,128)(2,1)} %bitcast.3), custom_call_target="tpu_custom_call" | custom-call | tf_op jit(solution)/shard_map/piece/pallas_call | solution.py:467
  1.8 5.1 %collective-permute-start.2 = (bf16[144,128]{1,0:T(8,128)(2,1)S(1)}, bf16[144,128]{1,0:T(8,128)(2,1)S(1)}, u32[]{:S(2)}, u32[]{:S(2)}) collective-permute-start(bf16[144,128]{1,0:T(8,128)(2,1)S(1)} %piece.1), channel_id=1, source_target_pairs={{0,24},{4,28},{8,16},{12,20},{16,8},{20,12},{24,0},{28,4},{1,25},{... | collective-permute-start | bytes 110600 | tf_op jit(solution)/shard_map/ppermute | solution.py:461
  7.5 0.9 %copy-done.2 = bf16[128,576]{0,1:T(8,128)(2,1)S(1)} copy-done((bf16[128,576]{0,1:T(8,128)(2,1)S(1)}, bf16[128,576]{0,1:T(8,128)(2,1)}, u32[]{:S(2)}) %copy-start.2) | copy-done | bytes 147480
  9.4 2.3 %collective-permute-done.1.refs_1_ = bf16[144,128]{1,0:T(8,128)(2,1)S(1)} collective-permute-done((bf16[144,128]{1,0:T(8,128)(2,1)S(1)}, bf16[144,128]{1,0:T(8,128)(2,1)S(1)}, u32[]{:S(2)}, u32[]{:S(2)}) %collective-permute-start.1) | collective-permute-done | bytes 36896 | tf_op jit(solution)/shard_map/ppermute | solution.py:461
  11.9 2.5 %collective-permute-start.5 = (bf16[432,128]{1,0:T(8,128)(2,1)S(1)}, bf16[432,128]{1,0:T(8,128)(2,1)S(1)}, u32[]{:S(2)}, u32[]{:S(2)}) collective-permute-start(bf16[432,128]{1,0:T(8,128)(2,1)S(1)} %join_chips.1.unused_ref.refs_1_), channel_id=1, source_target_pairs={{0,3},{1,2},{2,1},{3,0},{4,7},{5,6},{6,5},{7,4},{8,11},{9,10},{10,... | collective-permute-start | bytes 331784 | tf_op jit(solution)/shard_map/ppermute | solution.py:464
  15.5 1.9 %project.1 = (bf16[2,1024,576]{2,1,0:T(8,128)(2,1)S(1)}, bf16[2,1040,512]{2,1,0:T(8,128)(2,1)S(1)}) custom-call(bf16[128,2048]{1,0:T(8,128)(2,1)S(1)} %copy-done.4, bf16[128,1024]{1,0:T(8,128)(2,1)S(1)} %copy-done.7, bf16[16,128,512]{2,1,0:T(8,128)(2,1)S(1)} %copy-done, bf16[128,2048]{1,0:T(8,128)(2,1)S(1)} %copy-done.5, bf16[128,2048]{1,0:T(8,128)(2,1)S(1)} %copy-done.6, ...), custom_call_target="tpu_custom_call" | custom-call | flops 536870912 | bytes 12582912 | tf_op jit(solution)/shard_map/project/pallas_call | solution.py:510
  17.4 1.4 %collective-permute-done.5.refs_4_ = bf16[432,128]{1,0:T(8,128)(2,1)S(1)} collective-permute-done((bf16[432,128]{1,0:T(8,128)(2,1)S(1)}, bf16[432,128]{1,0:T(8,128)(2,1)S(1)}, u32[]{:S(2)}, u32[]{:S(2)}) %collective-permute-start.5) | collective-permute-done | bytes 110624 | tf_op jit(solution)/shard_map/ppermute | solution.py:464
  18.8 0.8 %collective-permute-done.4.refs_3_ = bf16[432,128]{1,0:T(8,128)(2,1)S(1)} collective-permute-done((bf16[432,128]{1,0:T(8,128)(2,1)S(1)}, bf16[432,128]{1,0:T(8,128)(2,1)S(1)}, u32[]{:S(2)}, u32[]{:S(2)}) %collective-permute-start.4) | collective-permute-done | bytes 110624 | tf_op jit(solution)/shard_map/ppermute | solution.py:464
  20.5 1.3 %collective-permute-done.6.refs_1_ = bf16[2304,128]{1,0:T(8,128)(2,1)S(1)} collective-permute-done((bf16[2304,128]{1,0:T(8,128)(2,1)S(1)}, bf16[2304,128]{1,0:T(8,128)(2,1)S(1)}, u32[]{:S(2)}, u32[]{:S(2)}) %collective-permute-start.6) | collective-permute-done | bytes 589856 | tf_op jit(solution)/shard_map/ppermute | solution.py:458
  21.8 9.2 %attend.1 = (bf16[1024,576]{1,0:T(8,128)(2,1)S(1)}, bf16[1280,1024]{1,0:T(8,128)(2,1)S(1)}, bf16[2304,128]{1,0:T(8,128)(2,1)S(1)}, f32[1024,576]{1,0:T(8,128)S(1)}, f32[1024,512]{1,0:T(8,128)S(1)}) custom-call(s32[2,8]{1,0:T(2,128)S(1)} %bitcast.7, bf16[2304,128]{1,0:T(8,128)(2,1)S(1)} %collective-permute-done.6.refs_1_, ...), custom_call_target="tpu_custom_call", output_to_operand_aliasing={{0}: (2, {})} | custom-call | flops 5704253440 | bytes 12582912 | tf_op jit(solution)/shard_map/attend/pallas_call | solution.py:540
  31.9 1.1 %collective-permute-done.7.recv_ref = bf16[2304,128]{1,0:T(8,128)(2,1)S(1)} collective-permute-done((bf16[2304,128]{1,0:T(8,128)(2,1)S(1)}, bf16[2304,128]{1,0:T(8,128)(2,1)S(1)}, u32[]{:S(2)}, u32[]{:S(2)}) %collective-permute-start.7) | collective-permute-done | bytes 589856 | tf_op jit(solution)/shard_map/ppermute | solution.py:458
  33.2 1.6 %collective-permute-start.8 = (bf16[576,128]{1,0:T(8,128)(2,1)S(1)}, bf16[576,128]{1,0:T(8,128)(2,1)S(1)}, u32[]{:S(2)}, u32[]{:S(2)}) collective-permute-start(bf16[576,128]{1,0:T(8,128)(2,1)S(1)} %get-tuple-element.66), channel_id=1, source_target_pairs={{0,3},{1,2},{2,1},{3,0},{4,7},{5,6},{6,5},{7,4},{8,11},{9,10},{10,... | collective-permute-start | bytes 442376 | tf_op jit(solution)/shard_map/ppermute | solution.py:464
  35.4 1.3 %collective-permute-start.10 = (bf16[576,128]{1,0:T(8,128)(2,1)S(1)}, bf16[576,128]{1,0:T(8,128)(2,1)S(1)}, u32[]{:S(2)}, u32[]{:S(2)}) collective-permute-start(bf16[576,128]{1,0:T(8,128)(2,1)S(1)} %get-tuple-element.68), channel_id=1, source_target_pairs={{0,1},{1,0},{2,3},{3,2},{4,5},{5,4},{6,7},{7,6},{8,9},{9,8},{10,11... | collective-permute-start | bytes 442376 | tf_op jit(solution)/shard_map/ppermute | solution.py:464
  36.7 4.7 %query_grads.1 = (bf16[128,2048]{1,0:T(8,128)(2,1)}, bf16[128,1024]{1,0:T(8,128)(2,1)}) custom-call(s32[2,8]{1,0:T(2,128)S(1)} %bitcast.9, bf16[1024,576]{1,0:T(8,128)(2,1)S(1)} %get-tuple-element.69.keys_ref, bf16[1280,1024]{1,0:T(8,128)(2,1)S(1)} %get-tuple-element.70.ds_ref, bf16[16,128,512]{2,1,0:T(8,128)(2,1)S(1)} %copy-done), custom_call_target="tpu_custom_call" | custom-call | flops 1509949440 | bytes 8388608 | tf_op jit(solution)/shard_map/query_grads/pallas_call | solution.py:583
  41.5 1.7 %collective-permute-done.9.refs_2_ = bf16[576,128]{1,0:T(8,128)(2,1)S(1)} collective-permute-done((bf16[576,128]{1,0:T(8,128)(2,1)S(1)}, bf16[576,128]{1,0:T(8,128)(2,1)S(1)}, u32[]{:S(2)}, u32[]{:S(2)}) %collective-permute-start.9) | collective-permute-done | bytes 147488 | tf_op jit(solution)/shard_map/ppermute | solution.py:464
  43.4 1.5 %collective-permute-start.11 = (bf16[144,128]{1,0:T(8,128)(2,1)S(1)}, bf16[144,128]{1,0:T(8,128)(2,1)S(1)}, u32[]{:S(2)}, u32[]{:S(2)}) collective-permute-start(bf16[144,128]{1,0:T(8,128)(2,1)S(1)} %get-tuple-element.80), channel_id=1, source_target_pairs={{0,24},{4,28},{8,16},{12,20},{16,8},{20,12},{24,0},{28,4},{1,25},{... | collective-permute-start | bytes 110600 | tf_op jit(solution)/shard_map/ppermute | solution.py:461
  45.6 2.3 %collective-permute-start.13 = (bf16[144,128]{1,0:T(8,128)(2,1)S(1)}, bf16[144,128]{1,0:T(8,128)(2,1)S(1)}, u32[]{:S(2)}, u32[]{:S(2)}) collective-permute-start(bf16[144,128]{1,0:T(8,128)(2,1)S(1)} %get-tuple-element.82), channel_id=1, source_target_pairs={{0,8},{4,12},{8,0},{12,4},{16,24},{20,28},{24,16},{28,20},{1,9},{5... | collective-permute-start | bytes 110600 | tf_op jit(solution)/shard_map/ppermute | solution.py:461
  47.9 1.7 %collective-permute-done.11.refs_1_ = bf16[144,128]{1,0:T(8,128)(2,1)S(1)} collective-permute-done((bf16[144,128]{1,0:T(8,128)(2,1)S(1)}, bf16[144,128]{1,0:T(8,128)(2,1)S(1)}, u32[]{:S(2)}, u32[]{:S(2)}) %collective-permute-start.11) | collective-permute-done | bytes 36896 | tf_op jit(solution)/shard_map/ppermute | solution.py:461
  50.3 1.5 %collective-permute-start.16 = (bf16[144,128]{1,0:T(8,128)(2,1)S(1)}, bf16[144,128]{1,0:T(8,128)(2,1)S(1)}, u32[]{:S(2)}, u32[]{:S(2)}) collective-permute-start(bf16[144,128]{1,0:T(8,128)(2,1)S(1)} %chip_sum.1.refs_0_), channel_id=1, source_target_pairs={{0,3},{1,2},{2,1},{3,0},{4,7},{5,6},{6,5},{7,4},{8,11},{9,10},{10,... | collective-permute-start | bytes 110600 | tf_op jit(solution)/shard_map/ppermute | solution.py:464
  51.8 1.0 %collective-permute-start.15 = (bf16[144,128]{1,0:T(8,128)(2,1)S(1)}, bf16[144,128]{1,0:T(8,128)(2,1)S(1)}, u32[]{:S(2)}, u32[]{:S(2)}) collective-permute-start(bf16[144,128]{1,0:T(8,128)(2,1)S(1)} %chip_sum.1.refs_0_), channel_id=1, source_target_pairs={{0,2},{1,3},{2,0},{3,1},{4,6},{5,7},{6,4},{7,5},{8,10},{9,11},{10,... | collective-permute-start | bytes 110600 | tf_op jit(solution)/shard_map/ppermute | solution.py:464
  52.8 1.1 %collective-permute-start.14 = (bf16[144,128]{1,0:T(8,128)(2,1)S(1)}, bf16[144,128]{1,0:T(8,128)(2,1)S(1)}, u32[]{:S(2)}, u32[]{:S(2)}) collective-permute-start(bf16[144,128]{1,0:T(8,128)(2,1)S(1)} %chip_sum.1.refs_0_), channel_id=1, source_target_pairs={{0,1},{1,0},{2,3},{3,2},{4,5},{5,4},{6,7},{7,6},{8,9},{9,8},{10,11... | collective-permute-start | bytes 110600 | tf_op jit(solution)/shard_map/ppermute | solution.py:464
  53.9 1.4 %collective-permute-done.16.refs_3_ = bf16[144,128]{1,0:T(8,128)(2,1)S(1)} collective-permute-done((bf16[144,128]{1,0:T(8,128)(2,1)S(1)}, bf16[144,128]{1,0:T(8,128)(2,1)S(1)}, u32[]{:S(2)}, u32[]{:S(2)}) %collective-permute-start.16) | collective-permute-done | bytes 36896 | tf_op jit(solution)/shard_map/ppermute | solution.py:464
  55.8 1.0 %collective-permute-done.14.refs_1_ = bf16[144,128]{1,0:T(8,128)(2,1)S(1)} collective-permute-done((bf16[144,128]{1,0:T(8,128)(2,1)S(1)}, bf16[144,128]{1,0:T(8,128)(2,1)S(1)}, u32[]{:S(2)}, u32[]{:S(2)}) %collective-permute-start.14) | collective-permute-done | bytes 36896 | tf_op jit(solution)/shard_map/ppermute | solution.py:464
  56.7 1.0 %norm_back.1 = f32[576,128]{1,0:T(8,128)} custom-call(bf16[576,128]{1,0:T(8,128)(2,1)S(1)} %bitcast.5, bf16[512]{0:T(512)(128)(2,1)S(1)} %copy-done.10, bf16[144,128]{1,0:T(8,128)(2,1)S(1)} %chip_sum.1.refs_0_, bf16[144,128]{1,0:T(8,128)(2,1)S(1)} %collective-permute-done.14.refs_1_, bf16[144,128]{1,0:T(8,128)(2,1)S(1)} %collective-permute-done.15.refs_2_, ...), custom_call_target="tpu_custom_call" | custom-call | tf_op jit(solution)/shard_map/norm_back/pallas_call | solution.py:618
  (45 shorter events, 7.6 us)
Async XLA Ops:
  0.6 11.1 %copy-start.10 = (bf16[512]{0:T(512)(128)(2,1)S(1)}, bf16[512]{0:T(512)(128)(2,1)}, u32[]{:S(2)}) copy-start(bf16[512]{0:T(512)(128)(2,1)} %gain_ref.5) | copy-start | bytes 3076
  1.8 13.7 %copy-start = (bf16[16,128,512]{2,1,0:T(8,128)(2,1)S(1)}, bf16[16,128,512]{2,1,0:T(8,128)(2,1)}, u32[]{:S(2)}) copy-start(bf16[16,128,512]{2,1,0:T(8,128)(2,1)} %w_uk_ref.3) | copy-start | bytes 6291460
  1.8 13.7 %copy-start.1 = (bf16[16,512,128]{2,1,0:T(8,128)(2,1)S(1)}, bf16[16,512,128]{2,1,0:T(8,128)(2,1)}, u32[]{:S(2)}) copy-start(bf16[16,512,128]{2,1,0:T(8,128)(2,1)} %w_uv_ref.1) | copy-start | bytes 6291460
  1.8 7.7 %collective-permute-start.2 = (bf16[144,128]{1,0:T(8,128)(2,1)S(1)}, bf16[144,128]{1,0:T(8,128)(2,1)S(1)}, u32[]{:S(2)}, u32[]{:S(2)}) collective-permute-start(bf16[144,128]{1,0:T(8,128)(2,1)S(1)} %piece.1), channel_id=1, source_target_pairs={{0,24},{4,28},{8,16},{12,20},{16,8},{20,12},{24,0},{28,4},{1,25},{... | collective-permute-start | bytes 110600 | tf_op jit(solution)/shard_map/ppermute | solution.py:461
  6.9 4.9 %collective-permute-start.1 = (bf16[144,128]{1,0:T(8,128)(2,1)S(1)}, bf16[144,128]{1,0:T(8,128)(2,1)S(1)}, u32[]{:S(2)}, u32[]{:S(2)}) collective-permute-start(bf16[144,128]{1,0:T(8,128)(2,1)S(1)} %piece.1), channel_id=1, source_target_pairs={{0,16},{4,20},{8,24},{12,28},{16,0},{20,4},{24,8},{28,12},{1,17},{... | collective-permute-start | bytes 110600 | tf_op jit(solution)/shard_map/ppermute | solution.py:461
  6.9 4.9 %collective-permute-start = (bf16[144,128]{1,0:T(8,128)(2,1)S(1)}, bf16[144,128]{1,0:T(8,128)(2,1)S(1)}, u32[]{:S(2)}, u32[]{:S(2)}) collective-permute-start(bf16[144,128]{1,0:T(8,128)(2,1)S(1)} %piece.1), channel_id=1, source_target_pairs={{0,8},{4,12},{8,0},{12,4},{16,24},{20,28},{24,16},{28,20},{1,9},{5... | collective-permute-start | bytes 110600 | tf_op jit(solution)/shard_map/ppermute | solution.py:461
  9.1 6.4 %copy-start.6 = (bf16[128,2048]{1,0:T(8,128)(2,1)S(1)}, bf16[128,2048]{1,0:T(8,128)(2,1)}, u32[]{:S(2)}) copy-start(bf16[128,2048]{1,0:T(8,128)(2,1)} %out_ref.1) | copy-start | bytes 1572868
  9.1 6.4 %copy-start.7 = (bf16[128,1024]{1,0:T(8,128)(2,1)S(1)}, bf16[128,1024]{1,0:T(8,128)(2,1)}, u32[]{:S(2)}) copy-start(bf16[128,1024]{1,0:T(8,128)(2,1)} %rope_ref.1) | copy-start | bytes 786436
  11.9 7.9 %copy-start.8 = (s32[8,2]{0,1:T(2,128)S(1)}, s32[8,2]{0,1:T(2,128)}, u32[]{:S(2)}) copy-start(s32[8,2]{0,1:T(2,128)} %param.17) | copy-start | bytes 196
  11.9 6.9 %collective-permute-start.5 = (bf16[432,128]{1,0:T(8,128)(2,1)S(1)}, bf16[432,128]{1,0:T(8,128)(2,1)S(1)}, u32[]{:S(2)}, u32[]{:S(2)}) collective-permute-start(bf16[432,128]{1,0:T(8,128)(2,1)S(1)} %join_chips.1.unused_ref.refs_1_), channel_id=1, source_target_pairs={{0,3},{1,2},{2,1},{3,0},{4,7},{5,6},{6,5},{7,4},{8,11},{9,10},{10,... | collective-permute-start | bytes 331784 | tf_op jit(solution)/shard_map/ppermute | solution.py:464
  14.4 5.2 %collective-permute-start.4 = (bf16[432,128]{1,0:T(8,128)(2,1)S(1)}, bf16[432,128]{1,0:T(8,128)(2,1)S(1)}, u32[]{:S(2)}, u32[]{:S(2)}) collective-permute-start(bf16[432,128]{1,0:T(8,128)(2,1)S(1)} %join_chips.1.unused_ref.refs_1_), channel_id=1, source_target_pairs={{0,2},{1,3},{2,0},{3,1},{4,6},{5,7},{6,4},{7,5},{8,10},{9,11},{10,... | collective-permute-start | bytes 331784 | tf_op jit(solution)/shard_map/ppermute | solution.py:464
  14.9 4.7 %collective-permute-start.3 = (bf16[432,128]{1,0:T(8,128)(2,1)S(1)}, bf16[432,128]{1,0:T(8,128)(2,1)S(1)}, u32[]{:S(2)}, u32[]{:S(2)}) collective-permute-start(bf16[432,128]{1,0:T(8,128)(2,1)S(1)} %join_chips.1.unused_ref.refs_1_), channel_id=1, source_target_pairs={{0,1},{1,0},{2,3},{3,2},{4,5},{5,4},{6,7},{7,6},{8,9},{9,8},{10,11... | collective-permute-start | bytes 331784 | tf_op jit(solution)/shard_map/ppermute | solution.py:464
  19.7 2.1 %collective-permute-start.6 = (bf16[2304,128]{1,0:T(8,128)(2,1)S(1)}, bf16[2304,128]{1,0:T(8,128)(2,1)S(1)}, u32[]{:S(2)}, u32[]{:S(2)}) collective-permute-start(bf16[2304,128]{1,0:T(8,128)(2,1)S(1)} %join_heads.1.source), channel_id=1, source_target_pairs={{0,4},{4,0},{8,12},{12,8},{16,20},{20,16},{24,28},{28,24},{1,5},{5... | collective-permute-start | bytes 1769480 | tf_op jit(solution)/shard_map/ppermute | solution.py:458
  31.0 2.1 %collective-permute-start.7 = (bf16[2304,128]{1,0:T(8,128)(2,1)S(1)}, bf16[2304,128]{1,0:T(8,128)(2,1)S(1)}, u32[]{:S(2)}, u32[]{:S(2)}) collective-permute-start(bf16[2304,128]{1,0:T(8,128)(2,1)S(1)} %get-tuple-element.59), channel_id=1, source_target_pairs={{0,4},{4,0},{8,12},{12,8},{16,20},{20,16},{24,28},{28,24},{1,5},{5... | collective-permute-start | bytes 1769480 | tf_op jit(solution)/shard_map/ppermute | solution.py:458
  33.2 8.3 %collective-permute-start.8 = (bf16[576,128]{1,0:T(8,128)(2,1)S(1)}, bf16[576,128]{1,0:T(8,128)(2,1)S(1)}, u32[]{:S(2)}, u32[]{:S(2)}) collective-permute-start(bf16[576,128]{1,0:T(8,128)(2,1)S(1)} %get-tuple-element.66), channel_id=1, source_target_pairs={{0,3},{1,2},{2,1},{3,0},{4,7},{5,6},{6,5},{7,4},{8,11},{9,10},{10,... | collective-permute-start | bytes 442376 | tf_op jit(solution)/shard_map/ppermute | solution.py:464
  34.7 8.5 %collective-permute-start.9 = (bf16[576,128]{1,0:T(8,128)(2,1)S(1)}, bf16[576,128]{1,0:T(8,128)(2,1)S(1)}, u32[]{:S(2)}, u32[]{:S(2)}) collective-permute-start(bf16[576,128]{1,0:T(8,128)(2,1)S(1)} %get-tuple-element.67), channel_id=1, source_target_pairs={{0,2},{1,3},{2,0},{3,1},{4,6},{5,7},{6,4},{7,5},{8,10},{9,11},{10,... | collective-permute-start | bytes 442376 | tf_op jit(solution)/shard_map/ppermute | solution.py:464
  35.4 7.8 %collective-permute-start.10 = (bf16[576,128]{1,0:T(8,128)(2,1)S(1)}, bf16[576,128]{1,0:T(8,128)(2,1)S(1)}, u32[]{:S(2)}, u32[]{:S(2)}) collective-permute-start(bf16[576,128]{1,0:T(8,128)(2,1)S(1)} %get-tuple-element.68), channel_id=1, source_target_pairs={{0,1},{1,0},{2,3},{3,2},{4,5},{5,4},{6,7},{7,6},{8,9},{9,8},{10,11... | collective-permute-start | bytes 442376 | tf_op jit(solution)/shard_map/ppermute | solution.py:464
  36.7 20.0 %copy-start.3 = (bf16[128,576]{0,1:T(8,128)(2,1)S(1)}, bf16[128,576]{0,1:T(8,128)(2,1)}, u32[]{:S(2)}) copy-start(bf16[128,576]{0,1:T(8,128)(2,1)} %param.11) | copy-start | bytes 442372
  43.4 6.2 %collective-permute-start.11 = (bf16[144,128]{1,0:T(8,128)(2,1)S(1)}, bf16[144,128]{1,0:T(8,128)(2,1)S(1)}, u32[]{:S(2)}, u32[]{:S(2)}) collective-permute-start(bf16[144,128]{1,0:T(8,128)(2,1)S(1)} %get-tuple-element.80), channel_id=1, source_target_pairs={{0,24},{4,28},{8,16},{12,20},{16,8},{20,12},{24,0},{28,4},{1,25},{... | collective-permute-start | bytes 110600 | tf_op jit(solution)/shard_map/ppermute | solution.py:461
  44.9 5.0 %collective-permute-start.12 = (bf16[144,128]{1,0:T(8,128)(2,1)S(1)}, bf16[144,128]{1,0:T(8,128)(2,1)S(1)}, u32[]{:S(2)}, u32[]{:S(2)}) collective-permute-start(bf16[144,128]{1,0:T(8,128)(2,1)S(1)} %get-tuple-element.81), channel_id=1, source_target_pairs={{0,16},{4,20},{8,24},{12,28},{16,0},{20,4},{24,8},{28,12},{1,17},{... | collective-permute-start | bytes 110600 | tf_op jit(solution)/shard_map/ppermute | solution.py:461
  45.6 4.7 %collective-permute-start.13 = (bf16[144,128]{1,0:T(8,128)(2,1)S(1)}, bf16[144,128]{1,0:T(8,128)(2,1)S(1)}, u32[]{:S(2)}, u32[]{:S(2)}) collective-permute-start(bf16[144,128]{1,0:T(8,128)(2,1)S(1)} %get-tuple-element.82), channel_id=1, source_target_pairs={{0,8},{4,12},{8,0},{12,4},{16,24},{20,28},{24,16},{28,20},{1,9},{5... | collective-permute-start | bytes 110600 | tf_op jit(solution)/shard_map/ppermute | solution.py:461
  50.3 4.9 %collective-permute-start.16 = (bf16[144,128]{1,0:T(8,128)(2,1)S(1)}, bf16[144,128]{1,0:T(8,128)(2,1)S(1)}, u32[]{:S(2)}, u32[]{:S(2)}) collective-permute-start(bf16[144,128]{1,0:T(8,128)(2,1)S(1)} %chip_sum.1.refs_0_), channel_id=1, source_target_pairs={{0,3},{1,2},{2,1},{3,0},{4,7},{5,6},{6,5},{7,4},{8,11},{9,10},{10,... | collective-permute-start | bytes 110600 | tf_op jit(solution)/shard_map/ppermute | solution.py:464
  51.8 4.0 %collective-permute-start.15 = (bf16[144,128]{1,0:T(8,128)(2,1)S(1)}, bf16[144,128]{1,0:T(8,128)(2,1)S(1)}, u32[]{:S(2)}, u32[]{:S(2)}) collective-permute-start(bf16[144,128]{1,0:T(8,128)(2,1)S(1)} %chip_sum.1.refs_0_), channel_id=1, source_target_pairs={{0,2},{1,3},{2,0},{3,1},{4,6},{5,7},{6,4},{7,5},{8,10},{9,11},{10,... | collective-permute-start | bytes 110600 | tf_op jit(solution)/shard_map/ppermute | solution.py:464
  52.8 4.0 %collective-permute-start.14 = (bf16[144,128]{1,0:T(8,128)(2,1)S(1)}, bf16[144,128]{1,0:T(8,128)(2,1)S(1)}, u32[]{:S(2)}, u32[]{:S(2)}) collective-permute-start(bf16[144,128]{1,0:T(8,128)(2,1)S(1)} %chip_sum.1.refs_0_), channel_id=1, source_target_pairs={{0,1},{1,0},{2,3},{3,2},{4,5},{5,4},{6,7},{7,6},{8,9},{9,8},{10,11... | collective-permute-start | bytes 110600 | tf_op jit(solution)/shard_map/ppermute | solution.py:464
  (4 other events, 14.3 us)
